TPU v7x, 32 devices: a whole 2x2x4 slice. The times are simulated.
32 devices in a mesh: dp: 4 (over y, x), expert: 8 (over z, core).
Axes of the slice: x: 2, y: 2, z: 4, core: 2. Of those that a mesh axis runs over, the one named last changes fastest.
Arguments:
- tokens: bfloat16 [4096, 2048], P(('dp', 'expert')), may hold values from -6 to 6
- cotangent: bfloat16 [4096, 2048], P(('dp', 'expert')), may hold values from -6 to 6
- expert_ids: int32 [4096, 6], P(('dp', 'expert')), may hold values from 0 to 7, as said below
- gate_fixed: int32 [4096, 6], P(('dp', 'expert')), may hold values from 1024 to 65535
- w_gate: bfloat16 [8, 2048, 704], P('expert'), may hold values from -0.125 to 0.125
- w_up: bfloat16 [8, 2048, 704], P('expert'), may hold values from -0.125 to 0.125
- w_down: bfloat16 [8, 704, 2048], P('expert'), may hold values from -0.21875 to 0.21875
Outputs:
- mixed: bfloat16 [4096, 2048], P(('dp', 'expert'))
- token_grad: bfloat16 [4096, 2048], P(('dp', 'expert'))
- grad_gate: float32 [8, 2048, 704], P('expert', 'dp')
- grad_up: float32 [8, 2048, 704], P('expert', 'dp')
- grad_down: float32 [8, 704, 2048], P('expert', None, 'dp')
Inputs may be any that keep to these rules, and one draw needn't show every extreme that they name: `expert_ids`: each row names 6 different experts. Within the rows of one device (aligned blocks of 128 rows) no expert is named by more than 128 rows, and one expert, the same in every block, is named by exactly 128 rows.
All inputs are finite; a program needn't handle non-finite values.
Results may differ from a plain program's by a relative error of at most 0.0095.
Values may be sent and summed in bfloat16 or wider, within the bound.
No kernel may reach another device: no remote copies, remote signals or barrier semaphores. Data moves between devices by JAX's collectives and lax.ppermute only.
A program may use at most 192 MiB of HBM per device.

v0:
```python
from functools import partial

import jax
import jax.numpy as jnp
from jax import lax
from jax.sharding import PartitionSpec as P


def contract(left, right):
    return lax.dot_general(
        left, right, (((0,), (0,)), ((), ())), preferred_element_type=jnp.float32
    )


def trans_dot(left, right):
    return lax.dot_general(
        left, right, (((1,), (1,)), ((), ())), preferred_element_type=jnp.float32
    )


def forward_rows(gate_w, up_w, down_w, rows_in):
    gate_pre = jnp.dot(rows_in, gate_w, preferred_element_type=jnp.float32)
    up_pre = jnp.dot(rows_in, up_w, preferred_element_type=jnp.float32)
    hidden = (gate_pre * jax.nn.sigmoid(gate_pre) * up_pre).astype(jnp.bfloat16)
    expert_out = jnp.dot(hidden, down_w, preferred_element_type=jnp.float32).astype(jnp.bfloat16)
    return (expert_out, gate_pre, up_pre, hidden)


def backward_rows(gate_w, up_w, down_w, dy_rows, gate_pre, up_pre):
    sigma = jax.nn.sigmoid(gate_pre)
    activ = gate_pre * sigma
    d_hidden = trans_dot(dy_rows, down_w)
    d_gate = (d_hidden * up_pre * (sigma * (1.0 + gate_pre * (1.0 - sigma)))).astype(jnp.bfloat16)
    d_up = (d_hidden * activ).astype(jnp.bfloat16)
    d_rows = (trans_dot(d_gate, gate_w) + trans_dot(d_up, up_w)).astype(jnp.bfloat16)
    return (d_rows, d_gate, d_up)


def shards(tokens, cotangent, expert_ids, gate_fixed, w_gate, w_up, w_down):
    n_expert = lax.axis_size("expert")
    tok_rows = tokens.shape[0]
    width = tokens.shape[1]
    top_k = expert_ids.shape[1]
    capacity = 4 * tok_rows * top_k // (3 * n_expert)
    slot_count = n_expert * capacity
    gate_w = w_gate[0]
    up_w = w_up[0]
    down_w = w_down[0]
    flat_ids = expert_ids.reshape(-1)
    onehot = (flat_ids[:, None] == jnp.arange(n_expert, dtype=jnp.int32)[None, :]).astype(jnp.int32)
    before = jnp.cumsum(onehot, axis=0) - onehot
    rank_in = jnp.sum(before * onehot, axis=1)
    counts = jnp.sum(onehot, axis=0)
    slot_of = flat_ids * capacity + rank_in
    owner = jnp.arange(flat_ids.shape[0], dtype=jnp.int32) // top_k
    slot_token = jnp.zeros((slot_count,), jnp.int32).at[slot_of].set(owner)
    gate_values = gate_fixed.reshape(-1).astype(jnp.float32) / 65536.0
    slot_gate = jnp.zeros((slot_count,), jnp.float32).at[slot_of].set(gate_values)
    outgoing = jnp.where(
        (slot_gate > 0.0)[:, None], tokens[slot_token], jnp.zeros((), tokens.dtype)
    )
    received, arrived = (
        lax.all_to_all(outgoing, "expert", split_axis=0, concat_axis=0, tiled=True),
        lax.all_to_all(counts, "expert", split_axis=0, concat_axis=0, tiled=True),
    )

    def run_rows(row_fn, inputs):
        return row_fn(*inputs)

    def fold_rows(left, right):
        return contract(left, right)

    expert_out, gate_pre, up_pre, hidden = run_rows(
        partial(forward_rows, gate_w, up_w, down_w), (received,)
    )
    returned = lax.all_to_all(expert_out, "expert", split_axis=0, concat_axis=0, tiled=True)
    mixed_rows = returned[slot_of].astype(jnp.float32).reshape(tok_rows, top_k, width)
    mixed = jnp.sum(mixed_rows * gate_values.reshape(tok_rows, top_k)[:, :, None], axis=1).astype(
        jnp.bfloat16
    )
    dy_out = (cotangent[slot_token].astype(jnp.float32) * slot_gate[:, None]).astype(jnp.bfloat16)
    dy_in = lax.all_to_all(dy_out, "expert", split_axis=0, concat_axis=0, tiled=True)
    d_rows, d_gate, d_up = run_rows(
        partial(backward_rows, gate_w, up_w, down_w), (dy_in, gate_pre, up_pre)
    )
    back_rows = lax.all_to_all(d_rows, "expert", split_axis=0, concat_axis=0, tiled=True)
    token_grad = jnp.sum(
        back_rows[slot_of].astype(jnp.float32).reshape(tok_rows, top_k, width), axis=1
    ).astype(jnp.bfloat16)
    grad_gate, grad_up, grad_down = (
        lax.psum_scatter(
            fold_rows(received, d_gate).astype(jnp.bfloat16), "dp", scatter_dimension=0, tiled=True
        ).astype(jnp.float32),
        lax.psum_scatter(
            fold_rows(received, d_up).astype(jnp.bfloat16), "dp", scatter_dimension=0, tiled=True
        ).astype(jnp.float32),
        lax.psum_scatter(
            fold_rows(hidden, dy_in).astype(jnp.bfloat16), "dp", scatter_dimension=1, tiled=True
        ).astype(jnp.float32),
    )
    return (mixed, token_grad, grad_gate[None], grad_up[None], grad_down[None])


def solution(mesh):
    in_specs = (
        P(("dp", "expert"), None),
        P(("dp", "expert"), None),
        P(("dp", "expert"), None),
        P(("dp", "expert"), None),
        P("expert", None, None),
        P("expert", None, None),
        P("expert", None, None),
    )
    out_specs = (
        P(("dp", "expert"), None),
        P(("dp", "expert"), None),
        P("expert", "dp", None),
        P("expert", "dp", None),
        P("expert", None, "dp"),
    )
    return jax.shard_map(shards, mesh=mesh, in_specs=in_specs, out_specs=out_specs, check_vma=False)
```

profile of v0, /device:TPU:0, one launch (start us, length us, event | category | flops | bytes accessed | tf_op | source)
XLA Modules:
  0.0 478.3 jit_solution(11598855480209156034)
XLA Ops:
  20.0 6.0 %gather_fusion = bf16[1024,2048]{1,0:T(8,128)(2,1)} fusion(bf16[128,2048]{1,0:T(8,128)(2,1)S(1)} %copy-done.2, s32[1024]{0:T(1024)S(1)} %fusion.17), kind=kCustom, calls=%fused_computation | custom fusion | bytes 8392704 | tf_op jit(solution)/shard_map/gather | solution.py:60
  30.6 6.5 %all-to-all-start = ((bf16[8,128,2048]{2,1,0:T(8,128)(2,1)}), bf16[8,128,2048]{2,1,0:T(8,128)(2,1)}, u32[]{:S(2)}, u32[]{:S(2)}) async-start(bf16[8,128,2048]{2,1,0:T(8,128)(2,1)} %broadcast_select_fusion), calls=%async_computation | async-start | bytes 8388608 | tf_op jit(solution)/shard_map/all_to_all | solution.py:63
  37.0 6.0 %gather_fusion.2 = bf16[1024,2048]{1,0:T(8,128)(2,1)} fusion(bf16[128,2048]{1,0:T(8,128)(2,1)S(1)} %copy-done.3, s32[1024]{0:T(1024)S(1)} %fusion.17), kind=kCustom, calls=%fused_computation.2 | custom fusion | bytes 8392704 | tf_op jit(solution)/shard_map/gather | solution.py:81
  43.1 4.9 %fusion = bf16[8,128,2048]{2,1,0:T(8,128)(2,1)} fusion(bf16[8,128,2048]{2,1,0:T(8,128)(2,1)} %bitcast.63, f32[8,128]{1,0:T(8,128)S(1)} %bitcast.66), kind=kLoop, calls=%fused_computation.7 | loop fusion | flops 6291456 | bytes 8392704 | tf_op jit(solution)/shard_map/convert_element_type | solution.py:81
  48.0 83.2 %all-to-all-done = bf16[8,128,2048]{2,1,0:T(8,128)(2,1)} async-done(((bf16[8,128,2048]{2,1,0:T(8,128)(2,1)}), bf16[8,128,2048]{2,1,0:T(8,128)(2,1)}, u32[]{:S(2)}, u32[]{:S(2)}) %all-to-all-start) | async-done | bytes 4194336 | tf_op jit(solution)/shard_map/all_to_all | solution.py:63
  135.9 8.0 %fusion.5 = f32[1024,704]{0,1:T(8,128)} fusion(bf16[1024,2048]{1,0:T(8,128)(2,1)} %bitcast.5, bf16[1,2048,704]{1,2,0:T(8,128)(2,1)} %param.12), kind=kOutput, calls=%fused_computation.19 | convolution fusion | flops 2952790016 | bytes 9961472 | tf_op jit(solution)/shard_map/dot_general | solution.py:23
  143.9 6.9 %fusion.9 = f32[1024,704]{0,1:T(8,128)} fusion(bf16[1024,2048]{1,0:T(8,128)(2,1)} %bitcast.5, bf16[1,2048,704]{1,2,0:T(8,128)(2,1)S(1)} %copy-done.4), kind=kOutput, calls=%fused_computation.23 | convolution fusion | flops 2952790016 | bytes 9961472 | tf_op jit(solution)/shard_map/dot_general | solution.py:22
  150.8 78.9 %all-to-all-done.2 = bf16[8,128,2048]{2,1,0:T(8,128)(2,1)} async-done(((bf16[8,128,2048]{2,1,0:T(8,128)(2,1)}), bf16[8,128,2048]{2,1,0:T(8,128)(2,1)}, u32[]{:S(2)}, u32[]{:S(2)}) %all-to-all-start.2) | async-done | bytes 4194336 | tf_op jit(solution)/shard_map/all_to_all | solution.py:82
  229.7 8.5 %multiply_convert_fusion = (bf16[1024,704]{0,1:T(8,128)(2,1)}, bf16[1024,704]{0,1:T(8,128)(2,1)}, bf16[1024,704]{0,1:T(8,128)(2,1)S(1)}) fusion(f32[1024,704]{0,1:T(8,128)} %fusion.9, f32[1024,704]{0,1:T(8,128)} %fusion.5, bf16[1024,2048]{1,0:T(8,128)(2,1)} %bitcast.13, bf16[1,704,2048]{2,1,0:T(8,128)(2,1)S(1)} %copy-done), kind=kOutput, calls=%fused_computation.25 | convolution fusion | flops 2963603456 | bytes 17170432 | tf_op jit(solution)/shard_map/dot_general | solution.py:16
  239.3 6.6 %convolution_convert_fusion.3 = bf16[704,2048]{1,0:T(8,128)(2,1)} fusion(bf16[1024,704]{0,1:T(8,128)(2,1)S(1)} %get-tuple-element.7, bf16[1024,2048]{1,0:T(8,128)(2,1)} %bitcast.13), kind=kOutput, calls=%fused_computation.14 | convolution fusion | flops 2954231808 | bytes 8519680 | tf_op jit(solution)/shard_map/dot_general | solution.py:10
  246.0 6.4 %convolution_convert_fusion = bf16[1024,2048]{1,0:T(8,128)(2,1)} fusion(bf16[1024,704]{0,1:T(8,128)(2,1)} %copy-done.10, bf16[1,704,2048]{2,1,0:T(8,128)(2,1)S(1)} %copy-done), kind=kOutput, calls=%fused_computation.11 | convolution fusion | flops 2954887168 | bytes 8519680 | tf_op jit(solution)/shard_map/dot_general | solution.py:25
  257.3 6.8 %convolution_convert_fusion.1 = bf16[2048,704]{0,1:T(8,128)(2,1)} fusion(bf16[1024,704]{0,1:T(8,128)(2,1)S(1)} %copy-done.8, bf16[1024,2048]{1,0:T(8,128)(2,1)} %bitcast.5), kind=kOutput, calls=%fused_computation.12 | convolution fusion | flops 2954231808 | bytes 8519680 | tf_op jit(solution)/shard_map/dot_general | solution.py:10
  266.0 5.1 %fusion.7 = f32[1024,2048]{1,0:T(8,128)S(1)} fusion(bf16[1024,704]{0,1:T(8,128)(2,1)} %get-tuple-element.6, bf16[1,2048,704]{1,2,0:T(8,128)(2,1)S(1)} %copy-done.5), kind=kOutput, calls=%fused_computation.21 | convolution fusion | flops 2952790016 | bytes 12713984 | tf_op jit(solution)/shard_map/dot_general | solution.py:16
  271.1 5.4 %add_convert_fusion = bf16[1024,2048]{1,0:T(8,128)(2,1)} fusion(f32[1024,2048]{1,0:T(8,128)S(1)} %fusion.7, bf16[1024,704]{0,1:T(8,128)(2,1)S(1)} %copy-done.9, bf16[1,2048,704]{1,2,0:T(8,128)(2,1)S(1)} %copy-done.6), kind=kOutput, calls=%fused_computation.8 | convolution fusion | flops 2956984320 | bytes 16908288 | tf_op jit(solution)/shard_map/dot_general | solution.py:16
  276.5 74.6 %all-to-all-done.1 = bf16[8,128,2048]{2,1,0:T(8,128)(2,1)} async-done(((bf16[8,128,2048]{2,1,0:T(8,128)(2,1)}), bf16[8,128,2048]{2,1,0:T(8,128)(2,1)}, u32[]{:S(2)}, u32[]{:S(2)}) %all-to-all-start.1) | async-done | bytes 4194336 | tf_op jit(solution)/shard_map/all_to_all | solution.py:76
  356.1 6.7 %convolution_convert_fusion.2 = bf16[2048,704]{0,1:T(8,128)(2,1)} fusion(bf16[1024,704]{0,1:T(8,128)(2,1)S(1)} %copy-done.7, bf16[1024,2048]{1,0:T(8,128)(2,1)} %bitcast.5), kind=kOutput, calls=%fused_computation.13 | convolution fusion | flops 2954231808 | bytes 8519680 | tf_op jit(solution)/shard_map/dot_general | solution.py:10
  367.7 38.1 %reduce-scatter.4.cloned.1.call-done = bf16[512,704]{0,1:T(8,128)(2,1)} async-done(((bf16[2048,704]{0,1:T(8,128)(2,1)}), bf16[512,704]{0,1:T(8,128)(2,1)}) %reduce-scatter.4.cloned.1.call-update) | async-done | bytes 720912 | tf_op jit(solution)/shard_map/reduce_scatter | solution.py:91
  408.2 9.8 %gather_fusion.1 = bf16[768,2048]{1,0:T(8,128)(2,1)} fusion(bf16[1024,2048]{1,0:T(8,128)(2,1)} %bitcast.10, s32[1024]{0:T(1024)S(1)} %pad_clamp_fusion), kind=kCustom, calls=%fused_computation.1 | custom fusion | bytes 6294528 | tf_op jit(solution)/shard_map/gather | solution.py:77
  418.1 6.6 %reshape.95 = f32[128,6,2048]{2,1,0:T(8,128)} reshape(bf16[768,2048]{1,0:T(8,128)(2,1)} %gather_fusion.1) | data formatting | bytes 9437184 | tf_op jit(solution)/shard_map/convert_element_type | solution.py:77
  424.6 7.4 %multiply_reduce_fusion = bf16[128,2048]{1,0:T(8,128)(2,1)} fusion(f32[128,6,2048]{2,1,0:T(8,128)} %reshape.95, f32[128,6]{1,0:T(8,128)S(1)} %copy.20), kind=kLoop, calls=%fused_computation.9 | loop fusion | flops 2883584 | bytes 6818816 | tf_op jit(solution)/shard_map/reduce_sum | solution.py:78
  432.0 17.8 %all-to-all-done.3 = bf16[8,128,2048]{2,1,0:T(8,128)(2,1)} async-done(((bf16[8,128,2048]{2,1,0:T(8,128)(2,1)}), bf16[8,128,2048]{2,1,0:T(8,128)(2,1)}, u32[]{:S(2)}, u32[]{:S(2)}) %all-to-all-start.3) | async-done | bytes 4194336 | tf_op jit(solution)/shard_map/all_to_all | solution.py:86
  449.8 9.9 %gather_fusion.3 = bf16[768,2048]{1,0:T(8,128)(2,1)} fusion(bf16[1024,2048]{1,0:T(8,128)(2,1)} %bitcast.15, s32[1024]{0:T(1024)S(1)} %pad_clamp_fusion), kind=kCustom, calls=%fused_computation.3 | custom fusion | bytes 6294528 | tf_op jit(solution)/shard_map/gather | solution.py:88
  459.7 6.4 %gather.21 = bf16[128,6,2048]{2,1,0:T(8,128)(2,1)} reshape(bf16[768,2048]{1,0:T(8,128)(2,1)} %gather_fusion.3) | data formatting | bytes 6291456 | tf_op jit(solution)/shard_map/gather | solution.py:88
  466.1 5.7 %reduce_sum.35 = bf16[128,2048]{1,0:T(8,128)(2,1)} reduce(bf16[128,6,2048]{2,1,0:T(8,128)(2,1)} %gather.21, bf16[]{:T(256)} %constant.32.clone.1), dimensions={1}, to_apply=%region_6.7 | reduce | flops 1310720 | bytes 3670018 | tf_op jit(solution)/shard_map/reduce_sum | solution.py:87
  (60 shorter events, 42.3 us)
Async XLA Ops:
  7.2 222.5 %copy-start = (bf16[1,704,2048]{2,1,0:T(8,128)(2,1)S(1)}, bf16[1,704,2048]{2,1,0:T(8,128)(2,1)}, u32[]{:S(2)}) copy-start(bf16[1,704,2048]{2,1,0:T(8,128)(2,1)} %param.13) | copy-start | bytes 8650756
  7.2 12.8 %copy-start.2 = (bf16[128,2048]{1,0:T(8,128)(2,1)S(1)}, bf16[128,2048]{1,0:T(8,128)(2,1)}, u32[]{:S(2)}) copy-start(bf16[128,2048]{1,0:T(8,128)(2,1)} %param.7) | copy-start | bytes 1572868
  30.6 6.5 %copy-start.3 = (bf16[128,2048]{1,0:T(8,128)(2,1)S(1)}, bf16[128,2048]{1,0:T(8,128)(2,1)}, u32[]{:S(2)}) copy-start(bf16[128,2048]{1,0:T(8,128)(2,1)} %param.8) | copy-start | bytes 1572868
  30.6 100.6 %all-to-all-start = ((bf16[8,128,2048]{2,1,0:T(8,128)(2,1)}), bf16[8,128,2048]{2,1,0:T(8,128)(2,1)}, u32[]{:S(2)}, u32[]{:S(2)}) async-start(bf16[8,128,2048]{2,1,0:T(8,128)(2,1)} %broadcast_select_fusion), calls=%async_computation | async-start | bytes 8388608 | tf_op jit(solution)/shard_map/all_to_all | solution.py:63
  131.1 98.6 %all-to-all-start.2 = ((bf16[8,128,2048]{2,1,0:T(8,128)(2,1)}), bf16[8,128,2048]{2,1,0:T(8,128)(2,1)}, u32[]{:S(2)}, u32[]{:S(2)}) async-start(bf16[8,128,2048]{2,1,0:T(8,128)(2,1)} %fusion), calls=%async_computation.2 | async-start | bytes 8388608 | tf_op jit(solution)/shard_map/all_to_all | solution.py:82
  135.7 227.2 %reduce-scatter.8.cloned.1.call-start = ((), (), s32[]{:S(2)}) async-start(), calls=%async_computation.9 | async-start | bytes 3604480 | tf_op jit(solution)/shard_map/reduce_scatter | solution.py:97
  135.9 8.0 %copy-start.4 = (bf16[1,2048,704]{1,2,0:T(8,128)(2,1)S(1)}, bf16[1,2048,704]{1,2,0:T(8,128)(2,1)}, u32[]{:S(2)}) copy-start(bf16[1,2048,704]{1,2,0:T(8,128)(2,1)} %param.11) | copy-start | bytes 8650756
  238.2 1.1 copy-start.10
  252.4 5.0 %copy-start.8 = (bf16[1024,704]{0,1:T(8,128)(2,1)S(1)}, bf16[1024,704]{0,1:T(8,128)(2,1)}, u32[]{:S(2)}) copy-start(bf16[1024,704]{0,1:T(8,128)(2,1)} %get-tuple-element.5) | copy-start | bytes 4325380
  252.4 98.7 %all-to-all-start.1 = ((bf16[8,128,2048]{2,1,0:T(8,128)(2,1)}), bf16[8,128,2048]{2,1,0:T(8,128)(2,1)}, u32[]{:S(2)}, u32[]{:S(2)}) async-start(bf16[8,128,2048]{2,1,0:T(8,128)(2,1)} %bitcast.65), calls=%async_computation.1 | async-start | bytes 8388608 | tf_op jit(solution)/shard_map/all_to_all | solution.py:76
  257.1 108.2 %reduce-scatter.6.cloned.1.call-start = ((), (), s32[]{:S(2)}) async-start(), calls=%async_computation.8 | async-start | bytes 3604480 | tf_op jit(solution)/shard_map/reduce_scatter | solution.py:94
  264.2 1.9 copy-start.5
  266.0 5.1 %copy-start.6 = (bf16[1,2048,704]{1,2,0:T(8,128)(2,1)S(1)}, bf16[1,2048,704]{1,2,0:T(8,128)(2,1)}, u32[]{:S(2)}) copy-start(bf16[1,2048,704]{1,2,0:T(8,128)(2,1)} %param.12) | copy-start | bytes 8650756
  266.0 5.1 %copy-start.9 = (bf16[1024,704]{0,1:T(8,128)(2,1)S(1)}, bf16[1024,704]{0,1:T(8,128)(2,1)}, u32[]{:S(2)}) copy-start(bf16[1024,704]{0,1:T(8,128)(2,1)} %get-tuple-element.5) | copy-start | bytes 4325380
  351.1 5.1 %copy-start.7 = (bf16[1024,704]{0,1:T(8,128)(2,1)S(1)}, bf16[1024,704]{0,1:T(8,128)(2,1)}, u32[]{:S(2)}) copy-start(bf16[1024,704]{0,1:T(8,128)(2,1)} %get-tuple-element.6) | copy-start | bytes 4325380
  351.1 98.7 %all-to-all-start.3 = ((bf16[8,128,2048]{2,1,0:T(8,128)(2,1)}), bf16[8,128,2048]{2,1,0:T(8,128)(2,1)}, u32[]{:S(2)}, u32[]{:S(2)}) async-start(bf16[8,128,2048]{2,1,0:T(8,128)(2,1)} %bitcast.64), calls=%async_computation.3 | async-start | bytes 8388608 | tf_op jit(solution)/shard_map/all_to_all | solution.py:86
  355.8 50.0 %reduce-scatter.4.cloned.1.call-start = ((), (), s32[]{:S(2)}) async-start(), calls=%async_computation.7 | async-start | bytes 3604480 | tf_op jit(solution)/shard_map/reduce_scatter | solution.py:91
  459.7 12.1 %copy-start.1 = (bf16[1,704,2048]{2,1,0:T(8,128)(2,1)S(1)}, bf16[1,704,2048]{2,1,0:T(8,128)(2,1)}, u32[]{:S(2)}) copy-start(bf16[1,704,2048]{2,1,0:T(8,128)(2,1)} %param.13) | copy-start | bytes 8650756
Sparse Core Ops, SparseCore 0:
  246.1 40.6 reduce-scatter.7
  289.8 41.7 reduce-scatter.5
  362.9 42.8 reduce-scatter.3
where the time goes:
time: 480 us; the launch traced here: 478 us
  waiting for transfers between devices  293 us (61%)
  matrix products  60.4 us (13%)
  local copies, waits for them, and re-layouts  56.4 us (12%)
  other arithmetic  33.7 us (7%)
  starting transfers between devices  21.2 us (4%)
  between operations  14 us (3%)
    all_to_all x1, waiting for transfers between devices, shards(): lax.all_to_all(outgoing, 'expert', split_axis=0, concat_axis=0, tiled=True)  83.2 us
    all_to_all x1, waiting for transfers between devices, shards(): lax.all_to_all(dy_out, 'expert', split_axis=0, concat_axis=0, tiled=True)  78.9 us
    all_to_all x1, waiting for transfers between devices, shards(): lax.all_to_all(expert_out, 'expert', split_axis=0, concat_axis=0, tiled=T...  74.6 us
    reduce_scatter x1, waiting for transfers between devices, shards(): lax.psum_scatter(fold_rows(received, d_gate).astype(jnp.bfloat16), 'dp',...  38.1 us
    dot_general x3, matrix products, contract(): lax.dot_general(left, right, (((0,), (0,)), ((), ())), preferred_element_...  20.1 us
    dot_general x3, matrix products, trans_dot(): lax.dot_general(left, right, (((1,), (1,)), ((), ())), preferred_element_...  18.9 us
    all_to_all x1, waiting for transfers between devices, shards(): lax.all_to_all(d_rows, 'expert', split_axis=0, concat_axis=0, tiled=True)  17.8 us
    gather x2, local copies, waits for them, and re-layouts, shards(): back_rows[slot_of].astype(jnp.float32).reshape(tok_rows, top_k, width)  16.3 us
  transfers between devices with their start and end apart: 7, of which 5 were waited for; matrix products, arithmetic and copies ran while one was open for 18% of the time, Pallas kernels for 0%

commit v1 on v0

--- a/solution.py
+++ b/solution.py
@@ -36,7 +36,7 @@
     return (d_rows, d_gate, d_up)
 
 
-def shards(tokens, cotangent, expert_ids, gate_fixed, w_gate, w_up, w_down):
+def slot_shards(tokens, cotangent, expert_ids, gate_fixed, w_gate, w_up, w_down):
     n_expert = lax.axis_size("expert")
     tok_rows = tokens.shape[0]
     width = tokens.shape[1]
@@ -101,6 +101,118 @@
     return (mixed, token_grad, grad_gate[None], grad_up[None], grad_down[None])
 
 
+def ring_order(count):
+    return [0] + list(range(1, count, 2)) + [at for at in range(count - 1, 1, -1) if at % 2 == 0]
+
+
+def ring_pairs(n_expert):
+    order = ring_order(n_expert // 2)
+    follow = {at: order[(spot + 1) % len(order)] for spot, at in enumerate(order)}
+    return [(2 * at + core, 2 * follow[at] + core) for at in order for core in range(2)]
+
+
+def pair_pairs(n_expert):
+    return [(at, at ^ 1) for at in range(n_expert)]
+
+
+def gather_rows(mine, n_expert):
+    shards_in = [mine]
+    for _ in range(n_expert // 2 - 1):
+        shards_in.append(lax.ppermute(shards_in[-1], "expert", ring_pairs(n_expert)))
+    out = []
+    for shard in shards_in:
+        out.append((shard, lax.ppermute(shard, "expert", pair_pairs(n_expert))))
+    return out
+
+
+def add_rows(left, right):
+    return left.astype(jnp.float32) + right.astype(jnp.float32)
+
+
+def scatter_rows(partials, n_expert):
+    kept = []
+    for mine, other in partials:
+        arrived = lax.ppermute(other, "expert", pair_pairs(n_expert))
+        kept.append(add_rows(mine, arrived))
+    steps = len(kept)
+    moving = kept[1 % steps]
+    for step in range(1, steps):
+        moving = lax.ppermute(moving.astype(jnp.bfloat16), "expert", ring_pairs(n_expert))
+        moving = add_rows(moving, kept[(step + 1) % steps])
+    return moving.astype(jnp.bfloat16)
+
+
+def reduce_dp(grads, n_dp, dim):
+    size = grads.shape[dim] // n_dp
+    me = lax.axis_index("dp")
+    pairs = [[(at, at ^ flip) for at in range(n_dp)] for flip in (1, 2)]
+
+    def block(owner, half):
+        return lax.dynamic_slice_in_dim(grads, owner * size + half * (size // 2), size // 2, dim)
+
+    out = []
+    for half, (first, second) in enumerate(((1, 2), (2, 1))):
+        sent = [lax.ppermute(block(me ^ first ^ far, half), "dp", pairs[first - 1]) for far in (second, 0)]
+        far_sum = add_rows(block(me ^ second, half), sent[0]).astype(jnp.bfloat16)
+        near_sum = add_rows(block(me, half), sent[1])
+        out.append(add_rows(near_sum, lax.ppermute(far_sum, "dp", pairs[second - 1])))
+    return jnp.concatenate(out, axis=dim)
+
+
+def dense_shards(tokens, cotangent, expert_ids, gate_fixed, w_gate, w_up, w_down):
+    n_expert = lax.axis_size("expert")
+    n_dp = lax.axis_size("dp")
+    expert = lax.axis_index("expert")
+    gate_w, up_w, down_w = w_gate[0], w_up[0], w_down[0]
+    gate_values = gate_fixed.astype(jnp.float32) / 65536.0
+    table = jnp.sum(
+        jnp.where(
+            expert_ids[:, :, None] == jnp.arange(n_expert, dtype=jnp.int32)[None, None, :],
+            gate_values[:, :, None],
+            0.0,
+        ),
+        axis=1,
+    )
+    tables = gather_rows(table, n_expert)
+    token_rows = gather_rows(tokens, n_expert)
+    cot_rows = gather_rows(cotangent, n_expert)
+
+    def flat(parts):
+        return jnp.concatenate([part for pair in parts for part in pair], axis=0)
+
+    rows = flat(token_rows)
+    cots = flat(cot_rows)
+    all_tables = flat(tables)
+    weight = jnp.sum(
+        jnp.where(jnp.arange(n_expert, dtype=jnp.int32)[None, :] == expert, all_tables, 0.0), axis=1, keepdims=True
+    )
+
+    def unflat(partial):
+        parts = jnp.split(partial, n_expert, axis=0)
+        return list(zip(parts[0::2], parts[1::2]))
+
+    gate_pre = jnp.dot(rows, gate_w, preferred_element_type=jnp.float32)
+    up_pre = jnp.dot(rows, up_w, preferred_element_type=jnp.float32)
+    hidden = (gate_pre * jax.nn.sigmoid(gate_pre) * up_pre).astype(jnp.bfloat16)
+    expert_out = jnp.dot(hidden, down_w, preferred_element_type=jnp.float32)
+    mixed = scatter_rows(unflat((expert_out * weight).astype(jnp.bfloat16)), n_expert)
+    dy_rows = (cots.astype(jnp.float32) * weight).astype(jnp.bfloat16)
+    grad_down = reduce_dp(contract(hidden, dy_rows).astype(jnp.bfloat16), n_dp, 1)
+    d_rows, d_gate, d_up = backward_rows(gate_w, up_w, down_w, dy_rows, gate_pre, up_pre)
+    grad_gate = reduce_dp(contract(rows, d_gate).astype(jnp.bfloat16), n_dp, 0)
+    grad_up = reduce_dp(contract(rows, d_up).astype(jnp.bfloat16), n_dp, 0)
+    token_grad = scatter_rows(unflat(d_rows), n_expert)
+    return (mixed, token_grad, grad_gate[None], grad_up[None], grad_down[None])
+
+
+def shards(tokens, cotangent, expert_ids, gate_fixed, w_gate, w_up, w_down):
+    n_expert = lax.axis_size("expert")
+    capacity = 4 * tokens.shape[0] * expert_ids.shape[1] // (3 * n_expert)
+    dense = capacity >= tokens.shape[0] and n_expert % 2 == 0 and lax.axis_size("dp") == 4
+    run = dense_shards if dense else slot_shards
+    return run(tokens, cotangent, expert_ids, gate_fixed, w_gate, w_up, w_down)
+
+
 def solution(mesh):
     in_specs = (
         P(("dp", "expert"), None),

time: 480 us -> 267 us (0.56)
  waiting for transfers between devices: 293 us -> 162 us
  local copies, waits for them, and re-layouts: 56.4 us -> 18 us
  other arithmetic: 33.7 us -> 10.5 us
  matrix products: 60.4 us -> 39.7 us
  starting transfers between devices: 21.2 us -> 35.7 us
  between operations: 14 us -> 1.08 us
    all_to_all x4 -> x0, waiting for transfers between devices: 254 us -> none  [the longest x1 83.2 us: shards(): lax.all_to_all(outgoing, 'expert', split_axis=0, concat_axis=0, tiled=True)]
    ppermute x0 -> x53, waiting for transfers between devices: none -> 162 us  [the longest x9 56.8 us: gather_rows(): lax.ppermute(shards_in[-1], 'expert', ring_pairs(n_expert))]
    reduce_scatter x3 -> x0, waiting for transfers between devices: 38.1 us -> none  [the longest x1 38.1 us: shards(): lax.psum_scatter(fold_rows(received, d_gate).astype(jnp.bfloat16), 'dp',...]
    gather x5 -> x0, local copies, waits for them, and re-layouts: 38.1 us -> none  [the longest x2 16.3 us: shards(): back_rows[slot_of].astype(jnp.float32).reshape(tok_rows, top_k, width)]
    ppermute x0 -> x53, starting transfers between devices: none -> 35.7 us  [the longest x12 15.6 us: reduce_dp(): lax.ppermute(block(me ^ first ^ far, half), 'dp', pairs[first - 1])]
    all_to_all x4 -> x0, starting transfers between devices: 20.4 us -> none  [the longest x1 6.46 us: shards(): lax.all_to_all(outgoing, 'expert', split_axis=0, concat_axis=0, tiled=True)]
    reduce_sum x3 -> x2, other arithmetic: 13.2 us -> 0.81 us  [the longest x1 0.73 us: dense_shards(): jnp.sum(jnp.where(expert_ids[:, :, None] == jnp.arange(n_expert, dtype=jn...]
    unnamed x23 -> x33, local copies, waits for them, and re-layouts: 3.76 us -> 16.1 us
  transfers between devices with their start and end apart: 7 -> 53, of which waited for: 5 -> 21; matrix products, arithmetic and copies ran while one was open for 18% -> 16% of each run, Pallas kernels for 0% -> 0%
where the time goes in v1:
time: 267 us
  waiting for transfers between devices  162 us (61%)
  matrix products  39.7 us (15%)
  starting transfers between devices  35.7 us (13%)
  local copies, waits for them, and re-layouts  18 us (7%)
  other arithmetic  10.5 us (4%)
    ppermute x9, waiting for transfers between devices, gather_rows(): lax.ppermute(shards_in[-1], 'expert', ring_pairs(n_expert))  56.8 us
    ppermute x6, waiting for transfers between devices, scatter_rows(): lax.ppermute(moving.astype(jnp.bfloat16), 'expert', ring_pairs(n_expert))  44.1 us
    ppermute x6, waiting for transfers between devices, reduce_dp(): lax.ppermute(far_sum, 'dp', pairs[second - 1])  35.4 us
    ppermute x12, waiting for transfers between devices, reduce_dp(): lax.ppermute(block(me ^ first ^ far, half), 'dp', pairs[first - 1])  24.7 us
    dot_general x3, matrix products, trans_dot(): lax.dot_general(left, right, (((1,), (1,)), ((), ())), preferred_element_...  16.9 us
    unnamed x33, local copies, waits for them, and re-layouts  16.1 us
    ppermute x12, starting transfers between devices, reduce_dp(): lax.ppermute(block(me ^ first ^ far, half), 'dp', pairs[first - 1])  15.6 us
    ppermute x9, starting transfers between devices, gather_rows(): lax.ppermute(shards_in[-1], 'expert', ring_pairs(n_expert))  10.7 us
  transfers between devices with their start and end apart: 53, of which 21 were waited for; matrix products, arithmetic and copies ran while one was open for 16% of the time, Pallas kernels for 0%

profile of v1, /device:TPU:0, one launch (start us, length us, event | category | flops | bytes accessed | tf_op | source)
XLA Modules:
  0.0 267.1 jit_solution(2646711112600839742)
XLA Ops:
  12.7 19.0 %collective-permute-done.10 = f32[128,8]{0,1:T(8,128)S(1)} collective-permute-done((f32[128,8]{0,1:T(8,128)S(1)}, f32[128,8]{0,1:T(8,128)S(1)}, u32[]{:S(2)}, u32[]{:S(2)}) %collective-permute-start.10) | collective-permute-done | bytes 4128 | tf_op jit(solution)/shard_map/ppermute | solution.py:121
  46.4 7.2 %collective-permute-done.3 = bf16[128,2048]{1,0:T(8,128)(2,1)S(1)} collective-permute-done((bf16[128,2048]{1,0:T(8,128)(2,1)}, bf16[128,2048]{1,0:T(8,128)(2,1)S(1)}, u32[]{:S(2)}, u32[]{:S(2)}) %collective-permute-start.3) | collective-permute-done | bytes 524320 | tf_op jit(solution)/shard_map/ppermute | solution.py:121
  53.6 11.2 %collective-permute-done.24 = bf16[128,2048]{1,0:T(8,128)(2,1)S(1)} collective-permute-done((bf16[128,2048]{1,0:T(8,128)(2,1)S(1)}, bf16[128,2048]{1,0:T(8,128)(2,1)S(1)}, u32[]{:S(2)}, u32[]{:S(2)}) %collective-permute-start.24) | collective-permute-done | bytes 524320 | tf_op jit(solution)/shard_map/ppermute | solution.py:121
  68.2 7.9 %collective-permute-done.5 = bf16[128,2048]{1,0:T(8,128)(2,1)S(1)} collective-permute-done((bf16[128,2048]{1,0:T(8,128)(2,1)S(1)}, bf16[128,2048]{1,0:T(8,128)(2,1)S(1)}, u32[]{:S(2)}, u32[]{:S(2)}) %collective-permute-start.5) | collective-permute-done | bytes 524320 | tf_op jit(solution)/shard_map/ppermute | solution.py:121
  77.8 8.9 %collective-permute-done.26 = bf16[128,2048]{1,0:T(8,128)(2,1)S(1)} collective-permute-done((bf16[128,2048]{1,0:T(8,128)(2,1)S(1)}, bf16[128,2048]{1,0:T(8,128)(2,1)S(1)}, u32[]{:S(2)}, u32[]{:S(2)}) %collective-permute-start.26) | collective-permute-done | bytes 524320 | tf_op jit(solution)/shard_map/ppermute | solution.py:121
  89.4 5.4 %fusion.4 = f32[1024,704]{0,1:T(8,128)S(1)} fusion(bf16[1024,2048]{1,0:T(8,128)(2,1)} %constant_dynamic-update-slice_fusion, bf16[1,2048,704]{1,2,0:T(8,128)(2,1)S(1)} %copy-done.5), kind=kOutput, calls=%fused_computation.10 | convolution fusion | flops 2952790016 | bytes 9961472 | tf_op jit(solution)/shard_map/dot_general | solution.py:195
  98.0 5.0 %multiply_convert_fusion.2 = (bf16[1024,704]{0,1:T(8,128)(2,1)S(1)}, bf16[1024,704]{0,1:T(8,128)(2,1)S(1)}, bf16[1024,704]{0,1:T(8,128)(2,1)S(1)}) fusion(f32[1024,704]{0,1:T(8,128)S(1)} %fusion.8, f32[1024,704]{0,1:T(8,128)S(1)} %fusion.4, bf16[1,704,2048]{2,1,0:T(8,128)(2,1)S(1)} %copy-done, ...), kind=kOutput, calls=%fused_computation.16 | convolution fusion | flops 2969894912 | bytes 17174528 | tf_op jit(solution)/shard_map/dot_general | solution.py:16
  106.5 5.9 %fusion.6 = f32[1024,2048]{1,0:T(8,128)} fusion(bf16[1024,704]{0,1:T(8,128)(2,1)S(1)} %get-tuple-element.6, bf16[1,2048,704]{1,2,0:T(8,128)(2,1)S(1)} %copy-done.4), kind=kOutput, calls=%fused_computation.12 | convolution fusion | flops 2952790016 | bytes 12713984 | tf_op jit(solution)/shard_map/dot_general | solution.py:16
  112.4 3.6 %convolution_convert_fusion.2 = bf16[704,2048]{1,0:T(8,128)(2,1)S(1)} fusion(bf16[1024,704]{0,1:T(8,128)(2,1)S(1)} %get-tuple-element.7, bf16[1024,2048]{1,0:T(8,128)(2,1)S(1)} %constant_dynamic-update-slice_fusion.16, f32[1024]{0:T(1024)S(1)} %select_reduce_fusion), kind=kOutput, calls=%fused_computation.5 | convolution fusion | flops 2960523264 | bytes 8523776 | tf_op jit(solution)/shard_map/dot_general | solution.py:10
  116.0 4.0 %multiply_convert_fusion.1 = bf16[1024,2048]{1,0:T(8,128)(2,1)S(1)} fusion(bf16[1024,704]{0,1:T(8,128)(2,1)S(1)} %get-tuple-element.7, f32[1024]{0:T(1024)S(1)} %select_reduce_fusion, bf16[1,704,2048]{2,1,0:T(8,128)(2,1)S(1)} %copy-done), kind=kOutput, calls=%fused_computation.2 | convolution fusion | flops 2956984320 | bytes 8523776 | tf_op jit(solution)/shard_map/dot_general | solution.py:197
  129.7 5.9 %add_convert_fusion = bf16[1024,2048]{1,0:T(8,128)(2,1)S(1)} fusion(f32[1024,2048]{1,0:T(8,128)} %fusion.6, bf16[1024,704]{0,1:T(8,128)(2,1)S(1)} %get-tuple-element.5, bf16[1,2048,704]{1,2,0:T(8,128)(2,1)S(1)} %copy-done.5), kind=kOutput, calls=%fused_computation | convolution fusion | flops 2956984320 | bytes 16908288 | tf_op jit(solution)/shard_map/dot_general | solution.py:16
  136.2 10.7 %collective-permute-done.42 = bf16[256,704]{0,1:T(8,128)(2,1)S(1)} collective-permute-done((bf16[256,704]{0,1:T(8,128)(2,1)S(1)}, bf16[256,704]{0,1:T(8,128)(2,1)S(1)}, u32[]{:S(2)}, u32[]{:S(2)}) %collective-permute-start.42) | collective-permute-done | bytes 360480 | tf_op jit(solution)/shard_map/ppermute | solution.py:155
  148.5 6.1 %collective-permute-done.36 = bf16[256,704]{0,1:T(8,128)(2,1)S(1)} collective-permute-done((bf16[256,704]{0,1:T(8,128)(2,1)S(1)}, bf16[256,704]{0,1:T(8,128)(2,1)S(1)}, u32[]{:S(2)}, u32[]{:S(2)}) %collective-permute-start.36) | collective-permute-done | bytes 360480 | tf_op jit(solution)/shard_map/ppermute | solution.py:155
  163.8 9.9 %collective-permute-done.49 = bf16[704,256]{1,0:T(8,128)(2,1)S(1)} collective-permute-done((bf16[704,256]{1,0:T(8,128)(2,1)S(1)}, bf16[704,256]{1,0:T(8,128)(2,1)S(1)}, u32[]{:S(2)}, u32[]{:S(2)}) %collective-permute-start.49) | collective-permute-done | bytes 360480 | tf_op jit(solution)/shard_map/ppermute | solution.py:158
  175.6 5.8 %collective-permute-done.43 = bf16[256,704]{0,1:T(8,128)(2,1)S(1)} collective-permute-done((bf16[256,704]{0,1:T(8,128)(2,1)S(1)}, bf16[256,704]{0,1:T(8,128)(2,1)S(1)}, u32[]{:S(2)}, u32[]{:S(2)}) %collective-permute-start.43) | collective-permute-done | bytes 360480 | tf_op jit(solution)/shard_map/ppermute | solution.py:158
  183.3 5.8 %collective-permute-done.39 = bf16[256,704]{0,1:T(8,128)(2,1)S(1)} collective-permute-done((bf16[256,704]{0,1:T(8,128)(2,1)S(1)}, bf16[256,704]{0,1:T(8,128)(2,1)S(1)}, u32[]{:S(2)}, u32[]{:S(2)}) %collective-permute-start.39) | collective-permute-done | bytes 360480 | tf_op jit(solution)/shard_map/ppermute | solution.py:155
  189.2 7.7 %collective-permute-done.37 = bf16[256,704]{0,1:T(8,128)(2,1)S(1)} collective-permute-done((bf16[256,704]{0,1:T(8,128)(2,1)S(1)}, bf16[256,704]{0,1:T(8,128)(2,1)S(1)}, u32[]{:S(2)}, u32[]{:S(2)}) %collective-permute-start.37) | collective-permute-done | bytes 360480 | tf_op jit(solution)/shard_map/ppermute | solution.py:158
  201.1 9.8 %collective-permute-done.15 = bf16[128,2048]{1,0:T(8,128)(2,1)S(1)} collective-permute-done((bf16[128,2048]{1,0:T(8,128)(2,1)S(1)}, bf16[128,2048]{1,0:T(8,128)(2,1)S(1)}, u32[]{:S(2)}, u32[]{:S(2)}) %collective-permute-start.15) | collective-permute-done | bytes 524320 | tf_op jit(solution)/shard_map/ppermute | solution.py:140
  214.0 8.3 %collective-permute-done.46 = bf16[256,704]{0,1:T(8,128)(2,1)S(1)} collective-permute-done((bf16[256,704]{0,1:T(8,128)(2,1)S(1)}, bf16[256,704]{0,1:T(8,128)(2,1)S(1)}, u32[]{:S(2)}, u32[]{:S(2)}) %collective-permute-start.46) | collective-permute-done | bytes 360480 | tf_op jit(solution)/shard_map/ppermute | solution.py:158
  223.8 3.7 %collective-permute-done.40 = bf16[256,704]{0,1:T(8,128)(2,1)S(1)} collective-permute-done((bf16[256,704]{0,1:T(8,128)(2,1)S(1)}, bf16[256,704]{0,1:T(8,128)(2,1)S(1)}, u32[]{:S(2)}, u32[]{:S(2)}) %collective-permute-start.40) | collective-permute-done | bytes 360480 | tf_op jit(solution)/shard_map/ppermute | solution.py:158
  228.9 7.4 %collective-permute-done.31 = bf16[128,2048]{1,0:T(8,128)(2,1)S(1)} collective-permute-done((bf16[128,2048]{1,0:T(8,128)(2,1)S(1)}, bf16[128,2048]{1,0:T(8,128)(2,1)S(1)}, u32[]{:S(2)}, u32[]{:S(2)}) %collective-permute-start.31) | collective-permute-done | bytes 524320 | tf_op jit(solution)/shard_map/ppermute | solution.py:140
  236.6 10.9 %collective-permute-done.17 = bf16[128,2048]{1,0:T(8,128)(2,1)S(1)} collective-permute-done((bf16[128,2048]{1,0:T(8,128)(2,1)S(1)}, bf16[128,2048]{1,0:T(8,128)(2,1)S(1)}, u32[]{:S(2)}, u32[]{:S(2)}) %collective-permute-start.17) | collective-permute-done | bytes 524320 | tf_op jit(solution)/shard_map/ppermute | solution.py:140
  249.1 9.6 %collective-permute-done.33 = bf16[128,2048]{1,0:T(8,128)(2,1)S(1)} collective-permute-done((bf16[128,2048]{1,0:T(8,128)(2,1)S(1)}, bf16[128,2048]{1,0:T(8,128)(2,1)S(1)}, u32[]{:S(2)}, u32[]{:S(2)}) %collective-permute-start.33) | collective-permute-done | bytes 524320 | tf_op jit(solution)/shard_map/ppermute | solution.py:140
  259.8 6.3 %collective-permute-done.19 = bf16[128,2048]{1,0:T(8,128)(2,1)S(1)} collective-permute-done((bf16[128,2048]{1,0:T(8,128)(2,1)S(1)}, bf16[128,2048]{1,0:T(8,128)(2,1)S(1)}, u32[]{:S(2)}, u32[]{:S(2)}) %collective-permute-start.19) | collective-permute-done | bytes 524320 | tf_op jit(solution)/shard_map/ppermute | solution.py:140
  (156 shorter events, 80.0 us)
Async XLA Ops:
  5.3 32.2 %collective-permute-start.1 = (bf16[128,2048]{1,0:T(8,128)(2,1)}, bf16[128,2048]{1,0:T(8,128)(2,1)}, u32[]{:S(2)}, u32[]{:S(2)}) collective-permute-start(bf16[128,2048]{1,0:T(8,128)(2,1)} %param.7), channel_id=1, source_target_pairs={{0,2},{1,3},{2,6},{3,7},{6,4},{7,5},{4,0},{5,1},{8,10},{9,11},{10,... | collective-permute-start | bytes 1572872 | tf_op jit(solution)/shard_map/ppermute | solution.py:121
  7.9 30.7 %collective-permute-start = (bf16[128,2048]{1,0:T(8,128)(2,1)}, bf16[128,2048]{1,0:T(8,128)(2,1)}, u32[]{:S(2)}, u32[]{:S(2)}) collective-permute-start(bf16[128,2048]{1,0:T(8,128)(2,1)} %param.7), channel_id=1, source_target_pairs={{0,1},{1,0},{2,3},{3,2},{4,5},{5,4},{6,7},{7,6},{8,9},{9,8},{10,11... | collective-permute-start | bytes 1572872 | tf_op jit(solution)/shard_map/ppermute | solution.py:124
  7.9 30.6 %collective-permute-start.22 = (bf16[128,2048]{1,0:T(8,128)(2,1)}, bf16[128,2048]{1,0:T(8,128)(2,1)S(1)}, u32[]{:S(2)}, u32[]{:S(2)}) collective-permute-start(bf16[128,2048]{1,0:T(8,128)(2,1)} %param.8), channel_id=1, source_target_pairs={{0,2},{1,3},{2,6},{3,7},{6,4},{7,5},{4,0},{5,1},{8,10},{9,11},{10,... | collective-permute-start | bytes 1572872 | tf_op jit(solution)/shard_map/ppermute | solution.py:121
  37.5 27.3 %collective-permute-start.2 = (bf16[128,2048]{1,0:T(8,128)(2,1)}, bf16[128,2048]{1,0:T(8,128)(2,1)S(1)}, u32[]{:S(2)}, u32[]{:S(2)}) collective-permute-start(bf16[128,2048]{1,0:T(8,128)(2,1)} %collective-permute-done.1), channel_id=1, source_target_pairs={{0,1},{1,0},{2,3},{3,2},{4,5},{5,4},{6,7},{7,6},{8,9},{9,8},{10,11... | collective-permute-start | bytes 1572872 | tf_op jit(solution)/shard_map/ppermute | solution.py:124
  38.5 28.0 %collective-permute-start.23 = (bf16[128,2048]{1,0:T(8,128)(2,1)S(1)}, bf16[128,2048]{1,0:T(8,128)(2,1)S(1)}, u32[]{:S(2)}, u32[]{:S(2)}) collective-permute-start(bf16[128,2048]{1,0:T(8,128)(2,1)S(1)} %collective-permute-done.22), channel_id=1, source_target_pairs={{0,1},{1,0},{2,3},{3,2},{4,5},{5,4},{6,7},{7,6},{8,9},{9,8},{10,11... | collective-permute-start | bytes 1572872 | tf_op jit(solution)/shard_map/ppermute | solution.py:124
  38.6 26.2 %collective-permute-start.24 = (bf16[128,2048]{1,0:T(8,128)(2,1)S(1)}, bf16[128,2048]{1,0:T(8,128)(2,1)S(1)}, u32[]{:S(2)}, u32[]{:S(2)}) collective-permute-start(bf16[128,2048]{1,0:T(8,128)(2,1)S(1)} %collective-permute-done.22), channel_id=1, source_target_pairs={{0,2},{1,3},{2,6},{3,7},{6,4},{7,5},{4,0},{5,1},{8,10},{9,11},{10,... | collective-permute-start | bytes 1572872 | tf_op jit(solution)/shard_map/ppermute | solution.py:121
  53.6 22.5 %collective-permute-start.4 = (bf16[128,2048]{1,0:T(8,128)(2,1)S(1)}, bf16[128,2048]{1,0:T(8,128)(2,1)S(1)}, u32[]{:S(2)}, u32[]{:S(2)}) collective-permute-start(bf16[128,2048]{1,0:T(8,128)(2,1)S(1)} %collective-permute-done.3), channel_id=1, source_target_pairs={{0,1},{1,0},{2,3},{3,2},{4,5},{5,4},{6,7},{7,6},{8,9},{9,8},{10,11... | collective-permute-start | bytes 1572872 | tf_op jit(solution)/shard_map/ppermute | solution.py:124
  53.6 22.5 %collective-permute-start.5 = (bf16[128,2048]{1,0:T(8,128)(2,1)S(1)}, bf16[128,2048]{1,0:T(8,128)(2,1)S(1)}, u32[]{:S(2)}, u32[]{:S(2)}) collective-permute-start(bf16[128,2048]{1,0:T(8,128)(2,1)S(1)} %collective-permute-done.3), channel_id=1, source_target_pairs={{0,2},{1,3},{2,6},{3,7},{6,4},{7,5},{4,0},{5,1},{8,10},{9,11},{10,... | collective-permute-start | bytes 1572872 | tf_op jit(solution)/shard_map/ppermute | solution.py:121
  64.8 21.9 %collective-permute-start.25 = (bf16[128,2048]{1,0:T(8,128)(2,1)S(1)}, bf16[128,2048]{1,0:T(8,128)(2,1)S(1)}, u32[]{:S(2)}, u32[]{:S(2)}) collective-permute-start(bf16[128,2048]{1,0:T(8,128)(2,1)S(1)} %collective-permute-done.24), channel_id=1, source_target_pairs={{0,1},{1,0},{2,3},{3,2},{4,5},{5,4},{6,7},{7,6},{8,9},{9,8},{10,11... | collective-permute-start | bytes 1572872 | tf_op jit(solution)/shard_map/ppermute | solution.py:124
  64.8 21.9 %collective-permute-start.26 = (bf16[128,2048]{1,0:T(8,128)(2,1)S(1)}, bf16[128,2048]{1,0:T(8,128)(2,1)S(1)}, u32[]{:S(2)}, u32[]{:S(2)}) collective-permute-start(bf16[128,2048]{1,0:T(8,128)(2,1)S(1)} %collective-permute-done.24), channel_id=1, source_target_pairs={{0,2},{1,3},{2,6},{3,7},{6,4},{7,5},{4,0},{5,1},{8,10},{9,11},{10,... | collective-permute-start | bytes 1572872 | tf_op jit(solution)/shard_map/ppermute | solution.py:121
  121.7 34.8 %collective-permute-start.47 = (bf16[704,256]{1,0:T(8,128)(2,1)S(1)}, bf16[704,256]{1,0:T(8,128)(2,1)S(1)}, u32[]{:S(2)}, u32[]{:S(2)}) collective-permute-start(bf16[704,256]{1,0:T(8,128)(2,1)S(1)} %get-tuple-element.18), channel_id=1, source_target_pairs={{0,8},{8,0},{16,24},{24,16},{1,9},{9,1},{17,25},{25,17},{2,10},{10... | collective-permute-start | bytes 1081352 | tf_op jit(solution)/shard_map/ppermute | solution.py:155
  122.2 36.5 %collective-permute-start.51 = (bf16[704,256]{1,0:T(8,128)(2,1)S(1)}, bf16[704,256]{1,0:T(8,128)(2,1)S(1)}, u32[]{:S(2)}, u32[]{:S(2)}) collective-permute-start(bf16[704,256]{1,0:T(8,128)(2,1)S(1)} %get-tuple-element.19), channel_id=1, source_target_pairs={{0,16},{8,24},{16,0},{24,8},{1,17},{9,25},{17,1},{25,9},{2,18},{10... | collective-permute-start | bytes 1081352 | tf_op jit(solution)/shard_map/ppermute | solution.py:155
  129.1 25.5 %collective-permute-start.36 = (bf16[256,704]{0,1:T(8,128)(2,1)S(1)}, bf16[256,704]{0,1:T(8,128)(2,1)S(1)}, u32[]{:S(2)}, u32[]{:S(2)}) collective-permute-start(bf16[256,704]{0,1:T(8,128)(2,1)S(1)} %get-tuple-element.33), channel_id=1, source_target_pairs={{0,8},{8,0},{16,24},{24,16},{1,9},{9,1},{17,25},{25,17},{2,10},{10... | collective-permute-start | bytes 1081352 | tf_op jit(solution)/shard_map/ppermute | solution.py:155
  154.7 20.8 %collective-permute-start.45 = (bf16[256,704]{0,1:T(8,128)(2,1)S(1)}, bf16[256,704]{0,1:T(8,128)(2,1)S(1)}, u32[]{:S(2)}, u32[]{:S(2)}) collective-permute-start(bf16[256,704]{0,1:T(8,128)(2,1)S(1)} %get-tuple-element.25), channel_id=1, source_target_pairs={{0,16},{8,24},{16,0},{24,8},{1,17},{9,25},{17,1},{25,9},{2,18},{10... | collective-permute-start | bytes 1081352 | tf_op jit(solution)/shard_map/ppermute | solution.py:155
  157.0 24.4 %collective-permute-start.43 = (bf16[256,704]{0,1:T(8,128)(2,1)S(1)}, bf16[256,704]{0,1:T(8,128)(2,1)S(1)}, u32[]{:S(2)}, u32[]{:S(2)}) collective-permute-start(bf16[256,704]{0,1:T(8,128)(2,1)S(1)} %add_convert_fusion.12), channel_id=1, source_target_pairs={{0,16},{8,24},{16,0},{24,8},{1,17},{9,25},{17,1},{25,9},{2,18},{10... | collective-permute-start | bytes 1081352 | tf_op jit(solution)/shard_map/ppermute | solution.py:158
  158.7 23.1 %collective-permute-start.35 = (bf16[256,704]{0,1:T(8,128)(2,1)S(1)}, bf16[256,704]{0,1:T(8,128)(2,1)S(1)}, u32[]{:S(2)}, u32[]{:S(2)}) collective-permute-start(bf16[256,704]{0,1:T(8,128)(2,1)S(1)} %get-tuple-element.30), channel_id=1, source_target_pairs={{0,8},{8,0},{16,24},{24,16},{1,9},{9,1},{17,25},{25,17},{2,10},{10... | collective-permute-start | bytes 1081352 | tf_op jit(solution)/shard_map/ppermute | solution.py:155
  162.3 26.9 %collective-permute-start.39 = (bf16[256,704]{0,1:T(8,128)(2,1)S(1)}, bf16[256,704]{0,1:T(8,128)(2,1)S(1)}, u32[]{:S(2)}, u32[]{:S(2)}) collective-permute-start(bf16[256,704]{0,1:T(8,128)(2,1)S(1)} %get-tuple-element.31), channel_id=1, source_target_pairs={{0,16},{8,24},{16,0},{24,8},{1,17},{9,25},{17,1},{25,9},{2,18},{10... | collective-permute-start | bytes 1081352 | tf_op jit(solution)/shard_map/ppermute | solution.py:155
  173.7 23.2 %collective-permute-start.37 = (bf16[256,704]{0,1:T(8,128)(2,1)S(1)}, bf16[256,704]{0,1:T(8,128)(2,1)S(1)}, u32[]{:S(2)}, u32[]{:S(2)}) collective-permute-start(bf16[256,704]{0,1:T(8,128)(2,1)S(1)} %add_convert_fusion.14), channel_id=1, source_target_pairs={{0,16},{8,24},{16,0},{24,8},{1,17},{9,25},{17,1},{25,9},{2,18},{10... | collective-permute-start | bytes 1081352 | tf_op jit(solution)/shard_map/ppermute | solution.py:158
  175.5 21.7 %collective-permute-start.30 = (bf16[128,2048]{1,0:T(8,128)(2,1)S(1)}, bf16[128,2048]{1,0:T(8,128)(2,1)S(1)}, u32[]{:S(2)}, u32[]{:S(2)}) collective-permute-start(bf16[128,2048]{1,0:T(8,128)(2,1)S(1)} %get-tuple-element.11), channel_id=1, source_target_pairs={{0,1},{1,0},{2,3},{3,2},{4,5},{5,4},{6,7},{7,6},{8,9},{9,8},{10,11... | collective-permute-start | bytes 1572872 | tf_op jit(solution)/shard_map/ppermute | solution.py:135
  181.7 31.0 %collective-permute-start.50 = (bf16[704,256]{1,0:T(8,128)(2,1)S(1)}, bf16[704,256]{1,0:T(8,128)(2,1)S(1)}, u32[]{:S(2)}, u32[]{:S(2)}) collective-permute-start(bf16[704,256]{1,0:T(8,128)(2,1)S(1)} %get-tuple-element.20), channel_id=1, source_target_pairs={{0,16},{8,24},{16,0},{24,8},{1,17},{9,25},{17,1},{25,9},{2,18},{10... | collective-permute-start | bytes 1081352 | tf_op jit(solution)/shard_map/ppermute | solution.py:155
  198.8 25.0 %collective-permute-start.38 = (bf16[256,704]{0,1:T(8,128)(2,1)S(1)}, bf16[256,704]{0,1:T(8,128)(2,1)S(1)}, u32[]{:S(2)}, u32[]{:S(2)}) collective-permute-start(bf16[256,704]{0,1:T(8,128)(2,1)S(1)} %get-tuple-element.32), channel_id=1, source_target_pairs={{0,16},{8,24},{16,0},{24,8},{1,17},{9,25},{17,1},{25,9},{2,18},{10... | collective-permute-start | bytes 1081352 | tf_op jit(solution)/shard_map/ppermute | solution.py:155
  212.8 36.3 %collective-permute-start.34 = (bf16[128,2048]{1,0:T(8,128)(2,1)S(1)}, bf16[128,2048]{1,0:T(8,128)(2,1)S(1)}, u32[]{:S(2)}, u32[]{:S(2)}) collective-permute-start(bf16[128,2048]{1,0:T(8,128)(2,1)S(1)} %get-tuple-element.9), channel_id=1, source_target_pairs={{0,1},{1,0},{2,3},{3,2},{4,5},{5,4},{6,7},{7,6},{8,9},{9,8},{10,11... | collective-permute-start | bytes 1572872 | tf_op jit(solution)/shard_map/ppermute | solution.py:135
  228.9 30.9 %collective-permute-start.20 = (bf16[128,2048]{1,0:T(8,128)(2,1)S(1)}, bf16[128,2048]{1,0:T(8,128)(2,1)S(1)}, u32[]{:S(2)}, u32[]{:S(2)}) collective-permute-start(bf16[128,2048]{1,0:T(8,128)(2,1)S(1)} %get-tuple-element.13), channel_id=1, source_target_pairs={{0,1},{1,0},{2,3},{3,2},{4,5},{5,4},{6,7},{7,6},{8,9},{9,8},{10,11... | collective-permute-start | bytes 1572872 | tf_op jit(solution)/shard_map/ppermute | solution.py:135
  236.5 22.2 %collective-permute-start.33 = (bf16[128,2048]{1,0:T(8,128)(2,1)S(1)}, bf16[128,2048]{1,0:T(8,128)(2,1)S(1)}, u32[]{:S(2)}, u32[]{:S(2)}) collective-permute-start(bf16[128,2048]{1,0:T(8,128)(2,1)S(1)} %add_convert_fusion.2), channel_id=1, source_target_pairs={{0,2},{1,3},{2,6},{3,7},{6,4},{7,5},{4,0},{5,1},{8,10},{9,11},{10,... | collective-permute-start | bytes 1572872 | tf_op jit(solution)/shard_map/ppermute | solution.py:140
  (35 other events, 549.9 us)

commit v2 on v0

--- a/solution.py
+++ b/solution.py
@@ -3,6 +3,8 @@
 import jax
 import jax.numpy as jnp
 from jax import lax
+from jax.experimental import pallas as pl
+from jax.experimental.pallas import tpu as pltpu
 from jax.sharding import PartitionSpec as P
 
 
@@ -36,7 +38,7 @@
     return (d_rows, d_gate, d_up)
 
 
-def shards(tokens, cotangent, expert_ids, gate_fixed, w_gate, w_up, w_down):
+def slot_shards(tokens, cotangent, expert_ids, gate_fixed, w_gate, w_up, w_down):
     n_expert = lax.axis_size("expert")
     tok_rows = tokens.shape[0]
     width = tokens.shape[1]
@@ -101,6 +103,396 @@
     return (mixed, token_grad, grad_gate[None], grad_up[None], grad_down[None])
 
 
+BF16, F32 = jnp.bfloat16, jnp.float32
+VMEM = pl.BlockSpec(memory_space=pltpu.VMEM)
+SMEM = pl.BlockSpec(memory_space=pltpu.SMEM)
+PIECES = ((1, 0), (3, 0), (2, 1), (3, 1), (0, 0), (2, 0), (0, 1), (1, 1))
+
+
+def tie(*values):
+    return lax.optimization_barrier(values)
+
+
+def nt(left, right):
+    return lax.dot_general(left, right, (((1,), (1,)), ((), ())), preferred_element_type=F32)
+
+
+def nn(left, right):
+    return lax.dot_general(left, right, (((1,), (0,)), ((), ())), preferred_element_type=F32)
+
+
+def tn(left, right):
+    return lax.dot_general(left, right, (((0,), (0,)), ((), ())), preferred_element_type=F32)
+
+
+def call(name, kernel, outs, ins, scratch=(), smem=0):
+    return list(pl.pallas_call(
+        kernel,
+        name=name,
+        out_shape=[jax.ShapeDtypeStruct(shape, dtype) for shape, dtype in outs],
+        in_specs=[SMEM] * smem + [VMEM] * (len(ins) - smem),
+        out_specs=[VMEM] * len(outs),
+        scratch_shapes=[pltpu.VMEM(shape, dtype) for shape, dtype in scratch],
+        compiler_params=pltpu.CompilerParams(vmem_limit_bytes=16 * 1024 * 1024),
+        cost_estimate=pl.CostEstimate(flops=1, bytes_accessed=1, transcendentals=0),
+    )(*ins))
+
+
+def per_row(weights, row, width):
+    count = weights.shape[1]
+    square = jnp.broadcast_to(weights[row : row + 1, :], (count, count)).T
+    return jnp.concatenate([square] * (width // count), axis=1)
+
+
+def split_kernel(offs, whole, part_s, part_k):
+    size = whole.shape[1] // 8
+    for at in range(8):
+        here = pl.ds(pl.multiple_of(offs[at], size), size)
+        (part_s if at < 4 else part_k)[:, pl.ds(at % 4 * size, size)] = whole[:, here]
+
+
+def forward_kernel(
+    slot, offs, weights, mine_a, mine_b, other_a, other_b, gate, up, down, hid, fac_g, fac_u, out_m, out_o, rows_s, rows_k, rows
+):
+    n, width = out_m.shape
+    size = width // 8
+    stack((mine_a, mine_b, other_a, other_b), rows)
+    gate_pre = nt(rows[...], gate[...])
+    up_pre = nt(rows[...], up[...])
+    sigma = jax.nn.sigmoid(gate_pre)
+    activ = gate_pre * sigma
+    hidden = (activ * up_pre).astype(BF16)
+    hid[...] = hidden
+    fac_g[...] = up_pre * (sigma * (1.0 + gate_pre * (1.0 - sigma)))
+    fac_u[...] = activ
+    out = nn(hidden, down[...])
+    out_m[...] = (out[:n] * per_row(weights[...], slot, width)).astype(BF16)
+    out_o[...] = (out[n:] * per_row(weights[...], slot + 4, width)).astype(BF16)
+    for at in range(8):
+        here = pl.ds(pl.multiple_of(offs[at], size), size)
+        (rows_s if at < 4 else rows_k)[:, pl.ds(at % 4 * size, size)] = rows[:, here]
+
+
+def fill_dy(weights, cots, dy):
+    n, width = cots[0].shape
+    for slot in range(4):
+        for core in range(2):
+            row = slot + 4 * core
+            at = (2 * slot + core) * n
+            dy[at : at + n, :] = (cots[row][...].astype(F32) * per_row(weights[...], row, width)).astype(BF16)
+
+
+def early_kernel(weights, *refs):
+    cots, hids, (down, sent_a, sent_b, d_hid, dy, hid) = refs[:8], refs[8:12], refs[12:]
+    n = hids[0].shape[0]
+    fill_dy(weights, cots, dy)
+    for slot in range(4):
+        hid[slot * n : (slot + 1) * n, :] = hids[slot][...]
+    half = dy.shape[1] // 2
+    sent_a[...] = tn(hid[...], dy[:, :half]).astype(BF16)
+    sent_b[...] = tn(hid[...], dy[:, half:]).astype(BF16)
+    for at in range(2):
+        part = pl.ds(at * 2 * n, 2 * n)
+        d_hid[part, :] = nt(dy[part, :], down[...])
+
+
+def late_kernel(weights, *refs):
+    cots, facs_g, facs_u, (d_early, down, d_gate, d_up, dy) = refs[:8], refs[8:12], refs[12:16], refs[16:]
+    n = facs_g[0].shape[0]
+    fill_dy(weights, cots, dy)
+    for slot in range(4):
+        part = pl.ds(slot * n, n)
+        d_hid = d_early[part, :] + nt(dy[part, :], down[...])
+        d_gate[part, :] = (d_hid * facs_g[slot][...]).astype(BF16)
+        d_up[part, :] = (d_hid * facs_u[slot][...]).astype(BF16)
+
+
+def stack(parts, whole):
+    n = parts[0].shape[0]
+    for at, part in enumerate(parts):
+        whole[at * n : (at + 1) * n, :] = part[...]
+
+
+def grads_kernel(left, *refs):
+    rights, (out_a, out_b, right) = refs[:-3], refs[-3:]
+    stack(rights, right)
+    half = right.shape[1] // 2
+    out_a[...] = tn(left[...], right[:, :half]).astype(BF16)
+    out_b[...] = tn(left[...], right[:, half:]).astype(BF16)
+
+
+def hidden_grads_kernel(right, *refs):
+    hids, (out_a, out_b, left) = refs[:4], refs[4:]
+    stack(hids, left)
+    half = right.shape[1] // 2
+    out_a[...] = tn(left[...], right[:, :half]).astype(BF16)
+    out_b[...] = tn(left[...], right[:, half:]).astype(BF16)
+
+
+def cross_kernel(count, *refs):
+    ins, (far_a, far_b, near_a, near_b) = refs[: 4 * count], refs[4 * count :]
+    cut = far_a.shape[2]
+    for at in range(count):
+        came_a, came_b, own_a, own_b = ins[4 * at : 4 * at + 4]
+        for came, own, far, near in ((came_a, own_a, far_a, near_a), (came_b, own_b, far_b, near_b)):
+            both = came[...].astype(F32) + own[...].astype(F32)
+            near[at, :, :] = both[:, :cut]
+            far[at, :, :] = both[:, cut:].astype(BF16)
+
+
+def rows_kernel(slots, d_gate, d_up, gate, up, mine, other):
+    n = mine.shape[0] // len(slots)
+    for at, slot in enumerate(slots):
+        part = pl.ds(slot * 2 * n, 2 * n)
+        both = nn(d_gate[part, :], gate[...]) + nn(d_up[part, :], up[...])
+        mine[at * n : (at + 1) * n, :] = both[:n].astype(BF16)
+        other[at * n : (at + 1) * n, :] = both[n:].astype(BF16)
+
+
+def ring_order(count):
+    return [0] + list(range(1, count, 2)) + [at for at in range(count - 1, 1, -1) if at % 2 == 0]
+
+
+def step(value, n_expert):
+    order = ring_order(n_expert // 2)
+    follow = {at: order[(spot + 1) % len(order)] for spot, at in enumerate(order)}
+    return lax.ppermute(value, "expert", [(2 * at + core, 2 * follow[at] + core) for at in order for core in range(2)])
+
+
+def swap(value, n_expert):
+    return lax.ppermute(value, "expert", [(at, at ^ 1) for at in range(n_expert)])
+
+
+def flip(value, mask):
+    return lax.ppermute(value, "dp", [(at, at ^ mask) for at in range(4)])
+
+
+def add(*values):
+    return sum(value.astype(F32) for value in values)
+
+
+def slot_weights(expert_ids, gate_fixed, n_expert):
+    gate_values = gate_fixed.astype(F32) / 65536.0
+    experts = jnp.arange(n_expert, dtype=jnp.int32)[:, None, None]
+    table = jnp.sum(jnp.where(expert_ids.T[None] == jnp.broadcast_to(experts, (n_expert, 1, 1)), gate_values.T[None], 0.0), axis=1)
+    came = lax.all_to_all(table, "expert", split_axis=0, concat_axis=0, tiled=True)
+    me = lax.axis_index("expert")
+    order = ring_order(n_expert // 2)
+    spot = sum(jnp.where(me // 2 == at, where, 0) for where, at in enumerate(order))
+    rows = []
+    for core in (0, 1):
+        for slot in range(n_expert // 2):
+            back = lax.rem(spot - slot + len(order), len(order))
+            chip = sum(jnp.where(back == where, at, 0) for where, at in enumerate(order))
+            rows.append(2 * chip + lax.rem(me + core, 2))
+    source = jnp.stack(rows)
+    return jnp.sum(jnp.where(source[:, None, None] == jnp.arange(n_expert)[None, :, None], came[None], 0.0), axis=1)
+
+
+class Order:
+    def __init__(self, start):
+        self.last = start
+
+    def point(self, *values):
+        *values, self.last = lax.optimization_barrier((*values, self.last))
+        return values
+
+    def after(self, value):
+        return lax.optimization_barrier((value, self.last))[0]
+
+
+def dense_shards(tokens, cotangent, expert_ids, gate_fixed, w_gate, w_up, w_down):
+    n_expert = lax.axis_size("expert")
+    n, width = tokens.shape
+    ff = w_gate.shape[2]
+    half, cut = width // 2, width // 8
+
+    def ring(value, name):
+        with jax.named_scope(name):
+            return step(order.after(value), n_expert)
+
+    def twin(value, name):
+        with jax.named_scope(name):
+            return swap(order.after(value), n_expert)
+
+    def flips(pair, masks, name):
+        with jax.named_scope(name):
+            return [flip(order.after(value), mask) for value, mask in zip(pair, masks)]
+
+    def launch(name, kernel, outs, ins, scratch=(), smem=0):
+        return call(name, kernel, outs, [*ins[:smem], order.after(ins[smem]), *ins[smem + 1 :]], scratch, smem)
+
+    gate_w, up_w, down_w = w_gate[0].T, w_up[0].T, w_down[0]
+    me = lax.axis_index("dp")
+    offs = jnp.stack([((me ^ rel) * 2 + part) * (width // 8) for rel, part in PIECES]).astype(jnp.int32)
+
+    def forward(slot, mine_a, mine_b, other_a, other_b):
+        pair = 2 * n
+        return launch(
+            f"forward_{slot}",
+            partial(forward_kernel, slot),
+            [((pair, ff), BF16), ((pair, ff), F32), ((pair, ff), F32), ((n, width), BF16), ((n, width), BF16),
+             ((pair, half), BF16), ((pair, half), BF16)],
+            [offs, weights, mine_a, mine_b, other_a, other_b, gate_w, up_w, down_w],
+            [((pair, width), BF16)],
+            smem=1,
+        )
+
+    def row_grads(name, slots):
+        return launch(
+            name,
+            partial(rows_kernel, slots),
+            [((len(slots) * n, width), BF16)] * 2,
+            [d_gate, d_up, gate_w, up_w],
+        )
+
+    def pick(value, which):
+        return value[which * (n // 2) : (which + 1) * (n // 2)]
+
+    def kept(mine, other, which=None):
+        return add(mine, other) if which is None else add(pick(mine, which), pick(other, which))
+
+    def split(name, value):
+        return launch(name, split_kernel, [((value.shape[0], half), BF16)] * 2, [offs, value], smem=1)
+
+    def grads(name, left, rights):
+        return launch(name, grads_kernel, [((ff, half // 2), BF16)] * 2, [left, *rights], [((8 * n, half), BF16)])
+
+    def cross(name, *pairs):
+        count = len(pairs)
+        *sums, near_a, near_b = launch(
+            name,
+            partial(cross_kernel, count),
+            [((count, ff, cut), BF16)] * 2 + [((count, ff, cut), F32)] * 2,
+            [value for came, own in pairs for value in (*came, *own)],
+        )
+        return sums, (near_a, near_b)
+
+    def total(near, last, at):
+        return jnp.concatenate([add(part[at], more[at]) for part, more in zip(near, last)], axis=1)
+
+    def whole(part_a, part_b, mine, other):
+        return jnp.concatenate(
+            [add(part_a, kept(mine, other, 0)), add(part_b, kept(mine, other, 1))], axis=0
+        ).astype(BF16)
+
+    order = Order(jnp.zeros((8, 128), F32))
+    a0, b0 = pick(tokens, 0), pick(tokens, 1)
+    a1, b1 = ring(a0, "ta1"), ring(b0, "tb1")
+    s0, k0 = split("split_cot", cotangent)
+    s1 = ring(s0, "s1")
+    ap0, bp0 = twin(a0, "ap0"), twin(b0, "bp0")
+    weights = slot_weights(expert_ids, gate_fixed, n_expert)
+    down_s, down_k = split("split_down", down_w)
+    a1, s0, k0, weights, down_s, down_k = order.point(a1, s0, k0, weights, down_s, down_k)
+    a2, ap1 = ring(a1, "ta2"), twin(a1, "ap1")
+    (b1,) = order.point(b1)
+    b2, bp1 = ring(b1, "tb2"), twin(b1, "bp1")
+    (s1,) = order.point(s1)
+    s2, sp0 = ring(s1, "s2"), twin(s0, "sp0")
+    f0 = forward(0, a0, b0, ap0, bp0)
+    a2, *f0 = order.point(a2, *f0)
+    a3, ap2 = ring(a2, "ta3"), twin(a2, "ap2")
+    (b2,) = order.point(b2)
+    b3, bp2 = ring(b2, "tb3"), twin(b2, "bp2")
+    f1 = forward(1, a1, b1, ap1, bp1)
+    s2, *f1 = order.point(s2, *f1)
+    s3, sp1 = ring(s2, "s3"), twin(s1, "sp1")
+    o1 = twin(f1[4], "o1")
+    (a3,) = order.point(a3)
+    k1, ap3 = ring(k0, "k1"), twin(a3, "ap3")
+    b3, o1 = order.point(b3, o1)
+    bp3 = twin(b3, "bp3")
+    m_a = ring(kept(f1[3], o1, 0).astype(BF16), "ma1")
+    f2 = forward(2, a2, b2, ap2, bp2)
+    s3, *f2 = order.point(s3, *f2)
+    sp2, sp3, o2 = twin(s2, "sp2"), twin(s3, "sp3"), twin(f2[4], "o2")
+    f3 = forward(3, a3, b3, ap3, bp3)
+    k1, *f3 = order.point(k1, *f3)
+    k2, kp0, kp1 = ring(k1, "k2"), twin(k0, "kp0"), twin(k1, "kp1")
+    hids, facs_g, facs_u, outs_m = ([f[at] for f in (f0, f1, f2, f3)] for at in range(4))
+    rows_s, rows_k = ([f[at] for f in (f0, f1, f2, f3)] for at in (5, 6))
+    *sent, d_early = launch(
+        "early",
+        early_kernel,
+        [((ff, half // 2), BF16)] * 2 + [((8 * n, ff), F32)],
+        [weights, s0, s1, s2, s3, sp0, sp1, sp2, sp3, *hids, down_s],
+        [((8 * n, half), BF16), ((8 * n, ff), BF16)],
+    )
+    m_a, o2, d_early, *sent = order.point(m_a, o2, d_early, *sent)
+    down_came = flips(sent, (1, 2), "d1")
+    m_a = ring(add(m_a, kept(outs_m[2], o2, 0)).astype(BF16), "ma2")
+    o3 = twin(f3[4], "o3")
+    (k2,) = order.point(k2)
+    k3, kp2 = ring(k2, "k3"), twin(k2, "kp2")
+    m_a, o3 = order.point(m_a, o3)
+    m_a = ring(add(m_a, kept(outs_m[3], o3, 0)).astype(BF16), "ma3")
+    (k3,) = order.point(k3)
+    kp3 = twin(k3, "kp3")
+    m_b = ring(kept(outs_m[1], o1, 1).astype(BF16), "mb1")
+    d_gate, d_up, dy_k = launch(
+        "late",
+        late_kernel,
+        [((8 * n, ff), BF16)] * 2 + [((8 * n, half), BF16)],
+        [weights, k0, k1, k2, k3, kp0, kp1, kp2, kp3, *facs_g, *facs_u, d_early, down_k],
+    )
+    d_gate, d_up, dy_k, *down_came = order.point(d_gate, d_up, dy_k, *down_came)
+    sent = grads("gate_s", d_gate, rows_s)
+    d_up, m_a, *sent = order.point(d_up, m_a, *sent)
+    gate_came = flips(sent, (1, 2), "g1")
+    near_m, near_o = row_grads("rows_near", (1, 2))
+    m_b, near_m, near_o, d_up = order.point(m_b, near_m, near_o, d_up)
+    near_o = twin(near_o, "no")
+    m_b = ring(add(m_b, kept(outs_m[2], o2, 1)).astype(BF16), "mb2")
+    sent = grads("up_s", d_up, rows_s)
+    d_gate, d_up, near_o, *sent = order.point(d_gate, d_up, near_o, *sent)
+    up_came = flips(sent, (1, 2), "u1")
+    g_a = ring(kept(near_m[:n], near_o[:n], 0).astype(BF16), "ga1")
+    far_m, far_o = row_grads("rows_far", (3, 0))
+    far_m, far_o, dy_k = order.point(far_m, far_o, dy_k)
+    down_own = launch(
+        "down_k", hidden_grads_kernel, [((ff, half // 2), BF16)] * 2, [dy_k, *hids], [((8 * n, ff), BF16)]
+    )
+    m_b, d_gate, *down_own = order.point(m_b, d_gate, *down_own)
+    m_b = ring(add(m_b, kept(outs_m[3], o3, 1)).astype(BF16), "mb3")
+    far_o, o0 = twin(far_o, "fo"), twin(f0[4], "o0")
+    gate_own = grads("gate_k", d_gate, rows_k)
+    g_a, d_up, *gate_own = order.point(g_a, d_up, *gate_own)
+    g_a = ring(add(g_a, kept(near_m[n:], near_o[n:], 0)).astype(BF16), "ga2")
+    g_b = ring(kept(near_m[:n], near_o[:n], 1).astype(BF16), "gb1")
+    up_own = grads("up_k", d_up, rows_k)
+    gate_came[0], gate_came[1], *up_own = order.point(*gate_came, *up_own)
+    first_far, first_near = cross("first_cross", (down_came, down_own), (gate_came, gate_own))
+    m_b, o0, *rest = order.point(m_b, o0, *first_far, *first_near)
+    first_far, first_near = rest[:2], rest[2:]
+    first_last = flips(first_far, (2, 1), "dg2")
+    g_a, far_o = order.point(g_a, far_o)
+    g_a = ring(add(g_a, kept(far_m[:n], far_o[:n], 0)).astype(BF16), "ga3")
+    (g_b,) = order.point(g_b)
+    g_b = ring(add(g_b, kept(near_m[n:], near_o[n:], 1)).astype(BF16), "gb2")
+    mixed = whole(m_a, m_b, outs_m[0], o0)
+    up_came = order.point(*up_came)
+    up_far, up_near = cross("up_cross", (up_came, up_own))
+    up_far = order.point(*up_far)
+    up_last = flips(up_far, (2, 1), "u2")
+    g_b, mixed = order.point(g_b, mixed)
+    g_b = ring(add(g_b, kept(far_m[:n], far_o[:n], 1)).astype(BF16), "gb3")
+    first_last = order.point(*first_last)
+    grad_down, grad_gate = total(first_near, first_last, 0), total(first_near, first_last, 1)
+    grad_up = total(up_near, up_last, 0)
+    token_grad = whole(g_a, g_b, far_m[n:], far_o[n:])
+    return (mixed, token_grad, grad_gate.T[None], grad_up.T[None], grad_down[None])
+
+
+def shards(tokens, cotangent, expert_ids, gate_fixed, w_gate, w_up, w_down):
+    n_expert = lax.axis_size("expert")
+    rows, width = tokens.shape
+    capacity = 4 * rows * expert_ids.shape[1] // (3 * n_expert)
+    dense = capacity >= rows and n_expert == 8 and lax.axis_size("dp") == 4 and rows == 128 and width % 2048 == 0
+    run = dense_shards if dense else slot_shards
+    return run(tokens, cotangent, expert_ids, gate_fixed, w_gate, w_up, w_down)
+
+
 def solution(mesh):
     in_specs = (
         P(("dp", "expert"), None),

time: 480 us -> 191 us (0.40)
  waiting for transfers between devices: 293 us -> 82.3 us
  matrix products: 60.4 us -> 0 us
  local copies, waits for them, and re-layouts: 56.4 us -> 9.66 us
  Pallas kernels: 0 us -> 40.2 us
  starting transfers between devices: 21.2 us -> 47.4 us
  other arithmetic: 33.7 us -> 9.88 us
  between operations: 14 us -> 1.08 us
    all_to_all x4 -> x1, waiting for transfers between devices: 254 us -> 0.01 us  [slot_weights(): lax.all_to_all(table, 'expert', split_axis=0, concat_axis=0, tiled=True)]
    ppermute x0 -> x56, waiting for transfers between devices: none -> 82.3 us  [the longest x24 48.5 us: step(): lax.ppermute(value, 'expert', [(2 * at + core, 2 * follow[at] + core) for...]
    dot_general x9 -> x0, matrix products: 60.4 us -> none  [the longest x3 20.1 us: contract(): lax.dot_general(left, right, (((0,), (0,)), ((), ())), preferred_element_...]
    ppermute x0 -> x56, starting transfers between devices: none -> 44.1 us  [the longest x24 27.3 us: step(): lax.ppermute(value, 'expert', [(2 * at + core, 2 * follow[at] + core) for...]
    pallas_call x0 -> x17, Pallas kernels: none -> 40.2 us  [call(): pl.pallas_call(kernel, name=name, out_shape=[jax.ShapeDtypeStruct(shape,...]
    reduce_scatter x3 -> x0, waiting for transfers between devices: 38.1 us -> none  [the longest x1 38.1 us: shards(): lax.psum_scatter(fold_rows(received, d_gate).astype(jnp.bfloat16), 'dp',...]
    gather x5 -> x0, local copies, waits for them, and re-layouts: 38.1 us -> none  [the longest x2 16.3 us: shards(): back_rows[slot_of].astype(jnp.float32).reshape(tok_rows, top_k, width)]
    all_to_all x4 -> x1, starting transfers between devices: 20.4 us -> 3.31 us  [slot_weights(): lax.all_to_all(table, 'expert', split_axis=0, concat_axis=0, tiled=True)]
  transfers between devices with their start and end apart: 7 -> 57, of which waited for: 5 -> 24; matrix products, arithmetic and copies ran while one was open for 18% -> 5% of each run, Pallas kernels for 0% -> 21%
where the time goes in v2:
time: 191 us
  waiting for transfers between devices  82.3 us (43%)
  starting transfers between devices  47.4 us (25%)
  Pallas kernels  40.2 us (21%)
  other arithmetic  9.88 us (5%)
  local copies, waits for them, and re-layouts  9.66 us (5%)
    ppermute x24, waiting for transfers between devices, step(): lax.ppermute(value, 'expert', [(2 * at + core, 2 * follow[at] + core) for...  48.5 us
    pallas_call x17, Pallas kernels, call(): pl.pallas_call(kernel, name=name, out_shape=[jax.ShapeDtypeStruct(shape,...  40.2 us
    ppermute x10, waiting for transfers between devices, flip(): return lax.ppermute(value, 'dp', [(at, at ^ mask) for at in range(4)])  31.9 us
    ppermute x24, starting transfers between devices, step(): lax.ppermute(value, 'expert', [(2 * at + core, 2 * follow[at] + core) for...  27.3 us
    ppermute x10, starting transfers between devices, flip(): return lax.ppermute(value, 'dp', [(at, at ^ mask) for at in range(4)])  12.1 us
    unnamed x24, local copies, waits for them, and re-layouts  8.37 us
    ppermute x22, starting transfers between devices, swap(): lax.ppermute(value, 'expert', [(at, at ^ 1) for at in range(n_expert)])  4.69 us
  transfers between devices with their start and end apart: 57, of which 24 were waited for; matrix products, arithmetic and copies ran while one was open for 5% of the time, Pallas kernels for 21%

profile of v2, /device:TPU:0, one launch (start us, length us, event | category | flops | bytes accessed | tf_op | source)
XLA Modules:
  0.0 190.5 jit_solution(904495044151876837)
XLA Ops:
  2.3 2.6 %collective-permute-start.2 = (bf16[64,2048]{1,0:T(8,128)(2,1)S(1)}, bf16[64,2048]{1,0:T(8,128)(2,1)}, u32[]{:S(2)}, u32[]{:S(2)}) collective-permute-start(bf16[64,2048]{1,0:T(8,128)(2,1)S(1)} %get-tuple-element.265.mine_a), channel_id=1, source_target_pairs={{0,2},{1,3},{2,6},{3,7},{6,4},{7,5},{4,0},{5,1},{8,10},{9,11},{10,... | collective-permute-start | bytes 786440 | tf_op jit(solution)/shard_map/ta1/ppermute | solution.py:259
  5.1 2.6 %collective-permute-start.1 = (bf16[64,2048]{1,0:T(8,128)(2,1)S(1)}, bf16[64,2048]{1,0:T(8,128)(2,1)}, u32[]{:S(2)}, u32[]{:S(2)}) collective-permute-start(bf16[64,2048]{1,0:T(8,128)(2,1)S(1)} %get-tuple-element.264.mine_b), channel_id=1, source_target_pairs={{0,2},{1,3},{2,6},{3,7},{6,4},{7,5},{4,0},{5,1},{8,10},{9,11},{10,... | collective-permute-start | bytes 786440 | tf_op jit(solution)/shard_map/tb1/ppermute | solution.py:259
  9.7 3.3 %all-to-all-start = ((f32[8,1,128]{2,1,0:T(1,128)}), f32[8,1,128]{2,1,0:T(1,128)S(1)}, u32[]{:S(2)}, u32[]{:S(2)}) async-start(f32[8,1,128]{2,1,0:T(1,128)} %bitcast.19), calls=%async_computation | async-start | bytes 8192 | tf_op jit(solution)/shard_map/all_to_all | solution.py:278
  29.8 4.1 %forward_0.1 = (bf16[256,704]{1,0:T(8,128)(2,1)S(1)}, f32[256,704]{1,0:T(8,128)S(1)}, f32[256,704]{1,0:T(8,128)S(1)}, bf16[128,2048]{1,0:T(8,128)(2,1)S(1)}, bf1...) custom-call(s32[8]{0:T(128)S(1)} %stack.62.offs, ...), custom_call_target="tpu_custom_call" | custom-call | flops 1 | bytes 1 | tf_op jit(solution)/shard_map/forward_0/pallas_call | solution.py:129
  34.0 4.3 %collective-permute-done.4.mine_b = bf16[64,2048]{1,0:T(8,128)(2,1)S(1)} collective-permute-done((bf16[64,2048]{1,0:T(8,128)(2,1)}, bf16[64,2048]{1,0:T(8,128)(2,1)S(1)}, u32[]{:S(2)}, u32[]{:S(2)}) %collective-permute-start.4) | collective-permute-done | bytes 262176 | tf_op jit(solution)/shard_map/tb2/ppermute | solution.py:259
  38.3 4.0 %forward_1.1 = (bf16[256,704]{1,0:T(8,128)(2,1)S(1)}, f32[256,704]{1,0:T(8,128)S(1)}, f32[256,704]{1,0:T(8,128)S(1)}, bf16[128,2048]{1,0:T(8,128)(2,1)S(1)}, bf1...) custom-call(s32[8]{0:T(128)S(1)} %stack.62.offs, ...), custom_call_target="tpu_custom_call" | custom-call | flops 1 | bytes 1 | tf_op jit(solution)/shard_map/forward_1/pallas_call | solution.py:129
  46.0 6.8 %collective-permute-done.12.mine_a = bf16[64,2048]{1,0:T(8,128)(2,1)S(1)} collective-permute-done((bf16[64,2048]{1,0:T(8,128)(2,1)S(1)}, bf16[64,2048]{1,0:T(8,128)(2,1)S(1)}, u32[]{:S(2)}, u32[]{:S(2)}) %collective-permute-start.12) | collective-permute-done | bytes 262176 | tf_op jit(solution)/shard_map/ta3/ppermute | solution.py:259
  53.4 5.0 %collective-permute-done.10.mine_b = bf16[64,2048]{1,0:T(8,128)(2,1)S(1)} collective-permute-done((bf16[64,2048]{1,0:T(8,128)(2,1)S(1)}, bf16[64,2048]{1,0:T(8,128)(2,1)S(1)}, u32[]{:S(2)}, u32[]{:S(2)}) %collective-permute-start.10) | collective-permute-done | bytes 262176 | tf_op jit(solution)/shard_map/tb3/ppermute | solution.py:259
  59.5 3.4 %forward_2.1 = (bf16[256,704]{1,0:T(8,128)(2,1)S(1)}, f32[256,704]{1,0:T(8,128)S(1)}, f32[256,704]{1,0:T(8,128)S(1)}, bf16[128,2048]{1,0:T(8,128)(2,1)S(1)}, bf1...) custom-call(s32[8]{0:T(128)S(1)} %stack.62.offs, ...), custom_call_target="tpu_custom_call" | custom-call | flops 1 | bytes 1 | tf_op jit(solution)/shard_map/forward_2/pallas_call | solution.py:129
  64.5 4.7 %collective-permute-done.13.refs_1_ = bf16[128,1024]{1,0:T(8,128)(2,1)S(1)} collective-permute-done((bf16[128,1024]{1,0:T(8,128)(2,1)S(1)}, bf16[128,1024]{1,0:T(8,128)(2,1)S(1)}, u32[]{:S(2)}, u32[]{:S(2)}) %collective-permute-start.13) | collective-permute-done | bytes 262176 | tf_op jit(solution)/shard_map/k1/ppermute | solution.py:259
  70.7 3.4 %forward_3.1 = (bf16[256,704]{1,0:T(8,128)(2,1)S(1)}, f32[256,704]{1,0:T(8,128)S(1)}, f32[256,704]{1,0:T(8,128)S(1)}, bf16[128,2048]{1,0:T(8,128)(2,1)S(1)}, bf1...) custom-call(s32[8]{0:T(128)S(1)} %stack.62.offs, ...), custom_call_target="tpu_custom_call" | custom-call | flops 1 | bytes 1 | tf_op jit(solution)/shard_map/forward_3/pallas_call | solution.py:129
  76.6 4.5 %early.1 = (bf16[704,512]{1,0:T(8,128)(2,1)S(1)}, bf16[704,512]{1,0:T(8,128)(2,1)S(1)}, f32[1024,704]{1,0:T(8,128)S(1)}) custom-call(f32[8,128]{1,0:T(8,128)S(1)} %select_reduce_fusion.weights, bf16[128,1024]{1,0:T(8,128)(2,1)} %get-tuple-element.339.refs_0_, bf16[128,1024]{1,0:T(8,128)(2,1)} %collective-permute-done.refs_1_, ...), custom_call_target="tpu_custom_call" | custom-call | flops 1 | bytes 1 | tf_op jit(solution)/shard_map/early/pallas_call | solution.py:129
  81.5 3.4 %collective-permute-done.19.refs_2_ = bf16[128,1024]{1,0:T(8,128)(2,1)S(1)} collective-permute-done((bf16[128,1024]{1,0:T(8,128)(2,1)S(1)}, bf16[128,1024]{1,0:T(8,128)(2,1)S(1)}, u32[]{:S(2)}, u32[]{:S(2)}) %collective-permute-start.19) | collective-permute-done | bytes 262176 | tf_op jit(solution)/shard_map/k2/ppermute | solution.py:259
  85.4 6.0 %collective-permute-done.27 = bf16[64,2048]{1,0:T(8,128)(2,1)S(1)} collective-permute-done((bf16[64,2048]{1,0:T(8,128)(2,1)S(1)}, bf16[64,2048]{1,0:T(8,128)(2,1)S(1)}, u32[]{:S(2)}, u32[]{:S(2)}) %collective-permute-start.27) | collective-permute-done | bytes 262176 | tf_op jit(solution)/shard_map/ma2/ppermute | solution.py:259
  102.0 6.8 %collective-permute-done.35.refs_1_ = bf16[704,512]{1,0:T(8,128)(2,1)S(1)} collective-permute-done((bf16[704,512]{1,0:T(8,128)(2,1)S(1)}, bf16[704,512]{1,0:T(8,128)(2,1)S(1)}, u32[]{:S(2)}, u32[]{:S(2)}) %collective-permute-start.35) | collective-permute-done | bytes 720928 | tf_op jit(solution)/shard_map/d1/ppermute | solution.py:267
  111.7 3.5 %rows_near.1 = (bf16[256,2048]{1,0:T(8,128)(2,1)S(1)}, bf16[256,2048]{1,0:T(8,128)(2,1)S(1)}) custom-call(bf16[1024,704]{1,0:T(8,128)(2,1)S(1)} %get-tuple-element.428.left.d_gate, bf16[1024,704]{1,0:T(8,128)(2,1)S(1)} %get-tuple-element.451.d_up.left, bf16[704,2048]{1,0:T(8,128)(2,1)S(1)} %bitcast.56, bf16[704,2048]{1,0:T(8,128)(2,1)S(1)} %bitcast.62), custom_call_target="tpu_custom_call" | custom-call | flops 1 | bytes 1 | tf_op jit(solution)/shard_map/rows_near/pallas_call | solution.py:129
  122.6 3.4 %rows_far.1 = (bf16[256,2048]{1,0:T(8,128)(2,1)S(1)}, bf16[256,2048]{1,0:T(8,128)(2,1)S(1)}) custom-call(bf16[1024,704]{1,0:T(8,128)(2,1)S(1)} %get-tuple-element.428.left.d_gate, bf16[1024,704]{1,0:T(8,128)(2,1)S(1)} %get-tuple-element.451.d_up.left, bf16[704,2048]{1,0:T(8,128)(2,1)S(1)} %bitcast.57, bf16[704,2048]{1,0:T(8,128)(2,1)S(1)} %bitcast.63), custom_call_target="tpu_custom_call" | custom-call | flops 1 | bytes 1 | tf_op jit(solution)/shard_map/rows_far/pallas_call | solution.py:129
  129.9 3.1 %collective-permute-done.38 = bf16[64,2048]{1,0:T(8,128)(2,1)S(1)} collective-permute-done((bf16[64,2048]{1,0:T(8,128)(2,1)S(1)}, bf16[64,2048]{1,0:T(8,128)(2,1)S(1)}, u32[]{:S(2)}, u32[]{:S(2)}) %collective-permute-start.38) | collective-permute-done | bytes 262176 | tf_op jit(solution)/shard_map/ga1/ppermute | solution.py:259
  133.9 4.3 %collective-permute-done.46.refs_5_ = bf16[704,512]{1,0:T(8,128)(2,1)S(1)} collective-permute-done((bf16[704,512]{1,0:T(8,128)(2,1)S(1)}, bf16[704,512]{1,0:T(8,128)(2,1)S(1)}, u32[]{:S(2)}, u32[]{:S(2)}) %collective-permute-start.46) | collective-permute-done | bytes 720928 | tf_op jit(solution)/shard_map/g1/ppermute | solution.py:267
  145.2 3.6 %collective-permute-done.41 = bf16[64,2048]{1,0:T(8,128)(2,1)S(1)} collective-permute-done((bf16[64,2048]{1,0:T(8,128)(2,1)S(1)}, bf16[64,2048]{1,0:T(8,128)(2,1)S(1)}, u32[]{:S(2)}, u32[]{:S(2)}) %collective-permute-start.41) | collective-permute-done | bytes 262176 | tf_op jit(solution)/shard_map/ga2/ppermute | solution.py:259
  150.8 3.2 %collective-permute-done.40 = bf16[64,2048]{1,0:T(8,128)(2,1)S(1)} collective-permute-done((bf16[64,2048]{1,0:T(8,128)(2,1)S(1)}, bf16[64,2048]{1,0:T(8,128)(2,1)S(1)}, u32[]{:S(2)}, u32[]{:S(2)}) %collective-permute-start.40) | collective-permute-done | bytes 262176 | tf_op jit(solution)/shard_map/gb1/ppermute | solution.py:259
  155.3 7.0 %collective-permute-done.49.refs_1_ = bf16[704,512]{1,0:T(8,128)(2,1)S(1)} collective-permute-done((bf16[704,512]{1,0:T(8,128)(2,1)S(1)}, bf16[704,512]{1,0:T(8,128)(2,1)S(1)}, u32[]{:S(2)}, u32[]{:S(2)}) %collective-permute-start.49) | collective-permute-done | bytes 720928 | tf_op jit(solution)/shard_map/u1/ppermute | solution.py:267
  166.2 12.1 %collective-permute-done.53 = bf16[2,704,256]{2,1,0:T(8,128)(2,1)S(1)} collective-permute-done((bf16[2,704,256]{2,1,0:T(8,128)(2,1)S(1)}, bf16[2,704,256]{2,1,0:T(8,128)(2,1)S(1)}, u32[]{:S(2)}, u32[]{:S(2)}) %collective-permute-start.53) | collective-permute-done | bytes 720928 | tf_op jit(solution)/shard_map/dg2/ppermute | solution.py:267
  186.6 2.8 %collective-permute-done.50 = bf16[64,2048]{1,0:T(8,128)(2,1)S(1)} collective-permute-done((bf16[64,2048]{1,0:T(8,128)(2,1)S(1)}, bf16[64,2048]{1,0:T(8,128)(2,1)S(1)}, u32[]{:S(2)}, u32[]{:S(2)}) %collective-permute-start.50) | collective-permute-done | bytes 262176 | tf_op jit(solution)/shard_map/ga3/ppermute | solution.py:259
  (157 shorter events, 81.4 us)
Async XLA Ops:
  1.8 23.5 %collective-permute-start.6 = (bf16[64,2048]{1,0:T(8,128)(2,1)S(1)}, bf16[64,2048]{1,0:T(8,128)(2,1)}, u32[]{:S(2)}, u32[]{:S(2)}) collective-permute-start(bf16[64,2048]{1,0:T(8,128)(2,1)S(1)} %get-tuple-element.265.mine_a), channel_id=1, source_target_pairs={{0,1},{1,0},{2,3},{3,2},{4,5},{5,4},{6,7},{7,6},{8,9},{9,8},{10,11... | collective-permute-start | bytes 786440 | tf_op jit(solution)/shard_map/ap0/ppermute | solution.py:263
  2.3 20.0 %collective-permute-start.2 = (bf16[64,2048]{1,0:T(8,128)(2,1)S(1)}, bf16[64,2048]{1,0:T(8,128)(2,1)}, u32[]{:S(2)}, u32[]{:S(2)}) collective-permute-start(bf16[64,2048]{1,0:T(8,128)(2,1)S(1)} %get-tuple-element.265.mine_a), channel_id=1, source_target_pairs={{0,2},{1,3},{2,6},{3,7},{6,4},{7,5},{4,0},{5,1},{8,10},{9,11},{10,... | collective-permute-start | bytes 786440 | tf_op jit(solution)/shard_map/ta1/ppermute | solution.py:259
  4.9 20.9 %collective-permute-start.7 = (bf16[64,2048]{1,0:T(8,128)(2,1)S(1)}, bf16[64,2048]{1,0:T(8,128)(2,1)}, u32[]{:S(2)}, u32[]{:S(2)}) collective-permute-start(bf16[64,2048]{1,0:T(8,128)(2,1)S(1)} %get-tuple-element.264.mine_b), channel_id=1, source_target_pairs={{0,1},{1,0},{2,3},{3,2},{4,5},{5,4},{6,7},{7,6},{8,9},{9,8},{10,11... | collective-permute-start | bytes 786440 | tf_op jit(solution)/shard_map/bp0/ppermute | solution.py:263
  5.1 19.6 %collective-permute-start.1 = (bf16[64,2048]{1,0:T(8,128)(2,1)S(1)}, bf16[64,2048]{1,0:T(8,128)(2,1)}, u32[]{:S(2)}, u32[]{:S(2)}) collective-permute-start(bf16[64,2048]{1,0:T(8,128)(2,1)S(1)} %get-tuple-element.264.mine_b), channel_id=1, source_target_pairs={{0,2},{1,3},{2,6},{3,7},{6,4},{7,5},{4,0},{5,1},{8,10},{9,11},{10,... | collective-permute-start | bytes 786440 | tf_op jit(solution)/shard_map/tb1/ppermute | solution.py:259
  24.7 13.5 %collective-permute-start.4 = (bf16[64,2048]{1,0:T(8,128)(2,1)}, bf16[64,2048]{1,0:T(8,128)(2,1)S(1)}, u32[]{:S(2)}, u32[]{:S(2)}) collective-permute-start(bf16[64,2048]{1,0:T(8,128)(2,1)} %collective-permute-done.1.mine_b), channel_id=1, source_target_pairs={{0,2},{1,3},{2,6},{3,7},{6,4},{7,5},{4,0},{5,1},{8,10},{9,11},{10,... | collective-permute-start | bytes 786440 | tf_op jit(solution)/shard_map/tb2/ppermute | solution.py:259
  25.8 17.0 %collective-permute-start.3 = (bf16[128,1024]{1,0:T(8,128)(2,1)}, bf16[128,1024]{1,0:T(8,128)(2,1)S(1)}, u32[]{:S(2)}, u32[]{:S(2)}) collective-permute-start(bf16[128,1024]{1,0:T(8,128)(2,1)} %collective-permute-done.refs_1_), channel_id=1, source_target_pairs={{0,2},{1,3},{2,6},{3,7},{6,4},{7,5},{4,0},{5,1},{8,10},{9,11},{10,... | collective-permute-start | bytes 786440 | tf_op jit(solution)/shard_map/s2/ppermute | solution.py:259
  42.8 16.2 %collective-permute-start.11 = (bf16[128,2048]{1,0:T(8,128)(2,1)S(1)}, bf16[128,2048]{1,0:T(8,128)(2,1)S(1)}, u32[]{:S(2)}, u32[]{:S(2)}) collective-permute-start(bf16[128,2048]{1,0:T(8,128)(2,1)S(1)} %get-tuple-element.300), channel_id=1, source_target_pairs={{0,1},{1,0},{2,3},{3,2},{4,5},{5,4},{6,7},{7,6},{8,9},{9,8},{10,11... | collective-permute-start | bytes 1572872 | tf_op jit(solution)/shard_map/o1/ppermute | solution.py:263
  44.5 13.9 %collective-permute-start.10 = (bf16[64,2048]{1,0:T(8,128)(2,1)S(1)}, bf16[64,2048]{1,0:T(8,128)(2,1)S(1)}, u32[]{:S(2)}, u32[]{:S(2)}) collective-permute-start(bf16[64,2048]{1,0:T(8,128)(2,1)S(1)} %collective-permute-done.4.mine_b), channel_id=1, source_target_pairs={{0,2},{1,3},{2,6},{3,7},{6,4},{7,5},{4,0},{5,1},{8,10},{9,11},{10,... | collective-permute-start | bytes 786440 | tf_op jit(solution)/shard_map/tb3/ppermute | solution.py:259
  59.0 15.2 %collective-permute-start.23 = (bf16[128,1024]{1,0:T(8,128)(2,1)}, bf16[128,1024]{1,0:T(8,128)(2,1)S(1)}, u32[]{:S(2)}, u32[]{:S(2)}) collective-permute-start(bf16[128,1024]{1,0:T(8,128)(2,1)} %collective-permute-done.refs_1_), channel_id=1, source_target_pairs={{0,1},{1,0},{2,3},{3,2},{4,5},{5,4},{6,7},{7,6},{8,9},{9,8},{10,11... | collective-permute-start | bytes 786440 | tf_op jit(solution)/shard_map/sp1/ppermute | solution.py:263
  91.4 17.4 %collective-permute-start.35 = (bf16[704,512]{1,0:T(8,128)(2,1)S(1)}, bf16[704,512]{1,0:T(8,128)(2,1)S(1)}, u32[]{:S(2)}, u32[]{:S(2)}) collective-permute-start(bf16[704,512]{1,0:T(8,128)(2,1)S(1)} %get-tuple-element.382), channel_id=1, source_target_pairs={{0,16},{8,24},{16,0},{24,8},{1,17},{9,25},{17,1},{25,9},{2,18},{10... | collective-permute-start | bytes 2162696 | tf_op jit(solution)/shard_map/d1/ppermute | solution.py:267
  92.9 17.1 %collective-permute-start.34 = (bf16[704,512]{1,0:T(8,128)(2,1)S(1)}, bf16[704,512]{1,0:T(8,128)(2,1)S(1)}, u32[]{:S(2)}, u32[]{:S(2)}) collective-permute-start(bf16[704,512]{1,0:T(8,128)(2,1)S(1)} %get-tuple-element.380), channel_id=1, source_target_pairs={{0,8},{8,0},{16,24},{24,16},{1,9},{9,1},{17,25},{25,17},{2,10},{10... | collective-permute-start | bytes 2162696 | tf_op jit(solution)/shard_map/d1/ppermute | solution.py:267
  97.3 14.4 %collective-permute-start.36 = (bf16[64,2048]{1,0:T(8,128)(2,1)S(1)}, bf16[64,2048]{1,0:T(8,128)(2,1)S(1)}, u32[]{:S(2)}, u32[]{:S(2)}) collective-permute-start(bf16[64,2048]{1,0:T(8,128)(2,1)S(1)} %add_convert_fusion.12), channel_id=1, source_target_pairs={{0,2},{1,3},{2,6},{3,7},{6,4},{7,5},{4,0},{5,1},{8,10},{9,11},{10,... | collective-permute-start | bytes 786440 | tf_op jit(solution)/shard_map/ma3/ppermute | solution.py:259
  98.2 17.0 %collective-permute-start.29 = (bf16[64,2048]{1,0:T(8,128)(2,1)S(1)}, bf16[64,2048]{1,0:T(8,128)(2,1)S(1)}, u32[]{:S(2)}, u32[]{:S(2)}) collective-permute-start(bf16[64,2048]{1,0:T(8,128)(2,1)S(1)} %get-tuple-element.362), channel_id=1, source_target_pairs={{0,2},{1,3},{2,6},{3,7},{6,4},{7,5},{4,0},{5,1},{8,10},{9,11},{10,... | collective-permute-start | bytes 786440 | tf_op jit(solution)/shard_map/mb1/ppermute | solution.py:259
  118.2 14.9 %collective-permute-start.38 = (bf16[64,2048]{1,0:T(8,128)(2,1)S(1)}, bf16[64,2048]{1,0:T(8,128)(2,1)S(1)}, u32[]{:S(2)}, u32[]{:S(2)}) collective-permute-start(bf16[64,2048]{1,0:T(8,128)(2,1)S(1)} %get-tuple-element.412), channel_id=1, source_target_pairs={{0,2},{1,3},{2,6},{3,7},{6,4},{7,5},{4,0},{5,1},{8,10},{9,11},{10,... | collective-permute-start | bytes 786440 | tf_op jit(solution)/shard_map/ga1/ppermute | solution.py:259
  120.6 17.6 %collective-permute-start.46 = (bf16[704,512]{1,0:T(8,128)(2,1)S(1)}, bf16[704,512]{1,0:T(8,128)(2,1)S(1)}, u32[]{:S(2)}, u32[]{:S(2)}) collective-permute-start(bf16[704,512]{1,0:T(8,128)(2,1)S(1)} %get-tuple-element.449), channel_id=1, source_target_pairs={{0,16},{8,24},{16,0},{24,8},{1,17},{9,25},{17,1},{25,9},{2,18},{10... | collective-permute-start | bytes 2162696 | tf_op jit(solution)/shard_map/g1/ppermute | solution.py:267
  121.1 17.7 %collective-permute-start.45 = (bf16[704,512]{1,0:T(8,128)(2,1)S(1)}, bf16[704,512]{1,0:T(8,128)(2,1)S(1)}, u32[]{:S(2)}, u32[]{:S(2)}) collective-permute-start(bf16[704,512]{1,0:T(8,128)(2,1)S(1)} %get-tuple-element.447), channel_id=1, source_target_pairs={{0,8},{8,0},{16,24},{24,16},{1,9},{9,1},{17,25},{25,17},{2,10},{10... | collective-permute-start | bytes 2162696 | tf_op jit(solution)/shard_map/g1/ppermute | solution.py:267
  133.0 17.3 %collective-permute-start.42 = (bf16[256,2048]{1,0:T(8,128)(2,1)S(1)}, bf16[256,2048]{1,0:T(8,128)(2,1)S(1)}, u32[]{:S(2)}, u32[]{:S(2)}) collective-permute-start(bf16[256,2048]{1,0:T(8,128)(2,1)S(1)} %get-tuple-element.440), channel_id=1, source_target_pairs={{0,1},{1,0},{2,3},{3,2},{4,5},{5,4},{6,7},{7,6},{8,9},{9,8},{10,11... | collective-permute-start | bytes 3145736 | tf_op jit(solution)/shard_map/fo/ppermute | solution.py:263
  138.8 15.2 %collective-permute-start.40 = (bf16[64,2048]{1,0:T(8,128)(2,1)S(1)}, bf16[64,2048]{1,0:T(8,128)(2,1)S(1)}, u32[]{:S(2)}, u32[]{:S(2)}) collective-permute-start(bf16[64,2048]{1,0:T(8,128)(2,1)S(1)} %get-tuple-element.436), channel_id=1, source_target_pairs={{0,2},{1,3},{2,6},{3,7},{6,4},{7,5},{4,0},{5,1},{8,10},{9,11},{10,... | collective-permute-start | bytes 786440 | tf_op jit(solution)/shard_map/gb1/ppermute | solution.py:259
  143.2 19.1 %collective-permute-start.49 = (bf16[704,512]{1,0:T(8,128)(2,1)S(1)}, bf16[704,512]{1,0:T(8,128)(2,1)S(1)}, u32[]{:S(2)}, u32[]{:S(2)}) collective-permute-start(bf16[704,512]{1,0:T(8,128)(2,1)S(1)} %get-tuple-element.479), channel_id=1, source_target_pairs={{0,16},{8,24},{16,0},{24,8},{1,17},{9,25},{17,1},{25,9},{2,18},{10... | collective-permute-start | bytes 2162696 | tf_op jit(solution)/shard_map/u1/ppermute | solution.py:267
  143.7 19.1 %collective-permute-start.48 = (bf16[704,512]{1,0:T(8,128)(2,1)S(1)}, bf16[704,512]{1,0:T(8,128)(2,1)S(1)}, u32[]{:S(2)}, u32[]{:S(2)}) collective-permute-start(bf16[704,512]{1,0:T(8,128)(2,1)S(1)} %get-tuple-element.477), channel_id=1, source_target_pairs={{0,8},{8,0},{16,24},{24,16},{1,9},{9,1},{17,25},{25,17},{2,10},{10... | collective-permute-start | bytes 2162696 | tf_op jit(solution)/shard_map/u1/ppermute | solution.py:267
  148.8 29.4 %collective-permute-start.53 = (bf16[2,704,256]{2,1,0:T(8,128)(2,1)S(1)}, bf16[2,704,256]{2,1,0:T(8,128)(2,1)S(1)}, u32[]{:S(2)}, u32[]{:S(2)}) collective-permute-start(bf16[2,704,256]{2,1,0:T(8,128)(2,1)S(1)} %get-tuple-element.501), channel_id=1, source_target_pairs={{0,8},{8,0},{16,24},{24,16},{1,9},{9,1},{17,25},{25,17},{2,10},{10... | collective-permute-start | bytes 2162696 | tf_op jit(solution)/shard_map/dg2/ppermute | solution.py:267
  150.3 27.9 %collective-permute-start.52 = (bf16[2,704,256]{2,1,0:T(8,128)(2,1)S(1)}, bf16[2,704,256]{2,1,0:T(8,128)(2,1)S(1)}, u32[]{:S(2)}, u32[]{:S(2)}) collective-permute-start(bf16[2,704,256]{2,1,0:T(8,128)(2,1)S(1)} %get-tuple-element.499), channel_id=1, source_target_pairs={{0,16},{8,24},{16,0},{24,8},{1,17},{9,25},{17,1},{25,9},{2,18},{10... | collective-permute-start | bytes 2162696 | tf_op jit(solution)/shard_map/dg2/ppermute | solution.py:267
  163.1 20.9 %collective-permute-start.55 = (bf16[1,704,256]{2,1,0:T(8,128)(2,1)S(1)}, bf16[1,704,256]{2,1,0:T(8,128)(2,1)S(1)}, u32[]{:S(2)}, u32[]{:S(2)}) collective-permute-start(bf16[1,704,256]{2,1,0:T(8,128)(2,1)S(1)} %get-tuple-element.510), channel_id=1, source_target_pairs={{0,8},{8,0},{16,24},{24,16},{1,9},{9,1},{17,25},{25,17},{2,10},{10... | collective-permute-start | bytes 1081352 | tf_op jit(solution)/shard_map/u2/ppermute | solution.py:267
  164.6 19.4 %collective-permute-start.54 = (bf16[1,704,256]{2,1,0:T(8,128)(2,1)S(1)}, bf16[1,704,256]{2,1,0:T(8,128)(2,1)S(1)}, u32[]{:S(2)}, u32[]{:S(2)}) collective-permute-start(bf16[1,704,256]{2,1,0:T(8,128)(2,1)S(1)} %get-tuple-element.507), channel_id=1, source_target_pairs={{0,16},{8,24},{16,0},{24,8},{1,17},{9,25},{17,1},{25,9},{2,18},{10... | collective-permute-start | bytes 1081352 | tf_op jit(solution)/shard_map/u2/ppermute | solution.py:267
  (45 other events, 417.7 us)

commit v3 on v0

--- a/solution.py
+++ b/solution.py
@@ -3,6 +3,8 @@
 import jax
 import jax.numpy as jnp
 from jax import lax
+from jax.experimental import pallas as pl
+from jax.experimental.pallas import tpu as pltpu
 from jax.sharding import PartitionSpec as P
 
 
@@ -36,7 +38,7 @@
     return (d_rows, d_gate, d_up)
 
 
-def shards(tokens, cotangent, expert_ids, gate_fixed, w_gate, w_up, w_down):
+def slot_shards(tokens, cotangent, expert_ids, gate_fixed, w_gate, w_up, w_down):
     n_expert = lax.axis_size("expert")
     tok_rows = tokens.shape[0]
     width = tokens.shape[1]
@@ -101,6 +103,435 @@
     return (mixed, token_grad, grad_gate[None], grad_up[None], grad_down[None])
 
 
+BF16, F32 = jnp.bfloat16, jnp.float32
+VMEM = pl.BlockSpec(memory_space=pltpu.VMEM)
+SMEM = pl.BlockSpec(memory_space=pltpu.SMEM)
+PIECES = ((1, 0), (3, 0), (2, 1), (3, 1), (0, 0), (2, 0), (0, 1), (1, 1))
+
+
+def tie(*values):
+    return lax.optimization_barrier(values)
+
+
+def nt(left, right):
+    return lax.dot_general(left, right, (((1,), (1,)), ((), ())), preferred_element_type=F32)
+
+
+def nn(left, right):
+    return lax.dot_general(left, right, (((1,), (0,)), ((), ())), preferred_element_type=F32)
+
+
+def tn(left, right):
+    return lax.dot_general(left, right, (((0,), (0,)), ((), ())), preferred_element_type=F32)
+
+
+def call(name, kernel, outs, ins, scratch=(), smem=0, flops=1):
+    return list(pl.pallas_call(
+        kernel,
+        name=name,
+        out_shape=[jax.ShapeDtypeStruct(shape, dtype) for shape, dtype in outs],
+        in_specs=[SMEM] * smem + [VMEM] * (len(ins) - smem),
+        out_specs=[VMEM] * len(outs),
+        scratch_shapes=[pltpu.VMEM(shape, dtype) for shape, dtype in scratch],
+        compiler_params=pltpu.CompilerParams(vmem_limit_bytes=16 * 1024 * 1024),
+        cost_estimate=pl.CostEstimate(flops=flops, bytes_accessed=1, transcendentals=0),
+    )(*ins))
+
+
+def per_row(weights, row, width):
+    count = weights.shape[1]
+    square = jnp.broadcast_to(weights[row : row + 1, :], (count, count)).T
+    return jnp.concatenate([square] * (width // count), axis=1)
+
+
+def forward_kernel(offs, *refs):
+    parts, (gate, up, hid, fac_g, fac_u, rows_s, rows_k, rows) = refs[:-8], refs[-8:]
+    size = rows.shape[1] // 8
+    stack(parts, rows)
+    gate_pre = nt(rows[...], gate[...])
+    up_pre = nt(rows[...], up[...])
+    sigma = jax.nn.sigmoid(gate_pre)
+    activ = gate_pre * sigma
+    hid[...] = (activ * up_pre).astype(BF16)
+    fac_g[...] = up_pre * (sigma * (1.0 + gate_pre * (1.0 - sigma)))
+    fac_u[...] = activ
+    for at in range(8):
+        here = pl.ds(pl.multiple_of(offs[at], size), size)
+        (rows_s if at < 4 else rows_k)[:, pl.ds(at % 4 * size, size)] = rows[:, here]
+
+
+def stack(parts, whole):
+    at = 0
+    for part in parts:
+        whole[at : at + part.shape[0], :] = part[...]
+        at += part.shape[0]
+
+
+def backward_kernel(slot, offs, weights, hid, fac_g, fac_u, down, mine, *refs):
+    others, (out_m, out_o, d_gate, d_up, dy_s, dy_k, dy) = refs[:-7], refs[-7:]
+    n, width = mine.shape
+    size = width // 8
+    stack((mine, *others), dy)
+    out = nn(hid[...], down[...])
+    for at, (row, held) in enumerate(((slot, out_m), (slot + 4, out_o))):
+        part = slice(at * n, (at + 1) * n)
+        weight = per_row(weights[...], row, width)
+        dy[part, :] = (dy[part, :].astype(F32) * weight).astype(BF16)
+        held[...] = (out[part] * weight).astype(BF16)
+    d_hid = nt(dy[...], down[...])
+    d_gate[...] = (d_hid * fac_g[...]).astype(BF16)
+    d_up[...] = (d_hid * fac_u[...]).astype(BF16)
+    for at in range(8):
+        here = pl.ds(pl.multiple_of(offs[at], size), size)
+        (dy_s if at < 4 else dy_k)[:, pl.ds(at % 4 * size, size)] = dy[:, here]
+
+
+def split_kernel(offs, whole, part_s, part_k):
+    size = whole.shape[1] // 8
+    for at in range(8):
+        here = pl.ds(pl.multiple_of(offs[at], size), size)
+        (part_s if at < 4 else part_k)[:, pl.ds(at % 4 * size, size)] = whole[:, here]
+
+
+def weigh(slot, weights, parts, dy):
+    stack(parts, dy)
+    n = dy.shape[0] // 2
+    for at, row in enumerate((slot, slot + 4)):
+        part = slice(at * n, (at + 1) * n)
+        dy[part, :] = (dy[part, :].astype(F32) * per_row(weights[...], row, dy.shape[1])).astype(BF16)
+
+
+def early_kernel(weights, *refs):
+    hids, dys, parts, (out_a, out_b, dy, left, right) = refs[:4], refs[4:7], refs[7:-5], refs[-5:]
+    weigh(3, weights, parts, dy)
+    stack(hids, left)
+    stack((*dys, dy), right)
+    half = right.shape[1] // 2
+    out_a[0, :, :] = tn(left[...], right[:, :half]).astype(BF16)
+    out_b[0, :, :] = tn(left[...], right[:, half:]).astype(BF16)
+
+
+def out_kernel(slot, weights, hid, down, out_m, out_o):
+    n, width = out_m.shape
+    out = nn(hid[...], down[...])
+    out_m[...] = (out[:n] * per_row(weights[...], slot, width)).astype(BF16)
+    out_o[...] = (out[n:] * per_row(weights[...], slot + 4, width)).astype(BF16)
+
+
+def sum_kernel(*refs):
+    *parts, out = refs
+    out[...] = sum(part[...].astype(F32) for part in parts).astype(BF16)
+
+
+def last_kernel(offs, weights, fac_g, fac_u, down, dy_s, *refs):
+    parts, (d_gate, d_up, dy_k, dy) = refs[:-4], refs[-4:]
+    size = down.shape[1] // 8
+    weigh(3, weights, parts, dy_k)
+    for at in range(8):
+        here = pl.ds(pl.multiple_of(offs[at], size), size)
+        dy[:, here] = (dy_s if at < 4 else dy_k)[:, pl.ds(at % 4 * size, size)]
+    d_hid = nt(dy[...], down[...])
+    d_gate[...] = (d_hid * fac_g[...]).astype(BF16)
+    d_up[...] = (d_hid * fac_u[...]).astype(BF16)
+
+
+def grads_kernel(groups, *refs):
+    ins, (out_a, out_b, left, right) = refs[:-4], refs[-4:]
+    half = right.shape[1] // 2
+    held = None
+    for at, (first, second) in enumerate(groups):
+        stack(ins[4 * first : 4 * first + 4], left)
+        if second != held:
+            stack(ins[4 * second : 4 * second + 4], right)
+            held = second
+        out_a[at, :, :] = tn(left[...], right[:, :half]).astype(BF16)
+        out_b[at, :, :] = tn(left[...], right[:, half:]).astype(BF16)
+
+
+def cross_kernel(came_a, came_b, down_a, down_b, own_a, own_b, far_a, far_b, near_a, near_b):
+    cut = far_a.shape[2]
+    for came, down, own, far, near in (
+        (came_a, down_a, own_a, far_a, near_a),
+        (came_b, down_b, own_b, far_b, near_b),
+    ):
+        for at in range(3):
+            both = (down[0, :, :] if at == 2 else came[at, :, :]).astype(F32) + own[at, :, :].astype(F32)
+            near[at, :, :] = both[:, :cut]
+            far[at, :, :] = both[:, cut:].astype(BF16)
+
+
+def finish_kernel(near_a, near_b, last_a, last_b, *outs):
+    cut = near_a.shape[2]
+    for at, out in enumerate(outs):
+        out[:, :cut] = near_a[at, :, :] + last_a[at, :, :].astype(F32)
+        out[:, cut:] = near_b[at, :, :] + last_b[at, :, :].astype(F32)
+
+
+def rows_kernel(*refs):
+    d_gate, d_up, gate, up, mine, *others = refs
+    n = mine.shape[0]
+    size = others[0].shape[0]
+    both = nn(d_gate[...], gate[...]) + nn(d_up[...], up[...])
+    mine[...] = both[:n].astype(BF16)
+    for at, other in enumerate(others):
+        other[...] = both[n + at * size : n + (at + 1) * size].astype(BF16)
+
+
+def ring_order(count):
+    return [0] + list(range(1, count, 2)) + [at for at in range(count - 1, 1, -1) if at % 2 == 0]
+
+
+def step(value, n_expert):
+    order = ring_order(n_expert // 2)
+    follow = {at: order[(spot + 1) % len(order)] for spot, at in enumerate(order)}
+    return lax.ppermute(value, "expert", [(2 * at + core, 2 * follow[at] + core) for at in order for core in range(2)])
+
+
+def swap(value, n_expert):
+    return lax.ppermute(value, "expert", [(at, at ^ 1) for at in range(n_expert)])
+
+
+def flip(value, mask):
+    return lax.ppermute(value, "dp", [(at, at ^ mask) for at in range(4)])
+
+
+def add(*values):
+    return sum(value.astype(F32) for value in values)
+
+
+def slot_sources(n_expert):
+    me = lax.axis_index("expert")
+    order = ring_order(n_expert // 2)
+    spot = sum(jnp.where(me // 2 == at, where, 0) for where, at in enumerate(order))
+    rows = []
+    for core in (0, 1):
+        for slot in range(n_expert // 2):
+            back = lax.rem(spot - slot + len(order), len(order))
+            chip = sum(jnp.where(back == where, at, 0) for where, at in enumerate(order))
+            rows.append(2 * chip + lax.rem(me + core, 2))
+    return jnp.stack(rows).astype(jnp.int32)
+
+
+def slot_weights(sources, expert_ids, gate_fixed, n_expert):
+    gate_values = gate_fixed.astype(F32) / 65536.0
+    experts = jnp.arange(n_expert, dtype=jnp.int32)[:, None, None]
+    table = jnp.sum(jnp.where(expert_ids.T[None] == experts, gate_values.T[None], 0.0), axis=1)
+    came = lax.all_to_all(table, "expert", split_axis=0, concat_axis=0, tiled=True)
+    return jnp.sum(jnp.where(sources[:, None, None] == jnp.arange(n_expert)[None, :, None], came[None], 0.0), axis=1)
+
+
+class Order:
+    def __init__(self, start):
+        self.last = start
+
+    def point(self, *values):
+        *values, self.last = lax.optimization_barrier((*values, self.last))
+        return values
+
+    def after(self, value):
+        return lax.optimization_barrier((value, self.last))[0]
+
+
+def dense_shards(tokens, cotangent, expert_ids, gate_fixed, w_gate, w_up, w_down):
+    n_expert = lax.axis_size("expert")
+    n, width = tokens.shape
+    ff = w_gate.shape[2]
+    half, cut = width // 2, width // 8
+
+    def ring(value, name):
+        with jax.named_scope(name):
+            return step(order.after(value), n_expert)
+
+    def twin(value, name):
+        with jax.named_scope(name):
+            return swap(order.after(value), n_expert)
+
+    def flips(pair, masks, name):
+        with jax.named_scope(name):
+            return [flip(order.after(value), mask) for value, mask in zip(pair, masks)]
+
+    def launch(name, kernel, outs, ins, scratch=(), smem=0, flops=1):
+        return call(name, kernel, outs, [*ins[:smem], order.after(ins[smem]), *ins[smem + 1 :]], scratch, smem, flops)
+
+    gate_w, up_w, down_w = w_gate[0].T, w_up[0].T, w_down[0]
+    me = lax.axis_index("dp")
+    offs = jnp.stack([((me ^ rel) * 2 + part) * (width // 8) for rel, part in PIECES]).astype(jnp.int32)
+
+    def forward(slot, *parts):
+        pair = 2 * n
+        return launch(
+            f"forward_{slot}",
+            forward_kernel,
+            [((pair, ff), BF16), ((pair, ff), F32), ((pair, ff), F32), ((pair, half), BF16), ((pair, half), BF16)],
+            [offs, *parts, gate_w, up_w],
+            [((pair, width), BF16)],
+            smem=1,
+        )
+
+    def backward(slot, ahead, mine, *others):
+        pair = 2 * n
+        return launch(
+            f"backward_{slot}",
+            partial(backward_kernel, slot),
+            [((n, width), BF16)] * 2 + [((pair, ff), BF16)] * 2 + [((pair, half), BF16)] * 2,
+            [offs, weights, *ahead[:3], down_w, mine, *others],
+            [((pair, width), BF16)],
+            smem=1,
+        )
+
+    def grads(name, groups, *lists):
+        return launch(
+            name,
+            partial(grads_kernel, groups),
+            [((len(groups), ff, half // 2), BF16)] * 2,
+            [part for parts in lists for part in parts],
+            [((8 * n, ff), BF16), ((8 * n, half), BF16)],
+        )
+
+    def row_grads(name, slot, cuts=1):
+        return launch(
+            name,
+            rows_kernel,
+            [((n, width), BF16)] + [((n // cuts, width), BF16)] * cuts,
+            [d_gates[slot], d_ups[slot], gate_w, up_w],
+        )
+
+    def pick(value, which):
+        return value[which * (n // 2) : (which + 1) * (n // 2)]
+
+    def kept(mine, other, which=None):
+        return add(mine, other) if which is None else add(pick(mine, which), pick(other, which))
+
+    def total(near, last, at):
+        return jnp.concatenate([add(part[at], more[at]) for part, more in zip(near, last)], axis=1)
+
+    def whole(part_a, part_b, mine, other):
+        return jnp.concatenate(
+            [add(part_a, kept(mine, other, 0)), add(part_b, kept(mine, other, 1))], axis=0
+        ).astype(BF16)
+
+    def twins(value, name):
+        return [twin(pick(value, at), f"{name}_{at}") for at in range(2)]
+
+    def early(*parts):
+        return launch(
+            "early",
+            early_kernel,
+            [((1, ff, half // 2), BF16)] * 2 + [((2 * n, half), BF16)],
+            [weights, *hids, *dys_s, *parts],
+            [((8 * n, ff), BF16), ((8 * n, half), BF16)],
+        )
+
+    def outputs(slot, hid):
+        return launch(
+            f"out_{slot}", partial(out_kernel, slot), [((n, width), BF16)] * 2, [weights, hid, down_w]
+        )
+
+    def backward_last(dy_s, *parts):
+        return launch(
+            "backward_3",
+            last_kernel,
+            [((2 * n, ff), BF16)] * 2 + [((2 * n, half), BF16)],
+            [offs, weights, *f3[1:3], down_w, dy_s, *parts],
+            [((2 * n, width), BF16)],
+            smem=1,
+        )
+
+    def total_of(name, *parts):
+        return launch(name, sum_kernel, [(parts[0].shape, BF16)], parts)[0]
+
+    order = Order(jnp.zeros((8, 128), F32))
+    sources = slot_sources(n_expert)
+    t0, c0 = tokens, cotangent
+    t1, c1 = ring(t0, "t1"), ring(c0, "c1")
+    p0, q0 = twin(t0, "p0"), twin(c0, "q0")
+    weights = slot_weights(sources, expert_ids, gate_fixed, n_expert)
+    t1, weights = order.point(t1, weights)
+    t2, p1 = ring(t1, "t2"), twin(t1, "p1")
+    c1, p0 = order.point(c1, p0)
+    c2, q1 = ring(c1, "c2"), twin(c1, "q1")
+    f0 = forward(0, t0, p0)
+    f1 = forward(1, t1, p1)
+    t2, f0[0], f1[0] = order.point(t2, f0[0], f1[0])
+    t3, p2 = ring(t2, "t3"), twin(t2, "p2")
+    b0 = backward(0, f0, c0, q0)
+    b1 = backward(1, f1, c1, q1)
+    o1 = twin(b1[1], "o1")
+    c2, b0[0], b1[0] = order.point(c2, b0[0], b1[0])
+    c2s, c2k = launch("split", split_kernel, [((n, half), BF16)] * 2, [offs, c2], smem=1)
+    c3s, c3k = ring(c2s, "c3s"), ring(c2k, "c3k")
+    q2 = twins(c2, "q2")
+    f2 = forward(2, t2, p2)
+    b2 = backward(2, f2, c2, *q2)
+    o2 = twin(b2[1], "o2")
+    t3, o1, f2[0], b2[0] = order.point(t3, o1, f2[0], b2[0])
+    p3 = twins(t3, "p3")
+    c3s, o2 = order.point(c3s, o2)
+    q3s = twins(c3s, "q3s")
+    f3 = forward(3, t3, *p3)
+    hids, facs_g, facs_u, rows_s, rows_k = ([f[at] for f in (f0, f1, f2, f3)] for at in range(5))
+    dys_s = [b[4] for b in (b0, b1, b2)]
+    *sent, dy3 = early(c3s, *q3s)
+    dy3, *sent = order.point(dy3, *sent)
+    down_came = flips(sent, (1, 2), "d1")
+    m = ring(total_of("add_m1", b1[0], o1), "m1")
+    out3 = outputs(3, f3[0])
+    (c3k,) = order.point(c3k)
+    q3k = twin(c3k, "q3k")
+    b3 = backward_last(dy3, c3k, q3k)
+    b3 = [*out3, *b3[:2], dy3, b3[2]]
+    outs_m, outs_o, d_gates, d_ups, dys_s, dys_k = ([b[at] for b in (b0, b1, b2, b3)] for at in range(6))
+    sent = grads("both_s", ((0, 2), (1, 2)), d_gates, d_ups, rows_s)
+    d_gates[1], *sent = order.point(d_gates[1], *sent)
+    m1, r1 = row_grads("rows_1", 1)
+    m, d_gates[2], r1 = order.point(m, d_gates[2], r1)
+    m = ring(total_of("add_m2", m, outs_m[2], o2), "m2")
+    r1, o3 = twin(r1, "r1"), twin(outs_o[3], "o3")
+    m2, r2 = row_grads("rows_2", 2)
+    m3, r3 = row_grads("rows_3", 3)
+    m0, r0 = row_grads("rows_0", 0)
+    r1, o3, r2, r3, r0, d_gates[0], *down_came = order.point(r1, o3, r2, r3, r0, d_gates[0], *down_came)
+    both_came = flips(sent, (1, 2), "gu1")
+    g = ring(total_of("add_g1", m1, r1), "ga1")
+    own = grads("kept_k", ((0, 2), (1, 2), (3, 4)), d_gates, d_ups, rows_k, hids, dys_k)
+    o0 = twin(outs_o[0], "o0")
+    m, o0, *own = order.point(m, o0, *own)
+    m = ring(total_of("add_m3", m, outs_m[3], o3), "m3")
+    r2 = twin(r2, "r2")
+    g, r2 = order.point(g, r2)
+    g = ring(total_of("add_g2", g, m2, r2), "ga2")
+    r3 = twin(r3, "r3")
+    both_came = order.point(*both_came)
+    *far, near_a, near_b = launch(
+        "cross",
+        cross_kernel,
+        [((3, ff, cut), BF16)] * 2 + [((3, ff, cut), F32)] * 2,
+        [*both_came, *down_came, *own],
+    )
+    far = order.point(*far)
+    last = flips(far, (2, 1), "last")
+    g, r3, m = order.point(g, r3, m)
+    g = ring(add(g, kept(m3, r3)).astype(BF16), "ga3")
+    r0 = twin(r0, "r0")
+    mixed = total_of("add_m0", m, outs_m[0], o0)
+    mixed, r0, g = order.point(mixed, r0, g)
+    token_grad = add(g, kept(m0, r0)).astype(BF16)
+    token_grad, *last = order.point(token_grad, *last)
+    grad_gate, grad_up, grad_down = launch(
+        "finish", finish_kernel, [((ff, 2 * cut), F32)] * 3, [near_a, near_b, *last]
+    )
+    return (mixed, token_grad, grad_gate.T[None], grad_up.T[None], grad_down[None])
+
+
+def shards(tokens, cotangent, expert_ids, gate_fixed, w_gate, w_up, w_down):
+    n_expert = lax.axis_size("expert")
+    rows, width = tokens.shape
+    capacity = 4 * rows * expert_ids.shape[1] // (3 * n_expert)
+    dense = capacity >= rows and n_expert == 8 and lax.axis_size("dp") == 4 and rows == 128 and width % 2048 == 0
+    run = dense_shards if dense else slot_shards
+    return run(tokens, cotangent, expert_ids, gate_fixed, w_gate, w_up, w_down)
+
+
 def solution(mesh):
     in_specs = (
         P(("dp", "expert"), None),

time: 480 us -> 169 us (0.35)
  waiting for transfers between devices: 293 us -> 83.3 us
  matrix products: 60.4 us -> 0 us
  local copies, waits for them, and re-layouts: 56.4 us -> 4.96 us
  Pallas kernels: 0 us -> 45.6 us
  other arithmetic: 33.7 us -> 3.46 us
  between operations: 14 us -> 1.15 us
  starting transfers between devices: 21.2 us -> 29.7 us
    all_to_all x4 -> x1, waiting for transfers between devices: 254 us -> 17.4 us  [slot_weights(): lax.all_to_all(table, 'expert', split_axis=0, concat_axis=0, tiled=True)]
    ppermute x0 -> x39, waiting for transfers between devices: none -> 65.9 us  [the longest x13 53.6 us: step(): lax.ppermute(value, 'expert', [(2 * at + core, 2 * follow[at] + core) for...]
    dot_general x9 -> x0, matrix products: 60.4 us -> none  [the longest x3 20.1 us: contract(): lax.dot_general(left, right, (((0,), (0,)), ((), ())), preferred_element_...]
    pallas_call x0 -> x25, Pallas kernels: none -> 45.6 us  [call(): pl.pallas_call(kernel, name=name, out_shape=[jax.ShapeDtypeStruct(shape,...]
    reduce_scatter x3 -> x0, waiting for transfers between devices: 38.1 us -> none  [the longest x1 38.1 us: shards(): lax.psum_scatter(fold_rows(received, d_gate).astype(jnp.bfloat16), 'dp',...]
    gather x5 -> x0, local copies, waits for them, and re-layouts: 38.1 us -> none  [the longest x2 16.3 us: shards(): back_rows[slot_of].astype(jnp.float32).reshape(tok_rows, top_k, width)]
    ppermute x0 -> x39, starting transfers between devices: none -> 26.4 us  [the longest x13 14.6 us: step(): lax.ppermute(value, 'expert', [(2 * at + core, 2 * follow[at] + core) for...]
    all_to_all x4 -> x1, starting transfers between devices: 20.4 us -> 3.31 us  [slot_weights(): lax.all_to_all(table, 'expert', split_axis=0, concat_axis=0, tiled=True)]
  transfers between devices with their start and end apart: 7 -> 40, of which waited for: 5 -> 15; matrix products, arithmetic and copies ran while one was open for 18% -> 2% of each run, Pallas kernels for 0% -> 26%
where the time goes in v3:
time: 169 us; the launch traced here: 168 us
  waiting for transfers between devices  83.3 us (49%)
  Pallas kernels  45.6 us (27%)
  starting transfers between devices  29.7 us (18%)
  local copies, waits for them, and re-layouts  4.96 us (3%)
  other arithmetic  3.46 us (2%)
    ppermute x13, waiting for transfers between devices, step(): lax.ppermute(value, 'expert', [(2 * at + core, 2 * follow[at] + core) for...  53.6 us
    pallas_call x25, Pallas kernels, call(): pl.pallas_call(kernel, name=name, out_shape=[jax.ShapeDtypeStruct(shape,...  45.6 us
    all_to_all x1, waiting for transfers between devices, slot_weights(): lax.all_to_all(table, 'expert', split_axis=0, concat_axis=0, tiled=True)  17.4 us
    ppermute x13, starting transfers between devices, step(): lax.ppermute(value, 'expert', [(2 * at + core, 2 * follow[at] + core) for...  14.6 us
    ppermute x6, waiting for transfers between devices, flip(): return lax.ppermute(value, 'dp', [(at, at ^ mask) for at in range(4)])  11.7 us
    ppermute x6, starting transfers between devices, flip(): return lax.ppermute(value, 'dp', [(at, at ^ mask) for at in range(4)])  8.23 us
    unnamed x14, local copies, waits for them, and re-layouts  4.7 us
    ppermute x20, starting transfers between devices, swap(): lax.ppermute(value, 'expert', [(at, at ^ 1) for at in range(n_expert)])  3.53 us
  transfers between devices with their start and end apart: 40, of which 15 were waited for; matrix products, arithmetic and copies ran while one was open for 2% of the time, Pallas kernels for 26%

profile of v3, /device:TPU:0, one launch (start us, length us, event | category | flops | bytes accessed | tf_op | source)
XLA Modules:
  0.0 168.2 jit_solution(3506725865989290724)
XLA Ops:
  0.6 3.1 %collective-permute-start = (bf16[128,2048]{1,0:T(8,128)(2,1)}, bf16[128,2048]{1,0:T(8,128)(2,1)S(1)}, u32[]{:S(2)}, u32[]{:S(2)}) collective-permute-start(bf16[128,2048]{1,0:T(8,128)(2,1)} %refs_0_), channel_id=1, source_target_pairs={{0,2},{1,3},{2,6},{3,7},{6,4},{7,5},{4,0},{5,1},{8,10},{9,11},{10,... | collective-permute-start | bytes 1572872 | tf_op jit(solution)/shard_map/t1/ppermute | solution.py:287
  3.7 2.6 %collective-permute-start.2 = (bf16[128,2048]{1,0:T(8,128)(2,1)}, bf16[128,2048]{1,0:T(8,128)(2,1)S(1)}, u32[]{:S(2)}, u32[]{:S(2)}) collective-permute-start(bf16[128,2048]{1,0:T(8,128)(2,1)} %mine.1), channel_id=1, source_target_pairs={{0,2},{1,3},{2,6},{3,7},{6,4},{7,5},{4,0},{5,1},{8,10},{9,11},{10,... | collective-permute-start | bytes 1572872 | tf_op jit(solution)/shard_map/c1/ppermute | solution.py:287
  8.3 3.3 %all-to-all-start = ((f32[8,1,128]{2,1,0:T(1,128)}), f32[8,1,128]{2,1,0:T(1,128)S(1)}, u32[]{:S(2)}, u32[]{:S(2)}) async-start(f32[8,1,128]{2,1,0:T(1,128)} %bitcast.19), calls=%async_computation | async-start | bytes 8192 | tf_op jit(solution)/shard_map/all_to_all | solution.py:319
  11.8 17.4 %all-to-all-done = f32[8,1,128]{2,1,0:T(1,128)S(1)} async-done(((f32[8,1,128]{2,1,0:T(1,128)}), f32[8,1,128]{2,1,0:T(1,128)S(1)}, u32[]{:S(2)}, u32[]{:S(2)}) %all-to-all-start) | async-done | bytes 4128 | tf_op jit(solution)/shard_map/all_to_all | solution.py:319
  30.6 2.6 %collective-permute-start.7 = (bf16[128,2048]{1,0:T(8,128)(2,1)S(1)}, bf16[128,2048]{1,0:T(8,128)(2,1)S(1)}, u32[]{:S(2)}, u32[]{:S(2)}) collective-permute-start(bf16[128,2048]{1,0:T(8,128)(2,1)S(1)} %collective-permute-done.2.mine), channel_id=1, source_target_pairs={{0,2},{1,3},{2,6},{3,7},{6,4},{7,5},{4,0},{5,1},{8,10},{9,11},{10,... | collective-permute-start | bytes 1572872 | tf_op jit(solution)/shard_map/c2/ppermute | solution.py:287
  38.0 2.6 %forward_0.1 = (bf16[256,704]{1,0:T(8,128)(2,1)S(1)}, f32[256,704]{1,0:T(8,128)S(1)}, f32[256,704]{1,0:T(8,128)S(1)}, bf16[256,1024]{1,0:T(8,128)(2,1)S(1)}, bf16[256,1024]{1,0:T(8,128)(2,1)S(1)}) custom-call(s32[8]{0:T(128)S(1)} %stack.62.offs, bf16[128,2048]{1,0:T(8,128)(2,1)S(1)} %copy-done.5, bf16[128,2048]{1,0:T(8,128)(2,1)S(1)} %collective-permute-done.3.refs_1_, ...), custom_call_target="tpu_custom_call" | custom-call | flops 1 | bytes 1 | tf_op jit(solution)/shard_map/forward_0/pallas_call | solution.py:129
  40.6 3.2 %forward_1.1 = (bf16[256,704]{1,0:T(8,128)(2,1)S(1)}, f32[256,704]{1,0:T(8,128)S(1)}, f32[256,704]{1,0:T(8,128)S(1)}, bf16[256,1024]{1,0:T(8,128)(2,1)S(1)}, bf16[256,1024]{1,0:T(8,128)(2,1)S(1)}) custom-call(s32[8]{0:T(128)S(1)} %stack.62.offs, bf16[128,2048]{1,0:T(8,128)(2,1)S(1)} %collective-permute-done.refs_0_, ...), custom_call_target="tpu_custom_call" | custom-call | flops 1 | bytes 1 | tf_op jit(solution)/shard_map/forward_1/pallas_call | solution.py:129
  45.2 3.4 %backward_1.1 = (bf16[128,2048]{1,0:T(8,128)(2,1)S(1)}, bf16[128,2048]{1,0:T(8,128)(2,1)S(1)}, bf16[256,704]{1,0:T(8,128)(2,1)S(1)}, bf16[256,704]{1,0:T(8,128)(...) custom-call(s32[8]{0:T(128)S(1)} %stack.62.offs, f32[8,128]{1,0:T(8,128)S(1)} %select_reduce_fusion.weights, ...), custom_call_target="tpu_custom_call" | custom-call | flops 1 | bytes 1 | tf_op jit(solution)/shard_map/backward_1/pallas_call | solution.py:129
  48.7 2.9 %backward_0.1 = (bf16[128,2048]{1,0:T(8,128)(2,1)S(1)}, bf16[128,2048]{1,0:T(8,128)(2,1)S(1)}, bf16[256,704]{1,0:T(8,128)(2,1)S(1)}, bf16[256,704]{1,0:T(8,128)(...) custom-call(s32[8]{0:T(128)S(1)} %stack.62.offs, f32[8,128]{1,0:T(8,128)S(1)} %select_reduce_fusion.weights, ...), custom_call_target="tpu_custom_call" | custom-call | flops 1 | bytes 1 | tf_op jit(solution)/shard_map/backward_0/pallas_call | solution.py:129
  51.6 4.8 %collective-permute-done.7.whole.mine = bf16[128,2048]{1,0:T(8,128)(2,1)S(1)} collective-permute-done((bf16[128,2048]{1,0:T(8,128)(2,1)S(1)}, bf16[128,2048]{1,0:T(8,128)(2,1)S(1)}, u32[]{:S(2)}, u32[]{:S(2)}) %collective-permute-start.7) | collective-permute-done | bytes 524320 | tf_op jit(solution)/shard_map/c2/ppermute | solution.py:287
  57.1 2.6 %forward_2.1 = (bf16[256,704]{1,0:T(8,128)(2,1)S(1)}, f32[256,704]{1,0:T(8,128)S(1)}, f32[256,704]{1,0:T(8,128)S(1)}, bf16[256,1024]{1,0:T(8,128)(2,1)S(1)}, bf16[256,1024]{1,0:T(8,128)(2,1)S(1)}) custom-call(s32[8]{0:T(128)S(1)} %stack.62.offs, bf16[128,2048]{1,0:T(8,128)(2,1)S(1)} %collective-permute-done.1.refs_0_, ...), custom_call_target="tpu_custom_call" | custom-call | flops 1 | bytes 1 | tf_op jit(solution)/shard_map/forward_2/pallas_call | solution.py:129
  59.7 2.9 %backward_2.1 = (bf16[128,2048]{1,0:T(8,128)(2,1)S(1)}, bf16[128,2048]{1,0:T(8,128)(2,1)S(1)}, bf16[256,704]{1,0:T(8,128)(2,1)S(1)}, bf16[256,704]{1,0:T(8,128)(...) custom-call(s32[8]{0:T(128)S(1)} %stack.62.offs, f32[8,128]{1,0:T(8,128)S(1)} %select_reduce_fusion.weights, ...), custom_call_target="tpu_custom_call" | custom-call | flops 1 | bytes 1 | tf_op jit(solution)/shard_map/backward_2/pallas_call | solution.py:129
  63.8 3.4 %collective-permute-done.14.refs_0_ = bf16[128,2048]{1,0:T(8,128)(2,1)S(1)} collective-permute-done((bf16[128,2048]{1,0:T(8,128)(2,1)S(1)}, bf16[128,2048]{1,0:T(8,128)(2,1)S(1)}, u32[]{:S(2)}, u32[]{:S(2)}) %collective-permute-start.14) | collective-permute-done | bytes 524320 | tf_op jit(solution)/shard_map/t3/ppermute | solution.py:287
  67.8 5.2 %collective-permute-done.9.refs_7_ = bf16[128,1024]{1,0:T(8,128)(2,1)S(1)} collective-permute-done((bf16[128,1024]{1,0:T(8,128)(2,1)S(1)}, bf16[128,1024]{1,0:T(8,128)(2,1)S(1)}, u32[]{:S(2)}, u32[]{:S(2)}) %collective-permute-start.9) | collective-permute-done | bytes 262176 | tf_op jit(solution)/shard_map/c3s/ppermute | solution.py:287
  73.6 2.6 %forward_3.1 = (bf16[256,704]{1,0:T(8,128)(2,1)S(1)}, f32[256,704]{1,0:T(8,128)S(1)}, f32[256,704]{1,0:T(8,128)S(1)}, bf16[256,1024]{1,0:T(8,128)(2,1)S(1)}, bf16[256,1024]{1,0:T(8,128)(2,1)S(1)}) custom-call(s32[8]{0:T(128)S(1)} %stack.62.offs, bf16[128,2048]{1,0:T(8,128)(2,1)S(1)} %collective-permute-done.14.refs_0_, ...), custom_call_target="tpu_custom_call" | custom-call | flops 1 | bytes 1 | tf_op jit(solution)/shard_map/forward_3/pallas_call | solution.py:129
  78.1 3.4 %collective-permute-start.21 = (bf16[128,2048]{1,0:T(8,128)(2,1)S(1)}, bf16[128,2048]{1,0:T(8,128)(2,1)S(1)}, u32[]{:S(2)}, u32[]{:S(2)}) collective-permute-start(bf16[128,2048]{1,0:T(8,128)(2,1)S(1)} %add_m1.1), channel_id=1, source_target_pairs={{0,2},{1,3},{2,6},{3,7},{6,4},{7,5},{4,0},{5,1},{8,10},{9,11},{10,... | collective-permute-start | bytes 1572872 | tf_op jit(solution)/shard_map/m1/ppermute | solution.py:287
  89.3 3.2 %both_s.1 = (bf16[2,704,512]{2,1,0:T(8,128)(2,1)S(1)}, bf16[2,704,512]{2,1,0:T(8,128)(2,1)S(1)}) custom-call(bf16[256,704]{1,0:T(8,128)(2,1)S(1)} %get-tuple-element.322.refs_0_, bf16[256,704]{1,0:T(8,128)(2,1)S(1)} %get-tuple-element.285.refs_1_.refs_0_, bf16[256,704]{1,0:T(8,128)(2,1)S(1)} %get-tuple-element.299.refs_2_.refs_0_, ...), custom_call_target="tpu_custom_call" | custom-call | flops 1 | bytes 1 | tf_op jit(solution)/shard_map/both_s/pallas_call | solution.py:129
  106.9 4.8 %kept_k.1 = (bf16[3,704,512]{2,1,0:T(8,128)(2,1)S(1)}, bf16[3,704,512]{2,1,0:T(8,128)(2,1)S(1)}) custom-call(bf16[256,704]{1,0:T(8,128)(2,1)S(1)} %get-tuple-element.322.refs_0_, bf16[256,704]{1,0:T(8,128)(2,1)S(1)} %get-tuple-element.285.refs_1_.refs_0_, bf16[256,704]{1,0:T(8,128)(2,1)S(1)} %get-tuple-element.299.refs_2_.refs_0_, ...), custom_call_target="tpu_custom_call" | custom-call | flops 1 | bytes 1 | tf_op jit(solution)/shard_map/kept_k/pallas_call | solution.py:129
  111.7 4.6 %collective-permute-done.27.refs_0_ = bf16[128,2048]{1,0:T(8,128)(2,1)S(1)} collective-permute-done((bf16[128,2048]{1,0:T(8,128)(2,1)S(1)}, bf16[128,2048]{1,0:T(8,128)(2,1)S(1)}, u32[]{:S(2)}, u32[]{:S(2)}) %collective-permute-start.27) | collective-permute-done | bytes 524320 | tf_op jit(solution)/shard_map/m2/ppermute | solution.py:287
  116.6 11.0 %collective-permute-done.26.refs_0_ = bf16[128,2048]{1,0:T(8,128)(2,1)S(1)} collective-permute-done((bf16[128,2048]{1,0:T(8,128)(2,1)S(1)}, bf16[128,2048]{1,0:T(8,128)(2,1)S(1)}, u32[]{:S(2)}, u32[]{:S(2)}) %collective-permute-start.26) | collective-permute-done | bytes 524320 | tf_op jit(solution)/shard_map/ga1/ppermute | solution.py:287
  127.9 9.4 %collective-permute-done.33.came_a = bf16[2,704,512]{2,1,0:T(8,128)(2,1)S(1)} collective-permute-done((bf16[2,704,512]{2,1,0:T(8,128)(2,1)S(1)}, bf16[2,704,512]{2,1,0:T(8,128)(2,1)S(1)}, u32[]{:S(2)}, u32[]{:S(2)}) %collective-permute-start.33) | collective-permute-done | bytes 1441824 | tf_op jit(solution)/shard_map/gu1/ppermute | solution.py:295
  141.6 7.6 %collective-permute-done.30 = bf16[128,2048]{1,0:T(8,128)(2,1)S(1)} collective-permute-done((bf16[128,2048]{1,0:T(8,128)(2,1)S(1)}, bf16[128,2048]{1,0:T(8,128)(2,1)S(1)}, u32[]{:S(2)}, u32[]{:S(2)}) %collective-permute-start.30) | collective-permute-done | bytes 524320 | tf_op jit(solution)/shard_map/ga2/ppermute | solution.py:287
  151.0 13.7 %collective-permute-done.36 = bf16[128,2048]{1,0:T(8,128)(2,1)S(1)} collective-permute-done((bf16[128,2048]{1,0:T(8,128)(2,1)S(1)}, bf16[128,2048]{1,0:T(8,128)(2,1)S(1)}, u32[]{:S(2)}, u32[]{:S(2)}) %collective-permute-start.36) | collective-permute-done | bytes 524320 | tf_op jit(solution)/shard_map/ga3/ppermute | solution.py:287
  165.8 2.4 %finish.1 = (f32[704,512]{1,0:T(8,128)}, f32[704,512]{1,0:T(8,128)}, f32[704,512]{1,0:T(8,128)}) custom-call(f32[3,704,256]{2,1,0:T(8,128)S(1)} %get-tuple-element.383.near_a, f32[3,704,256]{2,1,0:T(8,128)S(1)} %get-tuple-element.384.near_b, bf16[3,704,256]{2,1,0:T(8,128)(2,1)S(1)} %collective-permute-done.37.last_a, ...), custom_call_target="tpu_custom_call" | custom-call | flops 1 | bytes 1 | tf_op jit(solution)/shard_map/finish/pallas_call | solution.py:129
  (106 shorter events, 44.4 us)
Async XLA Ops:
  0.6 28.8 %collective-permute-start = (bf16[128,2048]{1,0:T(8,128)(2,1)}, bf16[128,2048]{1,0:T(8,128)(2,1)S(1)}, u32[]{:S(2)}, u32[]{:S(2)}) collective-permute-start(bf16[128,2048]{1,0:T(8,128)(2,1)} %refs_0_), channel_id=1, source_target_pairs={{0,2},{1,3},{2,6},{3,7},{6,4},{7,5},{4,0},{5,1},{8,10},{9,11},{10,... | collective-permute-start | bytes 1572872 | tf_op jit(solution)/shard_map/t1/ppermute | solution.py:287
  3.7 26.4 %collective-permute-start.3 = (bf16[128,2048]{1,0:T(8,128)(2,1)}, bf16[128,2048]{1,0:T(8,128)(2,1)S(1)}, u32[]{:S(2)}, u32[]{:S(2)}) collective-permute-start(bf16[128,2048]{1,0:T(8,128)(2,1)} %refs_0_), channel_id=1, source_target_pairs={{0,1},{1,0},{2,3},{3,2},{4,5},{5,4},{6,7},{7,6},{8,9},{9,8},{10,11... | collective-permute-start | bytes 1572872 | tf_op jit(solution)/shard_map/p0/ppermute | solution.py:291
  3.7 26.4 %collective-permute-start.2 = (bf16[128,2048]{1,0:T(8,128)(2,1)}, bf16[128,2048]{1,0:T(8,128)(2,1)S(1)}, u32[]{:S(2)}, u32[]{:S(2)}) collective-permute-start(bf16[128,2048]{1,0:T(8,128)(2,1)} %mine.1), channel_id=1, source_target_pairs={{0,2},{1,3},{2,6},{3,7},{6,4},{7,5},{4,0},{5,1},{8,10},{9,11},{10,... | collective-permute-start | bytes 1572872 | tf_op jit(solution)/shard_map/c1/ppermute | solution.py:287
  8.3 21.0 %all-to-all-start = ((f32[8,1,128]{2,1,0:T(1,128)}), f32[8,1,128]{2,1,0:T(1,128)S(1)}, u32[]{:S(2)}, u32[]{:S(2)}) async-start(f32[8,1,128]{2,1,0:T(1,128)} %bitcast.19), calls=%async_computation | async-start | bytes 8192 | tf_op jit(solution)/shard_map/all_to_all | solution.py:319
  29.5 15.7 %collective-permute-start.1 = (bf16[128,2048]{1,0:T(8,128)(2,1)S(1)}, bf16[128,2048]{1,0:T(8,128)(2,1)S(1)}, u32[]{:S(2)}, u32[]{:S(2)}) collective-permute-start(bf16[128,2048]{1,0:T(8,128)(2,1)S(1)} %collective-permute-done.refs_0_), channel_id=1, source_target_pairs={{0,2},{1,3},{2,6},{3,7},{6,4},{7,5},{4,0},{5,1},{8,10},{9,11},{10,... | collective-permute-start | bytes 1572872 | tf_op jit(solution)/shard_map/t2/ppermute | solution.py:287
  30.1 15.1 %collective-permute-start.5 = (bf16[128,2048]{1,0:T(8,128)(2,1)S(1)}, bf16[128,2048]{1,0:T(8,128)(2,1)}, u32[]{:S(2)}, u32[]{:S(2)}) collective-permute-start(bf16[128,2048]{1,0:T(8,128)(2,1)S(1)} %collective-permute-done.2.mine), channel_id=1, source_target_pairs={{0,1},{1,0},{2,3},{3,2},{4,5},{5,4},{6,7},{7,6},{8,9},{9,8},{10,11... | collective-permute-start | bytes 1572872 | tf_op jit(solution)/shard_map/q1/ppermute | solution.py:291
  30.3 18.4 %collective-permute-start.6 = (bf16[128,2048]{1,0:T(8,128)(2,1)}, bf16[128,2048]{1,0:T(8,128)(2,1)S(1)}, u32[]{:S(2)}, u32[]{:S(2)}) collective-permute-start(bf16[128,2048]{1,0:T(8,128)(2,1)} %mine.1), channel_id=1, source_target_pairs={{0,1},{1,0},{2,3},{3,2},{4,5},{5,4},{6,7},{7,6},{8,9},{9,8},{10,11... | collective-permute-start | bytes 1572872 | tf_op jit(solution)/shard_map/q0/ppermute | solution.py:291
  30.6 25.8 %collective-permute-start.7 = (bf16[128,2048]{1,0:T(8,128)(2,1)S(1)}, bf16[128,2048]{1,0:T(8,128)(2,1)S(1)}, u32[]{:S(2)}, u32[]{:S(2)}) collective-permute-start(bf16[128,2048]{1,0:T(8,128)(2,1)S(1)} %collective-permute-done.2.mine), channel_id=1, source_target_pairs={{0,2},{1,3},{2,6},{3,7},{6,4},{7,5},{4,0},{5,1},{8,10},{9,11},{10,... | collective-permute-start | bytes 1572872 | tf_op jit(solution)/shard_map/c2/ppermute | solution.py:287
  45.2 11.9 %collective-permute-start.10 = (bf16[128,2048]{1,0:T(8,128)(2,1)S(1)}, bf16[128,2048]{1,0:T(8,128)(2,1)S(1)}, u32[]{:S(2)}, u32[]{:S(2)}) collective-permute-start(bf16[128,2048]{1,0:T(8,128)(2,1)S(1)} %collective-permute-done.1.refs_0_), channel_id=1, source_target_pairs={{0,1},{1,0},{2,3},{3,2},{4,5},{5,4},{6,7},{7,6},{8,9},{9,8},{10,11... | collective-permute-start | bytes 1572872 | tf_op jit(solution)/shard_map/p2/ppermute | solution.py:291
  45.2 22.0 %collective-permute-start.14 = (bf16[128,2048]{1,0:T(8,128)(2,1)S(1)}, bf16[128,2048]{1,0:T(8,128)(2,1)S(1)}, u32[]{:S(2)}, u32[]{:S(2)}) collective-permute-start(bf16[128,2048]{1,0:T(8,128)(2,1)S(1)} %collective-permute-done.1.refs_0_), channel_id=1, source_target_pairs={{0,2},{1,3},{2,6},{3,7},{6,4},{7,5},{4,0},{5,1},{8,10},{9,11},{10,... | collective-permute-start | bytes 1572872 | tf_op jit(solution)/shard_map/t3/ppermute | solution.py:287
  78.1 16.3 %collective-permute-start.21 = (bf16[128,2048]{1,0:T(8,128)(2,1)S(1)}, bf16[128,2048]{1,0:T(8,128)(2,1)S(1)}, u32[]{:S(2)}, u32[]{:S(2)}) collective-permute-start(bf16[128,2048]{1,0:T(8,128)(2,1)S(1)} %add_m1.1), channel_id=1, source_target_pairs={{0,2},{1,3},{2,6},{3,7},{6,4},{7,5},{4,0},{5,1},{8,10},{9,11},{10,... | collective-permute-start | bytes 1572872 | tf_op jit(solution)/shard_map/m1/ppermute | solution.py:287
  83.5 18.5 %collective-permute-start.24 = (bf16[1,704,512]{2,1,0:T(8,128)(2,1)S(1)}, bf16[1,704,512]{2,1,0:T(8,128)(2,1)S(1)}, u32[]{:S(2)}, u32[]{:S(2)}) collective-permute-start(bf16[1,704,512]{2,1,0:T(8,128)(2,1)S(1)} %get-tuple-element.306), channel_id=1, source_target_pairs={{0,8},{8,0},{16,24},{24,16},{1,9},{9,1},{17,25},{25,17},{2,10},{10... | collective-permute-start | bytes 2162696 | tf_op jit(solution)/shard_map/d1/ppermute | solution.py:295
  85.0 18.3 %collective-permute-start.25 = (bf16[1,704,512]{2,1,0:T(8,128)(2,1)S(1)}, bf16[1,704,512]{2,1,0:T(8,128)(2,1)S(1)}, u32[]{:S(2)}, u32[]{:S(2)}) collective-permute-start(bf16[1,704,512]{2,1,0:T(8,128)(2,1)S(1)} %get-tuple-element.308), channel_id=1, source_target_pairs={{0,16},{8,24},{16,0},{24,8},{1,17},{9,25},{17,1},{25,9},{2,18},{10... | collective-permute-start | bytes 2162696 | tf_op jit(solution)/shard_map/d1/ppermute | solution.py:295
  100.6 15.7 %collective-permute-start.27 = (bf16[128,2048]{1,0:T(8,128)(2,1)S(1)}, bf16[128,2048]{1,0:T(8,128)(2,1)S(1)}, u32[]{:S(2)}, u32[]{:S(2)}) collective-permute-start(bf16[128,2048]{1,0:T(8,128)(2,1)S(1)} %add_m2.1), channel_id=1, source_target_pairs={{0,2},{1,3},{2,6},{3,7},{6,4},{7,5},{4,0},{5,1},{8,10},{9,11},{10,... | collective-permute-start | bytes 1572872 | tf_op jit(solution)/shard_map/m2/ppermute | solution.py:287
  103.3 13.0 %collective-permute-start.28 = (bf16[128,2048]{1,0:T(8,128)(2,1)S(1)}, bf16[128,2048]{1,0:T(8,128)(2,1)S(1)}, u32[]{:S(2)}, u32[]{:S(2)}) collective-permute-start(bf16[128,2048]{1,0:T(8,128)(2,1)S(1)} %get-tuple-element.320), channel_id=1, source_target_pairs={{0,1},{1,0},{2,3},{3,2},{4,5},{5,4},{6,7},{7,6},{8,9},{9,8},{10,11... | collective-permute-start | bytes 1572872 | tf_op jit(solution)/shard_map/o0/ppermute | solution.py:291
  103.3 34.0 %collective-permute-start.33 = (bf16[2,704,512]{2,1,0:T(8,128)(2,1)S(1)}, bf16[2,704,512]{2,1,0:T(8,128)(2,1)S(1)}, u32[]{:S(2)}, u32[]{:S(2)}) collective-permute-start(bf16[2,704,512]{2,1,0:T(8,128)(2,1)S(1)} %get-tuple-element.349), channel_id=1, source_target_pairs={{0,8},{8,0},{16,24},{24,16},{1,9},{9,1},{17,25},{25,17},{2,10},{10... | collective-permute-start | bytes 4325384 | tf_op jit(solution)/shard_map/gu1/ppermute | solution.py:295
  103.9 33.6 %collective-permute-start.34 = (bf16[2,704,512]{2,1,0:T(8,128)(2,1)S(1)}, bf16[2,704,512]{2,1,0:T(8,128)(2,1)S(1)}, u32[]{:S(2)}, u32[]{:S(2)}) collective-permute-start(bf16[2,704,512]{2,1,0:T(8,128)(2,1)S(1)} %get-tuple-element.351), channel_id=1, source_target_pairs={{0,16},{8,24},{16,0},{24,8},{1,17},{9,25},{17,1},{25,9},{2,18},{10... | collective-permute-start | bytes 4325384 | tf_op jit(solution)/shard_map/gu1/ppermute | solution.py:295
  105.6 22.0 %collective-permute-start.26 = (bf16[128,2048]{1,0:T(8,128)(2,1)S(1)}, bf16[128,2048]{1,0:T(8,128)(2,1)S(1)}, u32[]{:S(2)}, u32[]{:S(2)}) collective-permute-start(bf16[128,2048]{1,0:T(8,128)(2,1)S(1)} %add_g1.1), channel_id=1, source_target_pairs={{0,2},{1,3},{2,6},{3,7},{6,4},{7,5},{4,0},{5,1},{8,10},{9,11},{10,... | collective-permute-start | bytes 1572872 | tf_op jit(solution)/shard_map/ga1/ppermute | solution.py:287
  116.5 25.1 %collective-permute-start.32 = (bf16[128,2048]{1,0:T(8,128)(2,1)S(1)}, bf16[128,2048]{1,0:T(8,128)(2,1)S(1)}, u32[]{:S(2)}, u32[]{:S(2)}) collective-permute-start(bf16[128,2048]{1,0:T(8,128)(2,1)S(1)} %add_m3.1), channel_id=1, source_target_pairs={{0,2},{1,3},{2,6},{3,7},{6,4},{7,5},{4,0},{5,1},{8,10},{9,11},{10,... | collective-permute-start | bytes 1572872 | tf_op jit(solution)/shard_map/m3/ppermute | solution.py:287
  127.7 21.4 %collective-permute-start.30 = (bf16[128,2048]{1,0:T(8,128)(2,1)S(1)}, bf16[128,2048]{1,0:T(8,128)(2,1)S(1)}, u32[]{:S(2)}, u32[]{:S(2)}) collective-permute-start(bf16[128,2048]{1,0:T(8,128)(2,1)S(1)} %add_g2.1), channel_id=1, source_target_pairs={{0,2},{1,3},{2,6},{3,7},{6,4},{7,5},{4,0},{5,1},{8,10},{9,11},{10,... | collective-permute-start | bytes 1572872 | tf_op jit(solution)/shard_map/ga2/ppermute | solution.py:287
  127.8 21.3 %collective-permute-start.31 = (bf16[128,2048]{1,0:T(8,128)(2,1)S(1)}, bf16[128,2048]{1,0:T(8,128)(2,1)S(1)}, u32[]{:S(2)}, u32[]{:S(2)}) collective-permute-start(bf16[128,2048]{1,0:T(8,128)(2,1)S(1)} %get-tuple-element.342), channel_id=1, source_target_pairs={{0,1},{1,0},{2,3},{3,2},{4,5},{5,4},{6,7},{7,6},{8,9},{9,8},{10,11... | collective-permute-start | bytes 1572872 | tf_op jit(solution)/shard_map/r3/ppermute | solution.py:291
  138.5 27.3 %collective-permute-start.37 = (bf16[3,704,256]{2,1,0:T(8,128)(2,1)S(1)}, bf16[3,704,256]{2,1,0:T(8,128)(2,1)S(1)}, u32[]{:S(2)}, u32[]{:S(2)}) collective-permute-start(bf16[3,704,256]{2,1,0:T(8,128)(2,1)S(1)} %get-tuple-element.379), channel_id=1, source_target_pairs={{0,16},{8,24},{16,0},{24,8},{1,17},{9,25},{17,1},{25,9},{2,18},{10... | collective-permute-start | bytes 3244040 | tf_op jit(solution)/shard_map/last/ppermute | solution.py:295
  140.1 25.7 %collective-permute-start.38 = (bf16[3,704,256]{2,1,0:T(8,128)(2,1)S(1)}, bf16[3,704,256]{2,1,0:T(8,128)(2,1)S(1)}, u32[]{:S(2)}, u32[]{:S(2)}) collective-permute-start(bf16[3,704,256]{2,1,0:T(8,128)(2,1)S(1)} %get-tuple-element.381), channel_id=1, source_target_pairs={{0,8},{8,0},{16,24},{24,16},{1,9},{9,1},{17,25},{25,17},{2,10},{10... | collective-permute-start | bytes 3244040 | tf_op jit(solution)/shard_map/last/ppermute | solution.py:295
  149.4 15.3 %collective-permute-start.36 = (bf16[128,2048]{1,0:T(8,128)(2,1)S(1)}, bf16[128,2048]{1,0:T(8,128)(2,1)S(1)}, u32[]{:S(2)}, u32[]{:S(2)}) collective-permute-start(bf16[128,2048]{1,0:T(8,128)(2,1)S(1)} %add_convert_fusion.1), channel_id=1, source_target_pairs={{0,2},{1,3},{2,6},{3,7},{6,4},{7,5},{4,0},{5,1},{8,10},{9,11},{10,... | collective-permute-start | bytes 1572872 | tf_op jit(solution)/shard_map/ga3/ppermute | solution.py:287
  (23 other events, 135.0 us)

commit v4 on v3

--- a/solution.py
+++ b/solution.py
@@ -138,10 +138,22 @@
     )(*ins))
 
 
-def per_row(weights, row, width):
-    count = weights.shape[1]
-    square = jnp.broadcast_to(weights[row : row + 1, :], (count, count)).T
-    return jnp.concatenate([square] * (width // count), axis=1)
+def pack_kernel(ids, gates, cot, out):
+    n, width = cot.shape
+    column = lax.broadcasted_iota(jnp.int32, (n, 128), 1)
+    extra = jnp.zeros((n, 128), jnp.int32)
+    for at in range(ids.shape[1]):
+        expert, gate = ids[:, at : at + 1], gates[:, at : at + 1]
+        extra += jnp.where(column == expert, gate >> 8, 0)
+        extra += jnp.where(column == expert + 8, gate & 255, 0)
+    out[:, :width] = cot[...]
+    out[:, width:] = extra.astype(F32).astype(BF16)
+
+
+def gate_column(expert, extra):
+    column = lax.broadcasted_iota(jnp.int32, extra.shape, 1)
+    scale = jnp.where(column == expert, 256.0, jnp.where(column == expert + 8, 1.0, 0.0))
+    return jnp.sum(extra.astype(F32) * scale, axis=1, keepdims=True) / 65536.0
 
 
 def forward_kernel(offs, *refs):
@@ -167,17 +179,17 @@
         at += part.shape[0]
 
 
-def backward_kernel(slot, offs, weights, hid, fac_g, fac_u, down, mine, *refs):
-    others, (out_m, out_o, d_gate, d_up, dy_s, dy_k, dy) = refs[:-7], refs[-7:]
-    n, width = mine.shape
+def backward_kernel(offs, hid, fac_g, fac_u, down, *refs):
+    parts, (out_m, out_o, d_gate, d_up, dy_s, dy_k, held, dy) = refs[:-8], refs[-8:]
+    n, width = out_m.shape
     size = width // 8
-    stack((mine, *others), dy)
+    stack(parts, held)
     out = nn(hid[...], down[...])
-    for at, (row, held) in enumerate(((slot, out_m), (slot + 4, out_o))):
+    for at, result in enumerate((out_m, out_o)):
         part = slice(at * n, (at + 1) * n)
-        weight = per_row(weights[...], row, width)
-        dy[part, :] = (dy[part, :].astype(F32) * weight).astype(BF16)
-        held[...] = (out[part] * weight).astype(BF16)
+        gate = gate_column(offs[8], held[part, width:])
+        dy[part, :] = (held[part, :width].astype(F32) * gate).astype(BF16)
+        result[...] = (out[part] * gate).astype(BF16)
     d_hid = nt(dy[...], down[...])
     d_gate[...] = (d_hid * fac_g[...]).astype(BF16)
     d_up[...] = (d_hid * fac_u[...]).astype(BF16)
@@ -187,46 +199,52 @@
 
 
 def split_kernel(offs, whole, part_s, part_k):
-    size = whole.shape[1] // 8
+    width = 2 * part_k.shape[1]
+    size = width // 8
     for at in range(8):
         here = pl.ds(pl.multiple_of(offs[at], size), size)
         (part_s if at < 4 else part_k)[:, pl.ds(at % 4 * size, size)] = whole[:, here]
-
-
-def weigh(slot, weights, parts, dy):
-    stack(parts, dy)
-    n = dy.shape[0] // 2
-    for at, row in enumerate((slot, slot + 4)):
-        part = slice(at * n, (at + 1) * n)
-        dy[part, :] = (dy[part, :].astype(F32) * per_row(weights[...], row, dy.shape[1])).astype(BF16)
-
-
-def early_kernel(weights, *refs):
-    hids, dys, parts, (out_a, out_b, dy, left, right) = refs[:4], refs[4:7], refs[7:-5], refs[-5:]
-    weigh(3, weights, parts, dy)
+    part_s[:, width // 2 :] = whole[:, width:]
+
+
+def early_kernel(offs, *refs):
+    hids, dys, parts, (out_a, out_b, dy, gates, held, left, right) = refs[:4], refs[4:7], refs[7:-7], refs[-7:]
+    stack(parts, held)
+    half = dy.shape[1]
+    gate = gate_column(offs[8], held[:, half:])
+    gates[...] = jnp.broadcast_to(gate, gates.shape)
+    dy[...] = (held[:, :half].astype(F32) * gate).astype(BF16)
     stack(hids, left)
     stack((*dys, dy), right)
-    half = right.shape[1] // 2
-    out_a[0, :, :] = tn(left[...], right[:, :half]).astype(BF16)
-    out_b[0, :, :] = tn(left[...], right[:, half:]).astype(BF16)
-
-
-def out_kernel(slot, weights, hid, down, out_m, out_o):
-    n, width = out_m.shape
-    out = nn(hid[...], down[...])
-    out_m[...] = (out[:n] * per_row(weights[...], slot, width)).astype(BF16)
-    out_o[...] = (out[n:] * per_row(weights[...], slot + 4, width)).astype(BF16)
-
-
-def sum_kernel(*refs):
+    out_a[0, :, :] = tn(left[...], right[:, : half // 2]).astype(BF16)
+    out_b[0, :, :] = tn(left[...], right[:, half // 2 :]).astype(BF16)
+
+
+def out_kernel(hid, down, gates, out_m, out_o):
+    n = out_m.shape[0]
+    out = nn(hid[...], down[...]) * gates[:, :1]
+    out_m[...] = out[:n].astype(BF16)
+    out_o[...] = out[n:].astype(BF16)
+
+
+def sum_kernel(spec, *refs):
     *parts, out = refs
-    out[...] = sum(part[...].astype(F32) for part in parts).astype(BF16)
-
-
-def last_kernel(offs, weights, fac_g, fac_u, down, dy_s, *refs):
+    total, at = 0.0, 0
+    for count, low in spec:
+        if count == 1:
+            term = parts[at][low : low + out.shape[0], :]
+        else:
+            term = jnp.concatenate([part[...] for part in parts[at : at + count]], axis=0)
+        total = total + term.astype(F32)
+        at += count
+    out[...] = total.astype(BF16)
+
+
+def last_kernel(offs, gates, fac_g, fac_u, down, dy_s, *refs):
     parts, (d_gate, d_up, dy_k, dy) = refs[:-4], refs[-4:]
     size = down.shape[1] // 8
-    weigh(3, weights, parts, dy_k)
+    stack(parts, dy_k)
+    dy_k[...] = (dy_k[...].astype(F32) * gates[:, :1]).astype(BF16)
     for at in range(8):
         here = pl.ds(pl.multiple_of(offs[at], size), size)
         dy[:, here] = (dy_s if at < 4 else dy_k)[:, pl.ds(at % 4 * size, size)]
@@ -299,27 +317,6 @@
     return sum(value.astype(F32) for value in values)
 
 
-def slot_sources(n_expert):
-    me = lax.axis_index("expert")
-    order = ring_order(n_expert // 2)
-    spot = sum(jnp.where(me // 2 == at, where, 0) for where, at in enumerate(order))
-    rows = []
-    for core in (0, 1):
-        for slot in range(n_expert // 2):
-            back = lax.rem(spot - slot + len(order), len(order))
-            chip = sum(jnp.where(back == where, at, 0) for where, at in enumerate(order))
-            rows.append(2 * chip + lax.rem(me + core, 2))
-    return jnp.stack(rows).astype(jnp.int32)
-
-
-def slot_weights(sources, expert_ids, gate_fixed, n_expert):
-    gate_values = gate_fixed.astype(F32) / 65536.0
-    experts = jnp.arange(n_expert, dtype=jnp.int32)[:, None, None]
-    table = jnp.sum(jnp.where(expert_ids.T[None] == experts, gate_values.T[None], 0.0), axis=1)
-    came = lax.all_to_all(table, "expert", split_axis=0, concat_axis=0, tiled=True)
-    return jnp.sum(jnp.where(sources[:, None, None] == jnp.arange(n_expert)[None, :, None], came[None], 0.0), axis=1)
-
-
 class Order:
     def __init__(self, start):
         self.last = start
@@ -355,7 +352,8 @@
 
     gate_w, up_w, down_w = w_gate[0].T, w_up[0].T, w_down[0]
     me = lax.axis_index("dp")
-    offs = jnp.stack([((me ^ rel) * 2 + part) * (width // 8) for rel, part in PIECES]).astype(jnp.int32)
+    offs = [((me ^ rel) * 2 + part) * (width // 8) for rel, part in PIECES]
+    offs = jnp.stack([*offs, lax.axis_index("expert")]).astype(jnp.int32)
 
     def forward(slot, *parts):
         pair = 2 * n
@@ -368,14 +366,14 @@
             smem=1,
         )
 
-    def backward(slot, ahead, mine, *others):
+    def backward(slot, ahead, *parts):
         pair = 2 * n
         return launch(
             f"backward_{slot}",
-            partial(backward_kernel, slot),
+            backward_kernel,
             [((n, width), BF16)] * 2 + [((pair, ff), BF16)] * 2 + [((pair, half), BF16)] * 2,
-            [offs, weights, *ahead[:3], down_w, mine, *others],
-            [((pair, width), BF16)],
+            [offs, *ahead[:3], down_w, *parts],
+            [((pair, width + 128), BF16), ((pair, width), BF16)],
             smem=1,
         )
 
@@ -417,38 +415,39 @@
         return launch(
             "early",
             early_kernel,
-            [((1, ff, half // 2), BF16)] * 2 + [((2 * n, half), BF16)],
-            [weights, *hids, *dys_s, *parts],
-            [((8 * n, ff), BF16), ((8 * n, half), BF16)],
+            [((1, ff, half // 2), BF16)] * 2 + [((2 * n, half), BF16), ((2 * n, 128), F32)],
+            [offs, *hids, *dys_s, *parts],
+            [((2 * n, half + 128), BF16), ((8 * n, ff), BF16), ((8 * n, half), BF16)],
+            smem=1,
         )
 
-    def outputs(slot, hid):
-        return launch(
-            f"out_{slot}", partial(out_kernel, slot), [((n, width), BF16)] * 2, [weights, hid, down_w]
-        )
-
-    def backward_last(dy_s, *parts):
+    def outputs(name, hid, gates):
+        return launch(name, out_kernel, [((n, width), BF16)] * 2, [hid, down_w, gates])
+
+    def backward_last(gates, dy_s, *parts):
         return launch(
             "backward_3",
             last_kernel,
             [((2 * n, ff), BF16)] * 2 + [((2 * n, half), BF16)],
-            [offs, weights, *f3[1:3], down_w, dy_s, *parts],
+            [offs, gates, *f3[1:3], down_w, dy_s, *parts],
             [((2 * n, width), BF16)],
             smem=1,
         )
 
-    def total_of(name, *parts):
-        return launch(name, sum_kernel, [(parts[0].shape, BF16)], parts)[0]
+    def sums(name, *terms, rows=n, low=0):
+        terms = [term if isinstance(term, list) else [term] for term in terms]
+        spec = tuple((len(term), low if term[0].shape[0] > rows else 0) for term in terms)
+        ins = [part for term in terms for part in term]
+        return launch(name, partial(sum_kernel, spec), [((rows, width), BF16)], ins)[0]
 
     order = Order(jnp.zeros((8, 128), F32))
-    sources = slot_sources(n_expert)
-    t0, c0 = tokens, cotangent
-    t1, c1 = ring(t0, "t1"), ring(c0, "c1")
-    p0, q0 = twin(t0, "p0"), twin(c0, "q0")
-    weights = slot_weights(sources, expert_ids, gate_fixed, n_expert)
-    t1, weights = order.point(t1, weights)
+    t0 = tokens
+    t1, p0 = ring(t0, "t1"), twin(t0, "p0")
+    c0 = launch("pack", pack_kernel, [((n, width + 128), BF16)], [expert_ids, gate_fixed, cotangent])[0]
+    c1, q0 = ring(c0, "c1"), twin(c0, "q0")
+    (t1,) = order.point(t1)
     t2, p1 = ring(t1, "t2"), twin(t1, "p1")
-    c1, p0 = order.point(c1, p0)
+    c1, p0, p1 = order.point(c1, p0, p1)
     c2, q1 = ring(c1, "c2"), twin(c1, "q1")
     f0 = forward(0, t0, p0)
     f1 = forward(1, t1, p1)
@@ -457,51 +456,52 @@
     b0 = backward(0, f0, c0, q0)
     b1 = backward(1, f1, c1, q1)
     o1 = twin(b1[1], "o1")
-    c2, b0[0], b1[0] = order.point(c2, b0[0], b1[0])
-    c2s, c2k = launch("split", split_kernel, [((n, half), BF16)] * 2, [offs, c2], smem=1)
-    c3s, c3k = ring(c2s, "c3s"), ring(c2k, "c3k")
+    c2, p2, b0[0], b1[0] = order.point(c2, p2, b0[0], b1[0])
+    c2s, c2k = launch("split", split_kernel, [((n, half + 128), BF16), ((n, half), BF16)], [offs, c2], smem=1)
+    c3s = ring(c2s, "c3s")
     q2 = twins(c2, "q2")
     f2 = forward(2, t2, p2)
     b2 = backward(2, f2, c2, *q2)
     o2 = twin(b2[1], "o2")
     t3, o1, f2[0], b2[0] = order.point(t3, o1, f2[0], b2[0])
+    c3k = ring(c2k, "c3k")
     p3 = twins(t3, "p3")
+    m = ring(sums("add_m1", b1[0], o1), "m1")
     c3s, o2 = order.point(c3s, o2)
     q3s = twins(c3s, "q3s")
     f3 = forward(3, t3, *p3)
     hids, facs_g, facs_u, rows_s, rows_k = ([f[at] for f in (f0, f1, f2, f3)] for at in range(5))
     dys_s = [b[4] for b in (b0, b1, b2)]
-    *sent, dy3 = early(c3s, *q3s)
+    *sent, dy3, gates3 = early(c3s, *q3s)
     dy3, *sent = order.point(dy3, *sent)
     down_came = flips(sent, (1, 2), "d1")
-    m = ring(total_of("add_m1", b1[0], o1), "m1")
-    out3 = outputs(3, f3[0])
+    out3 = outputs("out_3", f3[0], gates3)
     (c3k,) = order.point(c3k)
-    q3k = twin(c3k, "q3k")
-    b3 = backward_last(dy3, c3k, q3k)
+    q3k = twins(c3k, "q3k")
+    b3 = backward_last(gates3, dy3, c3k, *q3k)
     b3 = [*out3, *b3[:2], dy3, b3[2]]
     outs_m, outs_o, d_gates, d_ups, dys_s, dys_k = ([b[at] for b in (b0, b1, b2, b3)] for at in range(6))
     sent = grads("both_s", ((0, 2), (1, 2)), d_gates, d_ups, rows_s)
     d_gates[1], *sent = order.point(d_gates[1], *sent)
     m1, r1 = row_grads("rows_1", 1)
     m, d_gates[2], r1 = order.point(m, d_gates[2], r1)
-    m = ring(total_of("add_m2", m, outs_m[2], o2), "m2")
+    m = ring(sums("add_m2", m, outs_m[2], o2), "m2")
     r1, o3 = twin(r1, "r1"), twin(outs_o[3], "o3")
+    r1, o3, d_gates[0], *down_came = order.point(r1, o3, d_gates[0], *down_came)
+    both_came = flips(sent, (1, 2), "gu1")
+    g = ring(sums("add_g1", m1, r1), "ga1")
+    o0 = twin(outs_o[0], "o0")
     m2, r2 = row_grads("rows_2", 2)
     m3, r3 = row_grads("rows_3", 3)
     m0, r0 = row_grads("rows_0", 0)
-    r1, o3, r2, r3, r0, d_gates[0], *down_came = order.point(r1, o3, r2, r3, r0, d_gates[0], *down_came)
-    both_came = flips(sent, (1, 2), "gu1")
-    g = ring(total_of("add_g1", m1, r1), "ga1")
     own = grads("kept_k", ((0, 2), (1, 2), (3, 4)), d_gates, d_ups, rows_k, hids, dys_k)
-    o0 = twin(outs_o[0], "o0")
-    m, o0, *own = order.point(m, o0, *own)
-    m = ring(total_of("add_m3", m, outs_m[3], o3), "m3")
+    m, o0, m2, r2, m3, r3, m0, r0, *own = order.point(m, o0, m2, r2, m3, r3, m0, r0, *own)
+    m = ring(sums("add_m3", m, outs_m[3], o3), "m3")
     r2 = twin(r2, "r2")
     g, r2 = order.point(g, r2)
-    g = ring(total_of("add_g2", g, m2, r2), "ga2")
+    g = ring(sums("add_g2", g, m2, r2), "ga2")
     r3 = twin(r3, "r3")
-    both_came = order.point(*both_came)
+    both_came[0], both_came[1], m = order.point(*both_came, m)
     *far, near_a, near_b = launch(
         "cross",
         cross_kernel,
@@ -510,11 +510,11 @@
     )
     far = order.point(*far)
     last = flips(far, (2, 1), "last")
-    g, r3, m = order.point(g, r3, m)
+    g, r3 = order.point(g, r3)
     g = ring(add(g, kept(m3, r3)).astype(BF16), "ga3")
     r0 = twin(r0, "r0")
-    mixed = total_of("add_m0", m, outs_m[0], o0)
-    mixed, r0, g = order.point(mixed, r0, g)
+    mixed = sums("add_m0", m, outs_m[0], o0)
+    g, r0, mixed = order.point(g, r0, mixed)
     token_grad = add(g, kept(m0, r0)).astype(BF16)
     token_grad, *last = order.point(token_grad, *last)
     grad_gate, grad_up, grad_down = launch(

time: 169 us -> 161 us (0.953)
  waiting for transfers between devices: 83.3 us -> 65.7 us
  starting transfers between devices: 29.7 us -> 37.4 us
  local copies, waits for them, and re-layouts: 4.96 us -> 9.11 us
  other arithmetic: 3.46 us -> 1.28 us
    all_to_all x1 -> x0, waiting for transfers between devices: 17.4 us -> none  [slot_weights(): lax.all_to_all(table, 'expert', split_axis=0, concat_axis=0, tiled=True)]
    ppermute x13, starting transfers between devices: 14.6 us -> 27.1 us  [step(): lax.ppermute(value, 'expert', [(2 * at + core, 2 * follow[at] + core) for...]
    ppermute x13, waiting for transfers between devices: 53.6 us -> 61.1 us  [step(): lax.ppermute(value, 'expert', [(2 * at + core, 2 * follow[at] + core) for...]
    ppermute x6, waiting for transfers between devices: 11.7 us -> 4.51 us  [flip(): return lax.ppermute(value, 'dp', [(at, at ^ mask) for at in range(4)])]
    unnamed x14 -> x23, local copies, waits for them, and re-layouts: 4.7 us -> 8.11 us
    all_to_all x1 -> x0, starting transfers between devices: 3.31 us -> none  [slot_weights(): lax.all_to_all(table, 'expert', split_axis=0, concat_axis=0, tiled=True)]
    ppermute x6, starting transfers between devices: 8.23 us -> 6.5 us  [flip(): return lax.ppermute(value, 'dp', [(at, at ^ mask) for at in range(4)])]
    pallas_call x25 -> x26, Pallas kernels: 45.6 us -> 46.1 us  [call(): pl.pallas_call(kernel, name=name, out_shape=[jax.ShapeDtypeStruct(shape,...]
  transfers between devices with their start and end apart: 40 -> 40, of which waited for: 15 -> 13; matrix products, arithmetic and copies ran while one was open for 2% -> 2% of each run, Pallas kernels for 26% -> 27%
where the time goes in v4:
time: 161 us
  waiting for transfers between devices  65.7 us (41%)
  Pallas kernels  46.1 us (29%)
  starting transfers between devices  37.4 us (23%)
  local copies, waits for them, and re-layouts  9.11 us (6%)
    ppermute x13, waiting for transfers between devices, step(): lax.ppermute(value, 'expert', [(2 * at + core, 2 * follow[at] + core) for...  61.1 us
    pallas_call x26, Pallas kernels, call(): pl.pallas_call(kernel, name=name, out_shape=[jax.ShapeDtypeStruct(shape,...  46.1 us
    ppermute x13, starting transfers between devices, step(): lax.ppermute(value, 'expert', [(2 * at + core, 2 * follow[at] + core) for...  27.1 us
    unnamed x23, local copies, waits for them, and re-layouts  8.11 us
    ppermute x6, starting transfers between devices, flip(): return lax.ppermute(value, 'dp', [(at, at ^ mask) for at in range(4)])  6.5 us
    ppermute x6, waiting for transfers between devices, flip(): return lax.ppermute(value, 'dp', [(at, at ^ mask) for at in range(4)])  4.51 us
    ppermute x21, starting transfers between devices, swap(): lax.ppermute(value, 'expert', [(at, at ^ 1) for at in range(n_expert)])  3.79 us
  transfers between devices with their start and end apart: 40, of which 13 were waited for; matrix products, arithmetic and copies ran while one was open for 2% of the time, Pallas kernels for 27%

profile of v4, /device:TPU:0, one launch (start us, length us, event | category | flops | bytes accessed | tf_op | source)
XLA Modules:
  0.0 160.7 jit_solution(12023025815542528691)
XLA Ops:
  0.6 3.1 %collective-permute-start = (bf16[128,2048]{1,0:T(8,128)(2,1)}, bf16[128,2048]{1,0:T(8,128)(2,1)}, u32[]{:S(2)}, u32[]{:S(2)}) collective-permute-start(bf16[128,2048]{1,0:T(8,128)(2,1)} %refs_0_), channel_id=1, source_target_pairs={{0,2},{1,3},{2,6},{3,7},{6,4},{7,5},{4,0},{5,1},{8,10},{9,11},{10,... | collective-permute-start | bytes 1572872 | tf_op jit(solution)/shard_map/t1/ppermute | solution.py:305
  6.8 2.6 %collective-permute-start.2 = (bf16[128,2176]{1,0:T(8,128)(2,1)S(1)}, bf16[128,2176]{1,0:T(8,128)(2,1)S(1)}, u32[]{:S(2)}, u32[]{:S(2)}) collective-permute-start(bf16[128,2176]{1,0:T(8,128)(2,1)S(1)} %pack.1.refs_0_), channel_id=1, source_target_pairs={{0,2},{1,3},{2,6},{3,7},{6,4},{7,5},{4,0},{5,1},{8,10},{9,11},{10,... | collective-permute-start | bytes 1671176 | tf_op jit(solution)/shard_map/c1/ppermute | solution.py:305
  9.5 8.3 %collective-permute-done.refs_0_ = bf16[128,2048]{1,0:T(8,128)(2,1)} collective-permute-done((bf16[128,2048]{1,0:T(8,128)(2,1)}, bf16[128,2048]{1,0:T(8,128)(2,1)}, u32[]{:S(2)}, u32[]{:S(2)}) %collective-permute-start) | collective-permute-done | bytes 524320 | tf_op jit(solution)/shard_map/t1/ppermute | solution.py:305
  20.0 9.7 %collective-permute-done.2.refs_0_ = bf16[128,2176]{1,0:T(8,128)(2,1)S(1)} collective-permute-done((bf16[128,2176]{1,0:T(8,128)(2,1)S(1)}, bf16[128,2176]{1,0:T(8,128)(2,1)S(1)}, u32[]{:S(2)}, u32[]{:S(2)}) %collective-permute-start.2) | collective-permute-done | bytes 557088 | tf_op jit(solution)/shard_map/c1/ppermute | solution.py:305
  36.3 3.2 %forward_1.1 = (bf16[256,704]{1,0:T(8,128)(2,1)S(1)}, f32[256,704]{1,0:T(8,128)S(1)}, f32[256,704]{1,0:T(8,128)S(1)}, bf16[256,1024]{1,0:T(8,128)(2,1)S(1)}, bf16[256,1024]{1,0:T(8,128)(2,1)S(1)}) custom-call(s32[9]{0:T(128)S(1)} %stack.39.offs, bf16[128,2048]{1,0:T(8,128)(2,1)} %collective-permute-done.refs_0_, bf16[128,2048]{1,0:T(8,128)(2,1)S(1)} %copy-done.10, ...), custom_call_target="tpu_custom_call" | custom-call | flops 1 | bytes 1 | tf_op jit(solution)/shard_map/forward_1/pallas_call | solution.py:129
  39.6 2.6 %forward_0.1 = (bf16[256,704]{1,0:T(8,128)(2,1)S(1)}, f32[256,704]{1,0:T(8,128)S(1)}, f32[256,704]{1,0:T(8,128)S(1)}, bf16[256,1024]{1,0:T(8,128)(2,1)S(1)}, bf16[256,1024]{1,0:T(8,128)(2,1)S(1)}) custom-call(s32[9]{0:T(128)S(1)} %stack.39.offs, bf16[128,2048]{1,0:T(8,128)(2,1)S(1)} %copy-done.6, bf16[128,2048]{1,0:T(8,128)(2,1)S(1)} %copy-done.8, ...), custom_call_target="tpu_custom_call" | custom-call | flops 1 | bytes 1 | tf_op jit(solution)/shard_map/forward_0/pallas_call | solution.py:129
  42.5 3.4 %collective-permute-start.9 = (bf16[128,2048]{1,0:T(8,128)(2,1)S(1)}, bf16[128,2048]{1,0:T(8,128)(2,1)S(1)}, u32[]{:S(2)}, u32[]{:S(2)}) collective-permute-start(bf16[128,2048]{1,0:T(8,128)(2,1)S(1)} %collective-permute-done.1.refs_0_), channel_id=1, source_target_pairs={{0,2},{1,3},{2,6},{3,7},{6,4},{7,5},{4,0},{5,1},{8,10},{9,11},{10,... | collective-permute-start | bytes 1572872 | tf_op jit(solution)/shard_map/t3/ppermute | solution.py:305
  45.9 2.9 %backward_0.1 = (bf16[128,2048]{1,0:T(8,128)(2,1)S(1)}, bf16[128,2048]{1,0:T(8,128)(2,1)S(1)}, bf16[256,704]{1,0:T(8,128)(2,1)S(1)}, bf16[256,704]{1,0:T(8,128)(...) custom-call(s32[9]{0:T(128)S(1)} %stack.39.offs, ...), custom_call_target="tpu_custom_call" | custom-call | flops 1 | bytes 1 | tf_op jit(solution)/shard_map/backward_0/pallas_call | solution.py:129
  48.8 2.9 %backward_1.1 = (bf16[128,2048]{1,0:T(8,128)(2,1)S(1)}, bf16[128,2048]{1,0:T(8,128)(2,1)S(1)}, bf16[256,704]{1,0:T(8,128)(2,1)S(1)}, bf16[256,704]{1,0:T(8,128)(...) custom-call(s32[9]{0:T(128)S(1)} %stack.39.offs, ...), custom_call_target="tpu_custom_call" | custom-call | flops 1 | bytes 1 | tf_op jit(solution)/shard_map/backward_1/pallas_call | solution.py:129
  53.4 2.6 %forward_2.1 = (bf16[256,704]{1,0:T(8,128)(2,1)S(1)}, f32[256,704]{1,0:T(8,128)S(1)}, f32[256,704]{1,0:T(8,128)S(1)}, bf16[256,1024]{1,0:T(8,128)(2,1)S(1)}, bf16[256,1024]{1,0:T(8,128)(2,1)S(1)}) custom-call(s32[9]{0:T(128)S(1)} %stack.39.offs, bf16[128,2048]{1,0:T(8,128)(2,1)S(1)} %collective-permute-done.1.refs_0_, ...), custom_call_target="tpu_custom_call" | custom-call | flops 1 | bytes 1 | tf_op jit(solution)/shard_map/forward_2/pallas_call | solution.py:129
  56.0 2.9 %backward_2.1 = (bf16[128,2048]{1,0:T(8,128)(2,1)S(1)}, bf16[128,2048]{1,0:T(8,128)(2,1)S(1)}, bf16[256,704]{1,0:T(8,128)(2,1)S(1)}, bf16[256,704]{1,0:T(8,128)(...) custom-call(s32[9]{0:T(128)S(1)} %stack.39.offs, ...), custom_call_target="tpu_custom_call" | custom-call | flops 1 | bytes 1 | tf_op jit(solution)/shard_map/backward_2/pallas_call | solution.py:129
  65.1 5.4 %collective-permute-done.14.refs_7_ = bf16[128,1152]{1,0:T(8,128)(2,1)S(1)} collective-permute-done((bf16[128,1152]{1,0:T(8,128)(2,1)S(1)}, bf16[128,1152]{1,0:T(8,128)(2,1)S(1)}, u32[]{:S(2)}, u32[]{:S(2)}) %collective-permute-start.14) | collective-permute-done | bytes 294944 | tf_op jit(solution)/shard_map/c3s/ppermute | solution.py:305
  72.2 2.6 %forward_3.1 = (bf16[256,704]{1,0:T(8,128)(2,1)S(1)}, f32[256,704]{1,0:T(8,128)S(1)}, f32[256,704]{1,0:T(8,128)S(1)}, bf16[256,1024]{1,0:T(8,128)(2,1)S(1)}, bf16[256,1024]{1,0:T(8,128)(2,1)S(1)}) custom-call(s32[9]{0:T(128)S(1)} %stack.39.offs, bf16[128,2048]{1,0:T(8,128)(2,1)S(1)} %collective-permute-done.9.refs_0_, ...), custom_call_target="tpu_custom_call" | custom-call | flops 1 | bytes 1 | tf_op jit(solution)/shard_map/forward_3/pallas_call | solution.py:129
  83.6 3.2 %both_s.1 = (bf16[2,704,512]{2,1,0:T(8,128)(2,1)S(1)}, bf16[2,704,512]{2,1,0:T(8,128)(2,1)S(1)}) custom-call(bf16[256,704]{1,0:T(8,128)(2,1)S(1)} %get-tuple-element.333.refs_0_, bf16[256,704]{1,0:T(8,128)(2,1)S(1)} %get-tuple-element.297.refs_1_.refs_0_, bf16[256,704]{1,0:T(8,128)(2,1)S(1)} %get-tuple-element.326.refs_2_.refs_0_, ...), custom_call_target="tpu_custom_call" | custom-call | flops 1 | bytes 1 | tf_op jit(solution)/shard_map/both_s/pallas_call | solution.py:129
  89.4 3.7 %collective-permute-start.28 = (bf16[128,2048]{1,0:T(8,128)(2,1)S(1)}, bf16[128,2048]{1,0:T(8,128)(2,1)S(1)}, u32[]{:S(2)}, u32[]{:S(2)}) collective-permute-start(bf16[128,2048]{1,0:T(8,128)(2,1)S(1)} %add_m2.1), channel_id=1, source_target_pairs={{0,2},{1,3},{2,6},{3,7},{6,4},{7,5},{4,0},{5,1},{8,10},{9,11},{10,... | collective-permute-start | bytes 1572872 | tf_op jit(solution)/shard_map/m2/ppermute | solution.py:305
  104.1 3.4 %collective-permute-start.27 = (bf16[128,2048]{1,0:T(8,128)(2,1)S(1)}, bf16[128,2048]{1,0:T(8,128)(2,1)S(1)}, u32[]{:S(2)}, u32[]{:S(2)}) collective-permute-start(bf16[128,2048]{1,0:T(8,128)(2,1)S(1)} %add_g1.1), channel_id=1, source_target_pairs={{0,2},{1,3},{2,6},{3,7},{6,4},{7,5},{4,0},{5,1},{8,10},{9,11},{10,... | collective-permute-start | bytes 1572872 | tf_op jit(solution)/shard_map/ga1/ppermute | solution.py:305
  107.5 4.8 %kept_k.1 = (bf16[3,704,512]{2,1,0:T(8,128)(2,1)S(1)}, bf16[3,704,512]{2,1,0:T(8,128)(2,1)S(1)}) custom-call(bf16[256,704]{1,0:T(8,128)(2,1)S(1)} %get-tuple-element.333.refs_0_, bf16[256,704]{1,0:T(8,128)(2,1)S(1)} %get-tuple-element.297.refs_1_.refs_0_, bf16[256,704]{1,0:T(8,128)(2,1)S(1)} %get-tuple-element.326.refs_2_.refs_0_, ...), custom_call_target="tpu_custom_call" | custom-call | flops 1 | bytes 1 | tf_op jit(solution)/shard_map/kept_k/pallas_call | solution.py:129
  112.6 7.2 %collective-permute-done.27.refs_0_ = bf16[128,2048]{1,0:T(8,128)(2,1)S(1)} collective-permute-done((bf16[128,2048]{1,0:T(8,128)(2,1)S(1)}, bf16[128,2048]{1,0:T(8,128)(2,1)S(1)}, u32[]{:S(2)}, u32[]{:S(2)}) %collective-permute-start.27) | collective-permute-done | bytes 524320 | tf_op jit(solution)/shard_map/ga1/ppermute | solution.py:305
  120.1 2.5 %collective-permute-start.31 = (bf16[128,2048]{1,0:T(8,128)(2,1)S(1)}, bf16[128,2048]{1,0:T(8,128)(2,1)S(1)}, u32[]{:S(2)}, u32[]{:S(2)}) collective-permute-start(bf16[128,2048]{1,0:T(8,128)(2,1)S(1)} %add_g2.1), channel_id=1, source_target_pairs={{0,2},{1,3},{2,6},{3,7},{6,4},{7,5},{4,0},{5,1},{8,10},{9,11},{10,... | collective-permute-start | bytes 1572872 | tf_op jit(solution)/shard_map/ga2/ppermute | solution.py:305
  122.6 8.4 %collective-permute-done.35.refs_0_ = bf16[128,2048]{1,0:T(8,128)(2,1)S(1)} collective-permute-done((bf16[128,2048]{1,0:T(8,128)(2,1)S(1)}, bf16[128,2048]{1,0:T(8,128)(2,1)S(1)}, u32[]{:S(2)}, u32[]{:S(2)}) %collective-permute-start.35) | collective-permute-done | bytes 524320 | tf_op jit(solution)/shard_map/m3/ppermute | solution.py:305
  134.1 7.2 %collective-permute-done.31 = bf16[128,2048]{1,0:T(8,128)(2,1)S(1)} collective-permute-done((bf16[128,2048]{1,0:T(8,128)(2,1)S(1)}, bf16[128,2048]{1,0:T(8,128)(2,1)S(1)}, u32[]{:S(2)}, u32[]{:S(2)}) %collective-permute-start.31) | collective-permute-done | bytes 524320 | tf_op jit(solution)/shard_map/ga2/ppermute | solution.py:305
  141.6 2.5 %collective-permute-start.36 = (bf16[128,2048]{1,0:T(8,128)(2,1)S(1)}, bf16[128,2048]{1,0:T(8,128)(2,1)S(1)}, u32[]{:S(2)}, u32[]{:S(2)}) collective-permute-start(bf16[128,2048]{1,0:T(8,128)(2,1)S(1)} %add_convert_fusion.1), channel_id=1, source_target_pairs={{0,2},{1,3},{2,6},{3,7},{6,4},{7,5},{4,0},{5,1},{8,10},{9,11},{10,... | collective-permute-start | bytes 1572872 | tf_op jit(solution)/shard_map/ga3/ppermute | solution.py:305
  145.1 11.7 %collective-permute-done.36 = bf16[128,2048]{1,0:T(8,128)(2,1)S(1)} collective-permute-done((bf16[128,2048]{1,0:T(8,128)(2,1)S(1)}, bf16[128,2048]{1,0:T(8,128)(2,1)S(1)}, u32[]{:S(2)}, u32[]{:S(2)}) %collective-permute-start.36) | collective-permute-done | bytes 524320 | tf_op jit(solution)/shard_map/ga3/ppermute | solution.py:305
  158.2 2.4 %finish.1 = (f32[704,512]{1,0:T(8,128)}, f32[704,512]{1,0:T(8,128)}, f32[704,512]{1,0:T(8,128)}) custom-call(f32[3,704,256]{2,1,0:T(8,128)S(1)} %get-tuple-element.397.near_a, f32[3,704,256]{2,1,0:T(8,128)S(1)} %get-tuple-element.398.near_b, bf16[3,704,256]{2,1,0:T(8,128)(2,1)S(1)} %collective-permute-done.38.last_a, ...), custom_call_target="tpu_custom_call" | custom-call | flops 1 | bytes 1 | tf_op jit(solution)/shard_map/finish/pallas_call | solution.py:129
  (113 shorter events, 50.4 us)
Async XLA Ops:
  0.6 17.2 %collective-permute-start = (bf16[128,2048]{1,0:T(8,128)(2,1)}, bf16[128,2048]{1,0:T(8,128)(2,1)}, u32[]{:S(2)}, u32[]{:S(2)}) collective-permute-start(bf16[128,2048]{1,0:T(8,128)(2,1)} %refs_0_), channel_id=1, source_target_pairs={{0,2},{1,3},{2,6},{3,7},{6,4},{7,5},{4,0},{5,1},{8,10},{9,11},{10,... | collective-permute-start | bytes 1572872 | tf_op jit(solution)/shard_map/t1/ppermute | solution.py:305
  6.8 22.8 %collective-permute-start.2 = (bf16[128,2176]{1,0:T(8,128)(2,1)S(1)}, bf16[128,2176]{1,0:T(8,128)(2,1)S(1)}, u32[]{:S(2)}, u32[]{:S(2)}) collective-permute-start(bf16[128,2176]{1,0:T(8,128)(2,1)S(1)} %pack.1.refs_0_), channel_id=1, source_target_pairs={{0,2},{1,3},{2,6},{3,7},{6,4},{7,5},{4,0},{5,1},{8,10},{9,11},{10,... | collective-permute-start | bytes 1671176 | tf_op jit(solution)/shard_map/c1/ppermute | solution.py:305
  17.8 11.8 %collective-permute-start.4 = (bf16[128,2048]{1,0:T(8,128)(2,1)}, bf16[128,2048]{1,0:T(8,128)(2,1)S(1)}, u32[]{:S(2)}, u32[]{:S(2)}) collective-permute-start(bf16[128,2048]{1,0:T(8,128)(2,1)} %collective-permute-done.refs_0_), channel_id=1, source_target_pairs={{0,1},{1,0},{2,3},{3,2},{4,5},{5,4},{6,7},{7,6},{8,9},{9,8},{10,11... | collective-permute-start | bytes 1572872 | tf_op jit(solution)/shard_map/p1/ppermute | solution.py:309
  17.8 24.4 %collective-permute-start.1 = (bf16[128,2048]{1,0:T(8,128)(2,1)}, bf16[128,2048]{1,0:T(8,128)(2,1)S(1)}, u32[]{:S(2)}, u32[]{:S(2)}) collective-permute-start(bf16[128,2048]{1,0:T(8,128)(2,1)} %collective-permute-done.refs_0_), channel_id=1, source_target_pairs={{0,2},{1,3},{2,6},{3,7},{6,4},{7,5},{4,0},{5,1},{8,10},{9,11},{10,... | collective-permute-start | bytes 1572872 | tf_op jit(solution)/shard_map/t2/ppermute | solution.py:305
  18.9 27.0 %collective-permute-start.6 = (bf16[128,2176]{1,0:T(8,128)(2,1)S(1)}, bf16[128,2176]{1,0:T(8,128)(2,1)S(1)}, u32[]{:S(2)}, u32[]{:S(2)}) collective-permute-start(bf16[128,2176]{1,0:T(8,128)(2,1)S(1)} %pack.1.refs_0_), channel_id=1, source_target_pairs={{0,1},{1,0},{2,3},{3,2},{4,5},{5,4},{6,7},{7,6},{8,9},{9,8},{10,11... | collective-permute-start | bytes 1671176 | tf_op jit(solution)/shard_map/q0/ppermute | solution.py:309
  30.4 18.4 %collective-permute-start.5 = (bf16[128,2176]{1,0:T(8,128)(2,1)S(1)}, bf16[128,2176]{1,0:T(8,128)(2,1)S(1)}, u32[]{:S(2)}, u32[]{:S(2)}) collective-permute-start(bf16[128,2176]{1,0:T(8,128)(2,1)S(1)} %collective-permute-done.2.refs_0_), channel_id=1, source_target_pairs={{0,1},{1,0},{2,3},{3,2},{4,5},{5,4},{6,7},{7,6},{8,9},{9,8},{10,11... | collective-permute-start | bytes 1671176 | tf_op jit(solution)/shard_map/q1/ppermute | solution.py:309
  30.4 22.4 %collective-permute-start.7 = (bf16[128,2176]{1,0:T(8,128)(2,1)S(1)}, bf16[128,2176]{1,0:T(8,128)(2,1)S(1)}, u32[]{:S(2)}, u32[]{:S(2)}) collective-permute-start(bf16[128,2176]{1,0:T(8,128)(2,1)S(1)} %collective-permute-done.2.refs_0_), channel_id=1, source_target_pairs={{0,2},{1,3},{2,6},{3,7},{6,4},{7,5},{4,0},{5,1},{8,10},{9,11},{10,... | collective-permute-start | bytes 1671176 | tf_op jit(solution)/shard_map/c2/ppermute | solution.py:305
  42.5 20.7 %collective-permute-start.9 = (bf16[128,2048]{1,0:T(8,128)(2,1)S(1)}, bf16[128,2048]{1,0:T(8,128)(2,1)S(1)}, u32[]{:S(2)}, u32[]{:S(2)}) collective-permute-start(bf16[128,2048]{1,0:T(8,128)(2,1)S(1)} %collective-permute-done.1.refs_0_), channel_id=1, source_target_pairs={{0,2},{1,3},{2,6},{3,7},{6,4},{7,5},{4,0},{5,1},{8,10},{9,11},{10,... | collective-permute-start | bytes 1572872 | tf_op jit(solution)/shard_map/t3/ppermute | solution.py:305
  58.9 12.6 %collective-permute-start.15 = (bf16[128,2048]{1,0:T(8,128)(2,1)S(1)}, bf16[128,2048]{1,0:T(8,128)(2,1)S(1)}, u32[]{:S(2)}, u32[]{:S(2)}) collective-permute-start(bf16[128,2048]{1,0:T(8,128)(2,1)S(1)} %get-tuple-element.254), channel_id=1, source_target_pairs={{0,1},{1,0},{2,3},{3,2},{4,5},{5,4},{6,7},{7,6},{8,9},{9,8},{10,11... | collective-permute-start | bytes 1572872 | tf_op jit(solution)/shard_map/o2/ppermute | solution.py:309
  63.3 13.7 %collective-permute-start.13 = (bf16[128,1024]{1,0:T(8,128)(2,1)S(1)}, bf16[128,1024]{1,0:T(8,128)(2,1)S(1)}, u32[]{:S(2)}, u32[]{:S(2)}) collective-permute-start(bf16[128,1024]{1,0:T(8,128)(2,1)S(1)} %get-tuple-element.250), channel_id=1, source_target_pairs={{0,2},{1,3},{2,6},{3,7},{6,4},{7,5},{4,0},{5,1},{8,10},{9,11},{10,... | collective-permute-start | bytes 786440 | tf_op jit(solution)/shard_map/c3k/ppermute | solution.py:305
  70.4 18.2 %collective-permute-start.22 = (bf16[128,2048]{1,0:T(8,128)(2,1)S(1)}, bf16[128,2048]{1,0:T(8,128)(2,1)S(1)}, u32[]{:S(2)}, u32[]{:S(2)}) collective-permute-start(bf16[128,2048]{1,0:T(8,128)(2,1)S(1)} %add_m1.1), channel_id=1, source_target_pairs={{0,2},{1,3},{2,6},{3,7},{6,4},{7,5},{4,0},{5,1},{8,10},{9,11},{10,... | collective-permute-start | bytes 1572872 | tf_op jit(solution)/shard_map/m1/ppermute | solution.py:305
  77.1 18.2 %collective-permute-start.26 = (bf16[1,704,512]{2,1,0:T(8,128)(2,1)S(1)}, bf16[1,704,512]{2,1,0:T(8,128)(2,1)S(1)}, u32[]{:S(2)}, u32[]{:S(2)}) collective-permute-start(bf16[1,704,512]{2,1,0:T(8,128)(2,1)S(1)} %get-tuple-element.313), channel_id=1, source_target_pairs={{0,16},{8,24},{16,0},{24,8},{1,17},{9,25},{17,1},{25,9},{2,18},{10... | collective-permute-start | bytes 2162696 | tf_op jit(solution)/shard_map/d1/ppermute | solution.py:313
  78.7 17.8 %collective-permute-start.25 = (bf16[1,704,512]{2,1,0:T(8,128)(2,1)S(1)}, bf16[1,704,512]{2,1,0:T(8,128)(2,1)S(1)}, u32[]{:S(2)}, u32[]{:S(2)}) collective-permute-start(bf16[1,704,512]{2,1,0:T(8,128)(2,1)S(1)} %get-tuple-element.311), channel_id=1, source_target_pairs={{0,8},{8,0},{16,24},{24,16},{1,9},{9,1},{17,25},{25,17},{2,10},{10... | collective-permute-start | bytes 2162696 | tf_op jit(solution)/shard_map/d1/ppermute | solution.py:313
  89.4 22.9 %collective-permute-start.28 = (bf16[128,2048]{1,0:T(8,128)(2,1)S(1)}, bf16[128,2048]{1,0:T(8,128)(2,1)S(1)}, u32[]{:S(2)}, u32[]{:S(2)}) collective-permute-start(bf16[128,2048]{1,0:T(8,128)(2,1)S(1)} %add_m2.1), channel_id=1, source_target_pairs={{0,2},{1,3},{2,6},{3,7},{6,4},{7,5},{4,0},{5,1},{8,10},{9,11},{10,... | collective-permute-start | bytes 1572872 | tf_op jit(solution)/shard_map/m2/ppermute | solution.py:305
  96.5 15.8 %collective-permute-start.29 = (bf16[128,2048]{1,0:T(8,128)(2,1)S(1)}, bf16[128,2048]{1,0:T(8,128)(2,1)S(1)}, u32[]{:S(2)}, u32[]{:S(2)}) collective-permute-start(bf16[128,2048]{1,0:T(8,128)(2,1)S(1)} %get-tuple-element.324), channel_id=1, source_target_pairs={{0,1},{1,0},{2,3},{3,2},{4,5},{5,4},{6,7},{7,6},{8,9},{9,8},{10,11... | collective-permute-start | bytes 1572872 | tf_op jit(solution)/shard_map/o0/ppermute | solution.py:309
  96.5 34.5 %collective-permute-start.33 = (bf16[2,704,512]{2,1,0:T(8,128)(2,1)S(1)}, bf16[2,704,512]{2,1,0:T(8,128)(2,1)S(1)}, u32[]{:S(2)}, u32[]{:S(2)}) collective-permute-start(bf16[2,704,512]{2,1,0:T(8,128)(2,1)S(1)} %get-tuple-element.358), channel_id=1, source_target_pairs={{0,8},{8,0},{16,24},{24,16},{1,9},{9,1},{17,25},{25,17},{2,10},{10... | collective-permute-start | bytes 4325384 | tf_op jit(solution)/shard_map/gu1/ppermute | solution.py:313
  98.0 33.7 %collective-permute-start.34 = (bf16[2,704,512]{2,1,0:T(8,128)(2,1)S(1)}, bf16[2,704,512]{2,1,0:T(8,128)(2,1)S(1)}, u32[]{:S(2)}, u32[]{:S(2)}) collective-permute-start(bf16[2,704,512]{2,1,0:T(8,128)(2,1)S(1)} %get-tuple-element.360), channel_id=1, source_target_pairs={{0,16},{8,24},{16,0},{24,8},{1,17},{9,25},{17,1},{25,9},{2,18},{10... | collective-permute-start | bytes 4325384 | tf_op jit(solution)/shard_map/gu1/ppermute | solution.py:313
  104.1 15.8 %collective-permute-start.27 = (bf16[128,2048]{1,0:T(8,128)(2,1)S(1)}, bf16[128,2048]{1,0:T(8,128)(2,1)S(1)}, u32[]{:S(2)}, u32[]{:S(2)}) collective-permute-start(bf16[128,2048]{1,0:T(8,128)(2,1)S(1)} %add_g1.1), channel_id=1, source_target_pairs={{0,2},{1,3},{2,6},{3,7},{6,4},{7,5},{4,0},{5,1},{8,10},{9,11},{10,... | collective-permute-start | bytes 1572872 | tf_op jit(solution)/shard_map/ga1/ppermute | solution.py:305
  112.6 18.5 %collective-permute-start.35 = (bf16[128,2048]{1,0:T(8,128)(2,1)S(1)}, bf16[128,2048]{1,0:T(8,128)(2,1)S(1)}, u32[]{:S(2)}, u32[]{:S(2)}) collective-permute-start(bf16[128,2048]{1,0:T(8,128)(2,1)S(1)} %add_m3.1), channel_id=1, source_target_pairs={{0,2},{1,3},{2,6},{3,7},{6,4},{7,5},{4,0},{5,1},{8,10},{9,11},{10,... | collective-permute-start | bytes 1572872 | tf_op jit(solution)/shard_map/m3/ppermute | solution.py:305
  120.0 14.1 %collective-permute-start.32 = (bf16[128,2048]{1,0:T(8,128)(2,1)S(1)}, bf16[128,2048]{1,0:T(8,128)(2,1)S(1)}, u32[]{:S(2)}, u32[]{:S(2)}) collective-permute-start(bf16[128,2048]{1,0:T(8,128)(2,1)S(1)} %get-tuple-element.356), channel_id=1, source_target_pairs={{0,1},{1,0},{2,3},{3,2},{4,5},{5,4},{6,7},{7,6},{8,9},{9,8},{10,11... | collective-permute-start | bytes 1572872 | tf_op jit(solution)/shard_map/r3/ppermute | solution.py:309
  120.1 21.2 %collective-permute-start.31 = (bf16[128,2048]{1,0:T(8,128)(2,1)S(1)}, bf16[128,2048]{1,0:T(8,128)(2,1)S(1)}, u32[]{:S(2)}, u32[]{:S(2)}) collective-permute-start(bf16[128,2048]{1,0:T(8,128)(2,1)S(1)} %add_g2.1), channel_id=1, source_target_pairs={{0,2},{1,3},{2,6},{3,7},{6,4},{7,5},{4,0},{5,1},{8,10},{9,11},{10,... | collective-permute-start | bytes 1572872 | tf_op jit(solution)/shard_map/ga2/ppermute | solution.py:305
  132.7 25.2 %collective-permute-start.39 = (bf16[3,704,256]{2,1,0:T(8,128)(2,1)S(1)}, bf16[3,704,256]{2,1,0:T(8,128)(2,1)S(1)}, u32[]{:S(2)}, u32[]{:S(2)}) collective-permute-start(bf16[3,704,256]{2,1,0:T(8,128)(2,1)S(1)} %get-tuple-element.395), channel_id=1, source_target_pairs={{0,8},{8,0},{16,24},{24,16},{1,9},{9,1},{17,25},{25,17},{2,10},{10... | collective-permute-start | bytes 3244040 | tf_op jit(solution)/shard_map/last/ppermute | solution.py:313
  133.3 25.0 %collective-permute-start.38 = (bf16[3,704,256]{2,1,0:T(8,128)(2,1)S(1)}, bf16[3,704,256]{2,1,0:T(8,128)(2,1)S(1)}, u32[]{:S(2)}, u32[]{:S(2)}) collective-permute-start(bf16[3,704,256]{2,1,0:T(8,128)(2,1)S(1)} %get-tuple-element.393), channel_id=1, source_target_pairs={{0,16},{8,24},{16,0},{24,8},{1,17},{9,25},{17,1},{25,9},{2,18},{10... | collective-permute-start | bytes 3244040 | tf_op jit(solution)/shard_map/last/ppermute | solution.py:313
  141.6 15.2 %collective-permute-start.36 = (bf16[128,2048]{1,0:T(8,128)(2,1)S(1)}, bf16[128,2048]{1,0:T(8,128)(2,1)S(1)}, u32[]{:S(2)}, u32[]{:S(2)}) collective-permute-start(bf16[128,2048]{1,0:T(8,128)(2,1)S(1)} %add_convert_fusion.1), channel_id=1, source_target_pairs={{0,2},{1,3},{2,6},{3,7},{6,4},{7,5},{4,0},{5,1},{8,10},{9,11},{10,... | collective-permute-start | bytes 1572872 | tf_op jit(solution)/shard_map/ga3/ppermute | solution.py:305
  (27 other events, 118.3 us)

commit v5 on v4

--- a/solution.py
+++ b/solution.py
@@ -207,17 +207,22 @@
     part_s[:, width // 2 :] = whole[:, width:]
 
 
-def early_kernel(offs, *refs):
-    hids, dys, parts, (out_a, out_b, dy, gates, held, left, right) = refs[:4], refs[4:7], refs[7:-7], refs[-7:]
+def ahead_kernel(*refs):
+    hids, dys, (total, left, right) = refs[:3], refs[3:6], refs[6:]
+    stack(hids, left)
+    stack(dys, right)
+    total[...] = tn(left[...], right[...])
+
+
+def early_kernel(offs, ahead, hid, *refs):
+    parts, (out_a, out_b, dy, gates, held) = refs[:-5], refs[-5:]
     stack(parts, held)
     half = dy.shape[1]
     gate = gate_column(offs[8], held[:, half:])
     gates[...] = jnp.broadcast_to(gate, gates.shape)
     dy[...] = (held[:, :half].astype(F32) * gate).astype(BF16)
-    stack(hids, left)
-    stack((*dys, dy), right)
-    out_a[0, :, :] = tn(left[...], right[:, : half // 2]).astype(BF16)
-    out_b[0, :, :] = tn(left[...], right[:, half // 2 :]).astype(BF16)
+    out_a[0, :, :] = (ahead[:, : half // 2] + tn(hid[...], dy[:, : half // 2])).astype(BF16)
+    out_b[0, :, :] = (ahead[:, half // 2 :] + tn(hid[...], dy[:, half // 2 :])).astype(BF16)
 
 
 def out_kernel(hid, down, gates, out_m, out_o):
@@ -416,8 +421,8 @@
             "early",
             early_kernel,
             [((1, ff, half // 2), BF16)] * 2 + [((2 * n, half), BF16), ((2 * n, 128), F32)],
-            [offs, *hids, *dys_s, *parts],
-            [((2 * n, half + 128), BF16), ((8 * n, ff), BF16), ((8 * n, half), BF16)],
+            [offs, ahead, f3[0], *parts],
+            [((2 * n, half + 128), BF16)],
             smem=1,
         )
 
@@ -463,15 +468,21 @@
     f2 = forward(2, t2, p2)
     b2 = backward(2, f2, c2, *q2)
     o2 = twin(b2[1], "o2")
-    t3, o1, f2[0], b2[0] = order.point(t3, o1, f2[0], b2[0])
+    ahead = launch(
+        "ahead",
+        ahead_kernel,
+        [((ff, half), F32)],
+        [f0[0], f1[0], f2[0], b0[4], b1[4], b2[4]],
+        [((6 * n, ff), BF16), ((6 * n, half), BF16)],
+    )[0]
+    t3, o1, ahead, f2[0], b2[0] = order.point(t3, o1, ahead, f2[0], b2[0])
     c3k = ring(c2k, "c3k")
     p3 = twins(t3, "p3")
+    f3 = forward(3, t3, *p3)
+    c3s, o2, *f3 = order.point(c3s, o2, *f3)
     m = ring(sums("add_m1", b1[0], o1), "m1")
-    c3s, o2 = order.point(c3s, o2)
     q3s = twins(c3s, "q3s")
-    f3 = forward(3, t3, *p3)
     hids, facs_g, facs_u, rows_s, rows_k = ([f[at] for f in (f0, f1, f2, f3)] for at in range(5))
-    dys_s = [b[4] for b in (b0, b1, b2)]
     *sent, dy3, gates3 = early(c3s, *q3s)
     dy3, *sent = order.point(dy3, *sent)
     down_came = flips(sent, (1, 2), "d1")
@@ -487,15 +498,16 @@
     m, d_gates[2], r1 = order.point(m, d_gates[2], r1)
     m = ring(sums("add_m2", m, outs_m[2], o2), "m2")
     r1, o3 = twin(r1, "r1"), twin(outs_o[3], "o3")
-    r1, o3, d_gates[0], *down_came = order.point(r1, o3, d_gates[0], *down_came)
+    r1, o3, d_gates[0] = order.point(r1, o3, d_gates[0])
+    m2, r2 = row_grads("rows_2", 2)
+    r2, d_gates[0], *down_came = order.point(r2, d_gates[0], *down_came)
     both_came = flips(sent, (1, 2), "gu1")
     g = ring(sums("add_g1", m1, r1), "ga1")
     o0 = twin(outs_o[0], "o0")
-    m2, r2 = row_grads("rows_2", 2)
     m3, r3 = row_grads("rows_3", 3)
     m0, r0 = row_grads("rows_0", 0)
     own = grads("kept_k", ((0, 2), (1, 2), (3, 4)), d_gates, d_ups, rows_k, hids, dys_k)
-    m, o0, m2, r2, m3, r3, m0, r0, *own = order.point(m, o0, m2, r2, m3, r3, m0, r0, *own)
+    m, o0, m3, r3, m0, r0, *own = order.point(m, o0, m3, r3, m0, r0, *own)
     m = ring(sums("add_m3", m, outs_m[3], o3), "m3")
     r2 = twin(r2, "r2")
     g, r2 = order.point(g, r2)

time: 161 us -> 159 us (0.988)
  starting transfers between devices: 37.4 us -> 35.6 us
    ppermute x13, waiting for transfers between devices: 61.1 us -> 57.6 us  [step(): lax.ppermute(value, 'expert', [(2 * at + core, 2 * follow[at] + core) for...]
    ppermute x6, waiting for transfers between devices: 4.51 us -> 6.79 us  [flip(): return lax.ppermute(value, 'dp', [(at, at ^ mask) for at in range(4)])]
    pallas_call x26 -> x27, Pallas kernels: 46.1 us -> 46.3 us  [call(): pl.pallas_call(kernel, name=name, out_shape=[jax.ShapeDtypeStruct(shape,...]
  transfers between devices with their start and end apart: 40 -> 40, of which waited for: 13 -> 18; matrix products, arithmetic and copies ran while one was open for 2% -> 2% of each run, Pallas kernels for 27% -> 28%
where the time goes in v5:
time: 159 us
  waiting for transfers between devices  65.5 us (41%)
  Pallas kernels  46.3 us (29%)
  starting transfers between devices  35.6 us (22%)
  local copies, waits for them, and re-layouts  9.1 us (6%)
    ppermute x13, waiting for transfers between devices, step(): lax.ppermute(value, 'expert', [(2 * at + core, 2 * follow[at] + core) for...  57.6 us
    pallas_call x27, Pallas kernels, call(): pl.pallas_call(kernel, name=name, out_shape=[jax.ShapeDtypeStruct(shape,...  46.3 us
    ppermute x13, starting transfers between devices, step(): lax.ppermute(value, 'expert', [(2 * at + core, 2 * follow[at] + core) for...  25.6 us
    unnamed x23, local copies, waits for them, and re-layouts  8.11 us
    ppermute x6, waiting for transfers between devices, flip(): return lax.ppermute(value, 'dp', [(at, at ^ mask) for at in range(4)])  6.79 us
    ppermute x6, starting transfers between devices, flip(): return lax.ppermute(value, 'dp', [(at, at ^ mask) for at in range(4)])  6.25 us
    ppermute x21, starting transfers between devices, swap(): lax.ppermute(value, 'expert', [(at, at ^ 1) for at in range(n_expert)])  3.73 us
  transfers between devices with their start and end apart: 40, of which 18 were waited for; matrix products, arithmetic and copies ran while one was open for 2% of the time, Pallas kernels for 28%

profile of v5, /device:TPU:0, one launch (start us, length us, event | category | flops | bytes accessed | tf_op | source)
XLA Modules:
  0.0 158.9 jit_solution(1314070774567396196)
XLA Ops:
  0.6 3.1 %collective-permute-start = (bf16[128,2048]{1,0:T(8,128)(2,1)}, bf16[128,2048]{1,0:T(8,128)(2,1)}, u32[]{:S(2)}, u32[]{:S(2)}) collective-permute-start(bf16[128,2048]{1,0:T(8,128)(2,1)} %refs_0_), channel_id=1, source_target_pairs={{0,2},{1,3},{2,6},{3,7},{6,4},{7,5},{4,0},{5,1},{8,10},{9,11},{10,... | collective-permute-start | bytes 1572872 | tf_op jit(solution)/shard_map/t1/ppermute | solution.py:310
  6.8 2.6 %collective-permute-start.2 = (bf16[128,2176]{1,0:T(8,128)(2,1)S(1)}, bf16[128,2176]{1,0:T(8,128)(2,1)S(1)}, u32[]{:S(2)}, u32[]{:S(2)}) collective-permute-start(bf16[128,2176]{1,0:T(8,128)(2,1)S(1)} %pack.1.refs_0_), channel_id=1, source_target_pairs={{0,2},{1,3},{2,6},{3,7},{6,4},{7,5},{4,0},{5,1},{8,10},{9,11},{10,... | collective-permute-start | bytes 1671176 | tf_op jit(solution)/shard_map/c1/ppermute | solution.py:310
  9.5 8.3 %collective-permute-done.refs_0_ = bf16[128,2048]{1,0:T(8,128)(2,1)} collective-permute-done((bf16[128,2048]{1,0:T(8,128)(2,1)}, bf16[128,2048]{1,0:T(8,128)(2,1)}, u32[]{:S(2)}, u32[]{:S(2)}) %collective-permute-start) | collective-permute-done | bytes 524320 | tf_op jit(solution)/shard_map/t1/ppermute | solution.py:310
  20.0 9.7 %collective-permute-done.2.refs_0_ = bf16[128,2176]{1,0:T(8,128)(2,1)S(1)} collective-permute-done((bf16[128,2176]{1,0:T(8,128)(2,1)S(1)}, bf16[128,2176]{1,0:T(8,128)(2,1)S(1)}, u32[]{:S(2)}, u32[]{:S(2)}) %collective-permute-start.2) | collective-permute-done | bytes 557088 | tf_op jit(solution)/shard_map/c1/ppermute | solution.py:310
  31.7 1.8 %copy-done = bf16[1,2048,704]{1,2,0:T(8,128)(2,1)S(1)} copy-done((bf16[1,2048,704]{1,2,0:T(8,128)(2,1)S(1)}, bf16[1,2048,704]{1,2,0:T(8,128)(2,1)}, u32[]{:S(2)}) %copy-start) | copy-done | bytes 2883608
  36.3 3.2 %forward_1.1 = (bf16[256,704]{1,0:T(8,128)(2,1)S(1)}, f32[256,704]{1,0:T(8,128)S(1)}, f32[256,704]{1,0:T(8,128)S(1)}, bf16[256,1024]{1,0:T(8,128)(2,1)S(1)}, bf16[256,1024]{1,0:T(8,128)(2,1)S(1)}) custom-call(s32[9]{0:T(128)S(1)} %stack.39.offs, bf16[128,2048]{1,0:T(8,128)(2,1)} %collective-permute-done.refs_0_, bf16[128,2048]{1,0:T(8,128)(2,1)S(1)} %copy-done.10, ...), custom_call_target="tpu_custom_call" | custom-call | flops 1 | bytes 1 | tf_op jit(solution)/shard_map/forward_1/pallas_call | solution.py:129
  39.6 2.6 %forward_0.1 = (bf16[256,704]{1,0:T(8,128)(2,1)S(1)}, f32[256,704]{1,0:T(8,128)S(1)}, f32[256,704]{1,0:T(8,128)S(1)}, bf16[256,1024]{1,0:T(8,128)(2,1)S(1)}, bf16[256,1024]{1,0:T(8,128)(2,1)S(1)}) custom-call(s32[9]{0:T(128)S(1)} %stack.39.offs, bf16[128,2048]{1,0:T(8,128)(2,1)S(1)} %copy-done.6, bf16[128,2048]{1,0:T(8,128)(2,1)S(1)} %copy-done.8, ...), custom_call_target="tpu_custom_call" | custom-call | flops 1 | bytes 1 | tf_op jit(solution)/shard_map/forward_0/pallas_call | solution.py:129
  42.5 3.4 %collective-permute-start.9 = (bf16[128,2048]{1,0:T(8,128)(2,1)S(1)}, bf16[128,2048]{1,0:T(8,128)(2,1)S(1)}, u32[]{:S(2)}, u32[]{:S(2)}) collective-permute-start(bf16[128,2048]{1,0:T(8,128)(2,1)S(1)} %collective-permute-done.1.refs_0_), channel_id=1, source_target_pairs={{0,2},{1,3},{2,6},{3,7},{6,4},{7,5},{4,0},{5,1},{8,10},{9,11},{10,... | collective-permute-start | bytes 1572872 | tf_op jit(solution)/shard_map/t3/ppermute | solution.py:310
  45.9 2.9 %backward_0.1 = (bf16[128,2048]{1,0:T(8,128)(2,1)S(1)}, bf16[128,2048]{1,0:T(8,128)(2,1)S(1)}, bf16[256,704]{1,0:T(8,128)(2,1)S(1)}, bf16[256,704]{1,0:T(8,128)(...) custom-call(s32[9]{0:T(128)S(1)} %stack.39.offs, ...), custom_call_target="tpu_custom_call" | custom-call | flops 1 | bytes 1 | tf_op jit(solution)/shard_map/backward_0/pallas_call | solution.py:129
  48.8 2.9 %backward_1.1 = (bf16[128,2048]{1,0:T(8,128)(2,1)S(1)}, bf16[128,2048]{1,0:T(8,128)(2,1)S(1)}, bf16[256,704]{1,0:T(8,128)(2,1)S(1)}, bf16[256,704]{1,0:T(8,128)(...) custom-call(s32[9]{0:T(128)S(1)} %stack.39.offs, ...), custom_call_target="tpu_custom_call" | custom-call | flops 1 | bytes 1 | tf_op jit(solution)/shard_map/backward_1/pallas_call | solution.py:129
  55.4 2.6 %forward_2.1 = (bf16[256,704]{1,0:T(8,128)(2,1)S(1)}, f32[256,704]{1,0:T(8,128)S(1)}, f32[256,704]{1,0:T(8,128)S(1)}, bf16[256,1024]{1,0:T(8,128)(2,1)S(1)}, bf16[256,1024]{1,0:T(8,128)(2,1)S(1)}) custom-call(s32[9]{0:T(128)S(1)} %stack.39.offs, bf16[128,2048]{1,0:T(8,128)(2,1)S(1)} %collective-permute-done.1.refs_0_, ...), custom_call_target="tpu_custom_call" | custom-call | flops 1 | bytes 1 | tf_op jit(solution)/shard_map/forward_2/pallas_call | solution.py:129
  58.0 2.9 %backward_2.1 = (bf16[128,2048]{1,0:T(8,128)(2,1)S(1)}, bf16[128,2048]{1,0:T(8,128)(2,1)S(1)}, bf16[256,704]{1,0:T(8,128)(2,1)S(1)}, bf16[256,704]{1,0:T(8,128)(...) custom-call(s32[9]{0:T(128)S(1)} %stack.39.offs, ...), custom_call_target="tpu_custom_call" | custom-call | flops 1 | bytes 1 | tf_op jit(solution)/shard_map/backward_2/pallas_call | solution.py:129
  66.4 2.6 %forward_3.1 = (bf16[256,704]{1,0:T(8,128)(2,1)S(1)}, f32[256,704]{1,0:T(8,128)S(1)}, f32[256,704]{1,0:T(8,128)S(1)}, bf16[256,1024]{1,0:T(8,128)(2,1)S(1)}, bf16[256,1024]{1,0:T(8,128)(2,1)S(1)}) custom-call(s32[9]{0:T(128)S(1)} %stack.39.offs, bf16[128,2048]{1,0:T(8,128)(2,1)S(1)} %collective-permute-done.9.refs_0_, ...), custom_call_target="tpu_custom_call" | custom-call | flops 1 | bytes 1 | tf_op jit(solution)/shard_map/forward_3/pallas_call | solution.py:129
  82.5 3.2 %both_s.1 = (bf16[2,704,512]{2,1,0:T(8,128)(2,1)S(1)}, bf16[2,704,512]{2,1,0:T(8,128)(2,1)S(1)}) custom-call(bf16[256,704]{1,0:T(8,128)(2,1)S(1)} %get-tuple-element.349.refs_0_, bf16[256,704]{1,0:T(8,128)(2,1)S(1)} %get-tuple-element.311.refs_1_.refs_0_, bf16[256,704]{1,0:T(8,128)(2,1)S(1)} %get-tuple-element.326.refs_2_.refs_0_, ...), custom_call_target="tpu_custom_call" | custom-call | flops 1 | bytes 1 | tf_op jit(solution)/shard_map/both_s/pallas_call | solution.py:129
  88.3 2.0 %collective-permute-start.28 = (bf16[128,2048]{1,0:T(8,128)(2,1)S(1)}, bf16[128,2048]{1,0:T(8,128)(2,1)S(1)}, u32[]{:S(2)}, u32[]{:S(2)}) collective-permute-start(bf16[128,2048]{1,0:T(8,128)(2,1)S(1)} %add_m2.1), channel_id=1, source_target_pairs={{0,2},{1,3},{2,6},{3,7},{6,4},{7,5},{4,0},{5,1},{8,10},{9,11},{10,... | collective-permute-start | bytes 1572872 | tf_op jit(solution)/shard_map/m2/ppermute | solution.py:310
  100.5 3.2 %collective-permute-start.27 = (bf16[128,2048]{1,0:T(8,128)(2,1)S(1)}, bf16[128,2048]{1,0:T(8,128)(2,1)S(1)}, u32[]{:S(2)}, u32[]{:S(2)}) collective-permute-start(bf16[128,2048]{1,0:T(8,128)(2,1)S(1)} %add_g1.1), channel_id=1, source_target_pairs={{0,2},{1,3},{2,6},{3,7},{6,4},{7,5},{4,0},{5,1},{8,10},{9,11},{10,... | collective-permute-start | bytes 1572872 | tf_op jit(solution)/shard_map/ga1/ppermute | solution.py:310
  103.6 4.8 %kept_k.1 = (bf16[3,704,512]{2,1,0:T(8,128)(2,1)S(1)}, bf16[3,704,512]{2,1,0:T(8,128)(2,1)S(1)}) custom-call(bf16[256,704]{1,0:T(8,128)(2,1)S(1)} %get-tuple-element.349.refs_0_, bf16[256,704]{1,0:T(8,128)(2,1)S(1)} %get-tuple-element.311.refs_1_.refs_0_, bf16[256,704]{1,0:T(8,128)(2,1)S(1)} %get-tuple-element.326.refs_2_.refs_0_, ...), custom_call_target="tpu_custom_call" | custom-call | flops 1 | bytes 1 | tf_op jit(solution)/shard_map/kept_k/pallas_call | solution.py:129
  109.0 7.5 %collective-permute-done.27.refs_0_ = bf16[128,2048]{1,0:T(8,128)(2,1)S(1)} collective-permute-done((bf16[128,2048]{1,0:T(8,128)(2,1)S(1)}, bf16[128,2048]{1,0:T(8,128)(2,1)S(1)}, u32[]{:S(2)}, u32[]{:S(2)}) %collective-permute-start.27) | collective-permute-done | bytes 524320 | tf_op jit(solution)/shard_map/ga1/ppermute | solution.py:310
  116.8 2.0 %collective-permute-start.31 = (bf16[128,2048]{1,0:T(8,128)(2,1)S(1)}, bf16[128,2048]{1,0:T(8,128)(2,1)S(1)}, u32[]{:S(2)}, u32[]{:S(2)}) collective-permute-start(bf16[128,2048]{1,0:T(8,128)(2,1)S(1)} %add_g2.1), channel_id=1, source_target_pairs={{0,2},{1,3},{2,6},{3,7},{6,4},{7,5},{4,0},{5,1},{8,10},{9,11},{10,... | collective-permute-start | bytes 1572872 | tf_op jit(solution)/shard_map/ga2/ppermute | solution.py:310
  118.8 9.0 %collective-permute-done.35.refs_0_ = bf16[128,2048]{1,0:T(8,128)(2,1)S(1)} collective-permute-done((bf16[128,2048]{1,0:T(8,128)(2,1)S(1)}, bf16[128,2048]{1,0:T(8,128)(2,1)S(1)}, u32[]{:S(2)}, u32[]{:S(2)}) %collective-permute-start.35) | collective-permute-done | bytes 524320 | tf_op jit(solution)/shard_map/m3/ppermute | solution.py:310
  132.0 6.0 %collective-permute-done.31 = bf16[128,2048]{1,0:T(8,128)(2,1)S(1)} collective-permute-done((bf16[128,2048]{1,0:T(8,128)(2,1)S(1)}, bf16[128,2048]{1,0:T(8,128)(2,1)S(1)}, u32[]{:S(2)}, u32[]{:S(2)}) %collective-permute-start.31) | collective-permute-done | bytes 524320 | tf_op jit(solution)/shard_map/ga2/ppermute | solution.py:310
  138.3 2.0 %collective-permute-start.36 = (bf16[128,2048]{1,0:T(8,128)(2,1)S(1)}, bf16[128,2048]{1,0:T(8,128)(2,1)S(1)}, u32[]{:S(2)}, u32[]{:S(2)}) collective-permute-start(bf16[128,2048]{1,0:T(8,128)(2,1)S(1)} %add_convert_fusion.1), channel_id=1, source_target_pairs={{0,2},{1,3},{2,6},{3,7},{6,4},{7,5},{4,0},{5,1},{8,10},{9,11},{10,... | collective-permute-start | bytes 1572872 | tf_op jit(solution)/shard_map/ga3/ppermute | solution.py:310
  141.2 12.2 %collective-permute-done.36 = bf16[128,2048]{1,0:T(8,128)(2,1)S(1)} collective-permute-done((bf16[128,2048]{1,0:T(8,128)(2,1)S(1)}, bf16[128,2048]{1,0:T(8,128)(2,1)S(1)}, u32[]{:S(2)}, u32[]{:S(2)}) %collective-permute-start.36) | collective-permute-done | bytes 524320 | tf_op jit(solution)/shard_map/ga3/ppermute | solution.py:310
  156.4 2.4 %finish.1 = (f32[704,512]{1,0:T(8,128)}, f32[704,512]{1,0:T(8,128)}, f32[704,512]{1,0:T(8,128)}) custom-call(f32[3,704,256]{2,1,0:T(8,128)S(1)} %get-tuple-element.413.near_a, f32[3,704,256]{2,1,0:T(8,128)S(1)} %get-tuple-element.414.near_b, bf16[3,704,256]{2,1,0:T(8,128)(2,1)S(1)} %collective-permute-done.38.last_a, ...), custom_call_target="tpu_custom_call" | custom-call | flops 1 | bytes 1 | tf_op jit(solution)/shard_map/finish/pallas_call | solution.py:129
  (114 shorter events, 55.1 us)
Async XLA Ops:
  0.6 17.2 %collective-permute-start = (bf16[128,2048]{1,0:T(8,128)(2,1)}, bf16[128,2048]{1,0:T(8,128)(2,1)}, u32[]{:S(2)}, u32[]{:S(2)}) collective-permute-start(bf16[128,2048]{1,0:T(8,128)(2,1)} %refs_0_), channel_id=1, source_target_pairs={{0,2},{1,3},{2,6},{3,7},{6,4},{7,5},{4,0},{5,1},{8,10},{9,11},{10,... | collective-permute-start | bytes 1572872 | tf_op jit(solution)/shard_map/t1/ppermute | solution.py:310
  6.8 22.8 %collective-permute-start.2 = (bf16[128,2176]{1,0:T(8,128)(2,1)S(1)}, bf16[128,2176]{1,0:T(8,128)(2,1)S(1)}, u32[]{:S(2)}, u32[]{:S(2)}) collective-permute-start(bf16[128,2176]{1,0:T(8,128)(2,1)S(1)} %pack.1.refs_0_), channel_id=1, source_target_pairs={{0,2},{1,3},{2,6},{3,7},{6,4},{7,5},{4,0},{5,1},{8,10},{9,11},{10,... | collective-permute-start | bytes 1671176 | tf_op jit(solution)/shard_map/c1/ppermute | solution.py:310
  17.8 11.8 %collective-permute-start.4 = (bf16[128,2048]{1,0:T(8,128)(2,1)}, bf16[128,2048]{1,0:T(8,128)(2,1)S(1)}, u32[]{:S(2)}, u32[]{:S(2)}) collective-permute-start(bf16[128,2048]{1,0:T(8,128)(2,1)} %collective-permute-done.refs_0_), channel_id=1, source_target_pairs={{0,1},{1,0},{2,3},{3,2},{4,5},{5,4},{6,7},{7,6},{8,9},{9,8},{10,11... | collective-permute-start | bytes 1572872 | tf_op jit(solution)/shard_map/p1/ppermute | solution.py:314
  17.8 24.4 %collective-permute-start.1 = (bf16[128,2048]{1,0:T(8,128)(2,1)}, bf16[128,2048]{1,0:T(8,128)(2,1)S(1)}, u32[]{:S(2)}, u32[]{:S(2)}) collective-permute-start(bf16[128,2048]{1,0:T(8,128)(2,1)} %collective-permute-done.refs_0_), channel_id=1, source_target_pairs={{0,2},{1,3},{2,6},{3,7},{6,4},{7,5},{4,0},{5,1},{8,10},{9,11},{10,... | collective-permute-start | bytes 1572872 | tf_op jit(solution)/shard_map/t2/ppermute | solution.py:310
  18.9 27.0 %collective-permute-start.6 = (bf16[128,2176]{1,0:T(8,128)(2,1)S(1)}, bf16[128,2176]{1,0:T(8,128)(2,1)S(1)}, u32[]{:S(2)}, u32[]{:S(2)}) collective-permute-start(bf16[128,2176]{1,0:T(8,128)(2,1)S(1)} %pack.1.refs_0_), channel_id=1, source_target_pairs={{0,1},{1,0},{2,3},{3,2},{4,5},{5,4},{6,7},{7,6},{8,9},{9,8},{10,11... | collective-permute-start | bytes 1671176 | tf_op jit(solution)/shard_map/q0/ppermute | solution.py:314
  30.4 18.4 %collective-permute-start.5 = (bf16[128,2176]{1,0:T(8,128)(2,1)S(1)}, bf16[128,2176]{1,0:T(8,128)(2,1)S(1)}, u32[]{:S(2)}, u32[]{:S(2)}) collective-permute-start(bf16[128,2176]{1,0:T(8,128)(2,1)S(1)} %collective-permute-done.2.refs_0_), channel_id=1, source_target_pairs={{0,1},{1,0},{2,3},{3,2},{4,5},{5,4},{6,7},{7,6},{8,9},{9,8},{10,11... | collective-permute-start | bytes 1671176 | tf_op jit(solution)/shard_map/q1/ppermute | solution.py:314
  30.4 22.4 %collective-permute-start.7 = (bf16[128,2176]{1,0:T(8,128)(2,1)S(1)}, bf16[128,2176]{1,0:T(8,128)(2,1)S(1)}, u32[]{:S(2)}, u32[]{:S(2)}) collective-permute-start(bf16[128,2176]{1,0:T(8,128)(2,1)S(1)} %collective-permute-done.2.refs_0_), channel_id=1, source_target_pairs={{0,2},{1,3},{2,6},{3,7},{6,4},{7,5},{4,0},{5,1},{8,10},{9,11},{10,... | collective-permute-start | bytes 1671176 | tf_op jit(solution)/shard_map/c2/ppermute | solution.py:310
  42.5 21.5 %collective-permute-start.9 = (bf16[128,2048]{1,0:T(8,128)(2,1)S(1)}, bf16[128,2048]{1,0:T(8,128)(2,1)S(1)}, u32[]{:S(2)}, u32[]{:S(2)}) collective-permute-start(bf16[128,2048]{1,0:T(8,128)(2,1)S(1)} %collective-permute-done.1.refs_0_), channel_id=1, source_target_pairs={{0,2},{1,3},{2,6},{3,7},{6,4},{7,5},{4,0},{5,1},{8,10},{9,11},{10,... | collective-permute-start | bytes 1572872 | tf_op jit(solution)/shard_map/t3/ppermute | solution.py:310
  51.7 12.3 %collective-permute-start.10 = (bf16[128,2048]{1,0:T(8,128)(2,1)S(1)}, bf16[128,2048]{1,0:T(8,128)(2,1)S(1)}, u32[]{:S(2)}, u32[]{:S(2)}) collective-permute-start(bf16[128,2048]{1,0:T(8,128)(2,1)S(1)} %get-tuple-element.247), channel_id=1, source_target_pairs={{0,1},{1,0},{2,3},{3,2},{4,5},{5,4},{6,7},{7,6},{8,9},{9,8},{10,11... | collective-permute-start | bytes 1572872 | tf_op jit(solution)/shard_map/o1/ppermute | solution.py:314
  54.0 16.3 %collective-permute-start.14 = (bf16[128,1152]{1,0:T(8,128)(2,1)S(1)}, bf16[128,1152]{1,0:T(8,128)(2,1)S(1)}, u32[]{:S(2)}, u32[]{:S(2)}) collective-permute-start(bf16[128,1152]{1,0:T(8,128)(2,1)S(1)} %get-tuple-element.265), channel_id=1, source_target_pairs={{0,2},{1,3},{2,6},{3,7},{6,4},{7,5},{4,0},{5,1},{8,10},{9,11},{10,... | collective-permute-start | bytes 884744 | tf_op jit(solution)/shard_map/c3s/ppermute | solution.py:310
  70.5 17.1 %collective-permute-start.22 = (bf16[128,2048]{1,0:T(8,128)(2,1)S(1)}, bf16[128,2048]{1,0:T(8,128)(2,1)S(1)}, u32[]{:S(2)}, u32[]{:S(2)}) collective-permute-start(bf16[128,2048]{1,0:T(8,128)(2,1)S(1)} %add_m1.1), channel_id=1, source_target_pairs={{0,2},{1,3},{2,6},{3,7},{6,4},{7,5},{4,0},{5,1},{8,10},{9,11},{10,... | collective-permute-start | bytes 1572872 | tf_op jit(solution)/shard_map/m1/ppermute | solution.py:310
  76.0 17.5 %collective-permute-start.26 = (bf16[1,704,512]{2,1,0:T(8,128)(2,1)S(1)}, bf16[1,704,512]{2,1,0:T(8,128)(2,1)S(1)}, u32[]{:S(2)}, u32[]{:S(2)}) collective-permute-start(bf16[1,704,512]{2,1,0:T(8,128)(2,1)S(1)} %get-tuple-element.332), channel_id=1, source_target_pairs={{0,16},{8,24},{16,0},{24,8},{1,17},{9,25},{17,1},{25,9},{2,18},{10... | collective-permute-start | bytes 2162696 | tf_op jit(solution)/shard_map/d1/ppermute | solution.py:318
  77.6 17.1 %collective-permute-start.25 = (bf16[1,704,512]{2,1,0:T(8,128)(2,1)S(1)}, bf16[1,704,512]{2,1,0:T(8,128)(2,1)S(1)}, u32[]{:S(2)}, u32[]{:S(2)}) collective-permute-start(bf16[1,704,512]{2,1,0:T(8,128)(2,1)S(1)} %get-tuple-element.330), channel_id=1, source_target_pairs={{0,8},{8,0},{16,24},{24,16},{1,9},{9,1},{17,25},{25,17},{2,10},{10... | collective-permute-start | bytes 2162696 | tf_op jit(solution)/shard_map/d1/ppermute | solution.py:318
  88.3 20.1 %collective-permute-start.28 = (bf16[128,2048]{1,0:T(8,128)(2,1)S(1)}, bf16[128,2048]{1,0:T(8,128)(2,1)S(1)}, u32[]{:S(2)}, u32[]{:S(2)}) collective-permute-start(bf16[128,2048]{1,0:T(8,128)(2,1)S(1)} %add_m2.1), channel_id=1, source_target_pairs={{0,2},{1,3},{2,6},{3,7},{6,4},{7,5},{4,0},{5,1},{8,10},{9,11},{10,... | collective-permute-start | bytes 1572872 | tf_op jit(solution)/shard_map/m2/ppermute | solution.py:310
  94.7 13.7 %collective-permute-start.29 = (bf16[128,2048]{1,0:T(8,128)(2,1)S(1)}, bf16[128,2048]{1,0:T(8,128)(2,1)S(1)}, u32[]{:S(2)}, u32[]{:S(2)}) collective-permute-start(bf16[128,2048]{1,0:T(8,128)(2,1)S(1)} %get-tuple-element.344), channel_id=1, source_target_pairs={{0,1},{1,0},{2,3},{3,2},{4,5},{5,4},{6,7},{7,6},{8,9},{9,8},{10,11... | collective-permute-start | bytes 1572872 | tf_op jit(solution)/shard_map/o0/ppermute | solution.py:314
  94.7 34.0 %collective-permute-start.33 = (bf16[2,704,512]{2,1,0:T(8,128)(2,1)S(1)}, bf16[2,704,512]{2,1,0:T(8,128)(2,1)S(1)}, u32[]{:S(2)}, u32[]{:S(2)}) collective-permute-start(bf16[2,704,512]{2,1,0:T(8,128)(2,1)S(1)} %get-tuple-element.374), channel_id=1, source_target_pairs={{0,8},{8,0},{16,24},{24,16},{1,9},{9,1},{17,25},{25,17},{2,10},{10... | collective-permute-start | bytes 4325384 | tf_op jit(solution)/shard_map/gu1/ppermute | solution.py:318
  96.3 33.7 %collective-permute-start.34 = (bf16[2,704,512]{2,1,0:T(8,128)(2,1)S(1)}, bf16[2,704,512]{2,1,0:T(8,128)(2,1)S(1)}, u32[]{:S(2)}, u32[]{:S(2)}) collective-permute-start(bf16[2,704,512]{2,1,0:T(8,128)(2,1)S(1)} %get-tuple-element.376), channel_id=1, source_target_pairs={{0,16},{8,24},{16,0},{24,8},{1,17},{9,25},{17,1},{25,9},{2,18},{10... | collective-permute-start | bytes 4325384 | tf_op jit(solution)/shard_map/gu1/ppermute | solution.py:318
  100.5 16.0 %collective-permute-start.27 = (bf16[128,2048]{1,0:T(8,128)(2,1)S(1)}, bf16[128,2048]{1,0:T(8,128)(2,1)S(1)}, u32[]{:S(2)}, u32[]{:S(2)}) collective-permute-start(bf16[128,2048]{1,0:T(8,128)(2,1)S(1)} %add_g1.1), channel_id=1, source_target_pairs={{0,2},{1,3},{2,6},{3,7},{6,4},{7,5},{4,0},{5,1},{8,10},{9,11},{10,... | collective-permute-start | bytes 1572872 | tf_op jit(solution)/shard_map/ga1/ppermute | solution.py:310
  108.7 19.0 %collective-permute-start.35 = (bf16[128,2048]{1,0:T(8,128)(2,1)S(1)}, bf16[128,2048]{1,0:T(8,128)(2,1)S(1)}, u32[]{:S(2)}, u32[]{:S(2)}) collective-permute-start(bf16[128,2048]{1,0:T(8,128)(2,1)S(1)} %add_m3.1), channel_id=1, source_target_pairs={{0,2},{1,3},{2,6},{3,7},{6,4},{7,5},{4,0},{5,1},{8,10},{9,11},{10,... | collective-permute-start | bytes 1572872 | tf_op jit(solution)/shard_map/m3/ppermute | solution.py:310
  116.7 15.3 %collective-permute-start.32 = (bf16[128,2048]{1,0:T(8,128)(2,1)S(1)}, bf16[128,2048]{1,0:T(8,128)(2,1)S(1)}, u32[]{:S(2)}, u32[]{:S(2)}) collective-permute-start(bf16[128,2048]{1,0:T(8,128)(2,1)S(1)} %get-tuple-element.372), channel_id=1, source_target_pairs={{0,1},{1,0},{2,3},{3,2},{4,5},{5,4},{6,7},{7,6},{8,9},{9,8},{10,11... | collective-permute-start | bytes 1572872 | tf_op jit(solution)/shard_map/r3/ppermute | solution.py:314
  116.8 21.2 %collective-permute-start.31 = (bf16[128,2048]{1,0:T(8,128)(2,1)S(1)}, bf16[128,2048]{1,0:T(8,128)(2,1)S(1)}, u32[]{:S(2)}, u32[]{:S(2)}) collective-permute-start(bf16[128,2048]{1,0:T(8,128)(2,1)S(1)} %add_g2.1), channel_id=1, source_target_pairs={{0,2},{1,3},{2,6},{3,7},{6,4},{7,5},{4,0},{5,1},{8,10},{9,11},{10,... | collective-permute-start | bytes 1572872 | tf_op jit(solution)/shard_map/ga2/ppermute | solution.py:310
  130.9 25.2 %collective-permute-start.39 = (bf16[3,704,256]{2,1,0:T(8,128)(2,1)S(1)}, bf16[3,704,256]{2,1,0:T(8,128)(2,1)S(1)}, u32[]{:S(2)}, u32[]{:S(2)}) collective-permute-start(bf16[3,704,256]{2,1,0:T(8,128)(2,1)S(1)} %get-tuple-element.411), channel_id=1, source_target_pairs={{0,8},{8,0},{16,24},{24,16},{1,9},{9,1},{17,25},{25,17},{2,10},{10... | collective-permute-start | bytes 3244040 | tf_op jit(solution)/shard_map/last/ppermute | solution.py:318
  131.5 25.0 %collective-permute-start.38 = (bf16[3,704,256]{2,1,0:T(8,128)(2,1)S(1)}, bf16[3,704,256]{2,1,0:T(8,128)(2,1)S(1)}, u32[]{:S(2)}, u32[]{:S(2)}) collective-permute-start(bf16[3,704,256]{2,1,0:T(8,128)(2,1)S(1)} %get-tuple-element.409), channel_id=1, source_target_pairs={{0,16},{8,24},{16,0},{24,8},{1,17},{9,25},{17,1},{25,9},{2,18},{10... | collective-permute-start | bytes 3244040 | tf_op jit(solution)/shard_map/last/ppermute | solution.py:318
  138.3 15.2 %collective-permute-start.36 = (bf16[128,2048]{1,0:T(8,128)(2,1)S(1)}, bf16[128,2048]{1,0:T(8,128)(2,1)S(1)}, u32[]{:S(2)}, u32[]{:S(2)}) collective-permute-start(bf16[128,2048]{1,0:T(8,128)(2,1)S(1)} %add_convert_fusion.1), channel_id=1, source_target_pairs={{0,2},{1,3},{2,6},{3,7},{6,4},{7,5},{4,0},{5,1},{8,10},{9,11},{10,... | collective-permute-start | bytes 1572872 | tf_op jit(solution)/shard_map/ga3/ppermute | solution.py:310
  (27 other events, 103.8 us)

commit v6 on v5

--- a/solution.py
+++ b/solution.py
@@ -271,16 +271,13 @@
         out_b[at, :, :] = tn(left[...], right[:, half:]).astype(BF16)
 
 
-def cross_kernel(came_a, came_b, down_a, down_b, own_a, own_b, far_a, far_b, near_a, near_b):
-    cut = far_a.shape[2]
-    for came, down, own, far, near in (
-        (came_a, down_a, own_a, far_a, near_a),
-        (came_b, down_b, own_b, far_b, near_b),
-    ):
+def cross_kernel(near, came_a, came_b, down_a, down_b, own_a, own_b, *outs):
+    cut = outs[0].shape[2]
+    part = slice(0, cut) if near else slice(cut, 2 * cut)
+    for came, down, own, out in ((came_a, down_a, own_a, outs[0]), (came_b, down_b, own_b, outs[1])):
         for at in range(3):
-            both = (down[0, :, :] if at == 2 else came[at, :, :]).astype(F32) + own[at, :, :].astype(F32)
-            near[at, :, :] = both[:, :cut]
-            far[at, :, :] = both[:, cut:].astype(BF16)
+            first = down[0, :, part] if at == 2 else came[at, :, part]
+            out[at, :, :] = (first.astype(F32) + own[at, :, part].astype(F32)).astype(out.dtype)
 
 
 def finish_kernel(near_a, near_b, last_a, last_b, *outs):
@@ -514,19 +511,16 @@
     g = ring(sums("add_g2", g, m2, r2), "ga2")
     r3 = twin(r3, "r3")
     both_came[0], both_came[1], m = order.point(*both_came, m)
-    *far, near_a, near_b = launch(
-        "cross",
-        cross_kernel,
-        [((3, ff, cut), BF16)] * 2 + [((3, ff, cut), F32)] * 2,
-        [*both_came, *down_came, *own],
-    )
+    parts = [*both_came, *down_came, *own]
+    far = launch("cross", partial(cross_kernel, False), [((3, ff, cut), BF16)] * 2, parts)
     far = order.point(*far)
     last = flips(far, (2, 1), "last")
+    near_a, near_b = launch("settle", partial(cross_kernel, True), [((3, ff, cut), F32)] * 2, parts)
     g, r3 = order.point(g, r3)
     g = ring(add(g, kept(m3, r3)).astype(BF16), "ga3")
     r0 = twin(r0, "r0")
     mixed = sums("add_m0", m, outs_m[0], o0)
-    g, r0, mixed = order.point(g, r0, mixed)
+    g, r0, mixed, near_a, near_b = order.point(g, r0, mixed, near_a, near_b)
     token_grad = add(g, kept(m0, r0)).astype(BF16)
     token_grad, *last = order.point(token_grad, *last)
     grad_gate, grad_up, grad_down = launch(

time: 159 us -> 159 us (level)
    pallas_call x27 -> x28, Pallas kernels: 46.3 us -> 46.4 us  [call(): pl.pallas_call(kernel, name=name, out_shape=[jax.ShapeDtypeStruct(shape,...]
where the time goes in v6:
time: 159 us; the launch traced here: 158 us
  waiting for transfers between devices  65 us (41%)
  Pallas kernels  46.4 us (29%)
  starting transfers between devices  35.6 us (22%)
  local copies, waits for them, and re-layouts  9.1 us (6%)
    ppermute x13, waiting for transfers between devices, step(): lax.ppermute(value, 'expert', [(2 * at + core, 2 * follow[at] + core) for...  57.6 us
    pallas_call x28, Pallas kernels, call(): pl.pallas_call(kernel, name=name, out_shape=[jax.ShapeDtypeStruct(shape,...  46.4 us
    ppermute x13, starting transfers between devices, step(): lax.ppermute(value, 'expert', [(2 * at + core, 2 * follow[at] + core) for...  25.6 us
    unnamed x23, local copies, waits for them, and re-layouts  8.11 us
    ppermute x6, waiting for transfers between devices, flip(): return lax.ppermute(value, 'dp', [(at, at ^ mask) for at in range(4)])  6.3 us
    ppermute x6, starting transfers between devices, flip(): return lax.ppermute(value, 'dp', [(at, at ^ mask) for at in range(4)])  6.24 us
    ppermute x21, starting transfers between devices, swap(): lax.ppermute(value, 'expert', [(at, at ^ 1) for at in range(n_expert)])  3.73 us
  transfers between devices with their start and end apart: 40, of which 18 were waited for; matrix products, arithmetic and copies ran while one was open for 2% of the time, Pallas kernels for 28%

profile of v6, /device:TPU:0, one launch (start us, length us, event | category | flops | bytes accessed | tf_op | source)
XLA Modules:
  0.0 158.5 jit_solution(14254329605196610081)
XLA Ops:
  0.6 3.1 %collective-permute-start = (bf16[128,2048]{1,0:T(8,128)(2,1)}, bf16[128,2048]{1,0:T(8,128)(2,1)}, u32[]{:S(2)}, u32[]{:S(2)}) collective-permute-start(bf16[128,2048]{1,0:T(8,128)(2,1)} %refs_0_), channel_id=1, source_target_pairs={{0,2},{1,3},{2,6},{3,7},{6,4},{7,5},{4,0},{5,1},{8,10},{9,11},{10,... | collective-permute-start | bytes 1572872 | tf_op jit(solution)/shard_map/t1/ppermute | solution.py:307
  6.8 2.6 %collective-permute-start.2 = (bf16[128,2176]{1,0:T(8,128)(2,1)S(1)}, bf16[128,2176]{1,0:T(8,128)(2,1)S(1)}, u32[]{:S(2)}, u32[]{:S(2)}) collective-permute-start(bf16[128,2176]{1,0:T(8,128)(2,1)S(1)} %pack.1.refs_0_), channel_id=1, source_target_pairs={{0,2},{1,3},{2,6},{3,7},{6,4},{7,5},{4,0},{5,1},{8,10},{9,11},{10,... | collective-permute-start | bytes 1671176 | tf_op jit(solution)/shard_map/c1/ppermute | solution.py:307
  9.5 8.3 %collective-permute-done.refs_0_ = bf16[128,2048]{1,0:T(8,128)(2,1)} collective-permute-done((bf16[128,2048]{1,0:T(8,128)(2,1)}, bf16[128,2048]{1,0:T(8,128)(2,1)}, u32[]{:S(2)}, u32[]{:S(2)}) %collective-permute-start) | collective-permute-done | bytes 524320 | tf_op jit(solution)/shard_map/t1/ppermute | solution.py:307
  20.0 9.7 %collective-permute-done.2.refs_0_ = bf16[128,2176]{1,0:T(8,128)(2,1)S(1)} collective-permute-done((bf16[128,2176]{1,0:T(8,128)(2,1)S(1)}, bf16[128,2176]{1,0:T(8,128)(2,1)S(1)}, u32[]{:S(2)}, u32[]{:S(2)}) %collective-permute-start.2) | collective-permute-done | bytes 557088 | tf_op jit(solution)/shard_map/c1/ppermute | solution.py:307
  36.3 3.2 %forward_1.1 = (bf16[256,704]{1,0:T(8,128)(2,1)S(1)}, f32[256,704]{1,0:T(8,128)S(1)}, f32[256,704]{1,0:T(8,128)S(1)}, bf16[256,1024]{1,0:T(8,128)(2,1)S(1)}, bf16[256,1024]{1,0:T(8,128)(2,1)S(1)}) custom-call(s32[9]{0:T(128)S(1)} %stack.39.offs, bf16[128,2048]{1,0:T(8,128)(2,1)} %collective-permute-done.refs_0_, bf16[128,2048]{1,0:T(8,128)(2,1)S(1)} %copy-done.10, ...), custom_call_target="tpu_custom_call" | custom-call | flops 1 | bytes 1 | tf_op jit(solution)/shard_map/forward_1/pallas_call | solution.py:129
  39.6 2.6 %forward_0.1 = (bf16[256,704]{1,0:T(8,128)(2,1)S(1)}, f32[256,704]{1,0:T(8,128)S(1)}, f32[256,704]{1,0:T(8,128)S(1)}, bf16[256,1024]{1,0:T(8,128)(2,1)S(1)}, bf16[256,1024]{1,0:T(8,128)(2,1)S(1)}) custom-call(s32[9]{0:T(128)S(1)} %stack.39.offs, bf16[128,2048]{1,0:T(8,128)(2,1)S(1)} %copy-done.6, bf16[128,2048]{1,0:T(8,128)(2,1)S(1)} %copy-done.8, ...), custom_call_target="tpu_custom_call" | custom-call | flops 1 | bytes 1 | tf_op jit(solution)/shard_map/forward_0/pallas_call | solution.py:129
  42.5 3.4 %collective-permute-start.9 = (bf16[128,2048]{1,0:T(8,128)(2,1)S(1)}, bf16[128,2048]{1,0:T(8,128)(2,1)S(1)}, u32[]{:S(2)}, u32[]{:S(2)}) collective-permute-start(bf16[128,2048]{1,0:T(8,128)(2,1)S(1)} %collective-permute-done.1.refs_0_), channel_id=1, source_target_pairs={{0,2},{1,3},{2,6},{3,7},{6,4},{7,5},{4,0},{5,1},{8,10},{9,11},{10,... | collective-permute-start | bytes 1572872 | tf_op jit(solution)/shard_map/t3/ppermute | solution.py:307
  45.9 2.9 %backward_0.1 = (bf16[128,2048]{1,0:T(8,128)(2,1)S(1)}, bf16[128,2048]{1,0:T(8,128)(2,1)S(1)}, bf16[256,704]{1,0:T(8,128)(2,1)S(1)}, bf16[256,704]{1,0:T(8,128)(...) custom-call(s32[9]{0:T(128)S(1)} %stack.39.offs, ...), custom_call_target="tpu_custom_call" | custom-call | flops 1 | bytes 1 | tf_op jit(solution)/shard_map/backward_0/pallas_call | solution.py:129
  48.8 2.9 %backward_1.1 = (bf16[128,2048]{1,0:T(8,128)(2,1)S(1)}, bf16[128,2048]{1,0:T(8,128)(2,1)S(1)}, bf16[256,704]{1,0:T(8,128)(2,1)S(1)}, bf16[256,704]{1,0:T(8,128)(...) custom-call(s32[9]{0:T(128)S(1)} %stack.39.offs, ...), custom_call_target="tpu_custom_call" | custom-call | flops 1 | bytes 1 | tf_op jit(solution)/shard_map/backward_1/pallas_call | solution.py:129
  55.4 2.6 %forward_2.1 = (bf16[256,704]{1,0:T(8,128)(2,1)S(1)}, f32[256,704]{1,0:T(8,128)S(1)}, f32[256,704]{1,0:T(8,128)S(1)}, bf16[256,1024]{1,0:T(8,128)(2,1)S(1)}, bf16[256,1024]{1,0:T(8,128)(2,1)S(1)}) custom-call(s32[9]{0:T(128)S(1)} %stack.39.offs, bf16[128,2048]{1,0:T(8,128)(2,1)S(1)} %collective-permute-done.1.refs_0_, ...), custom_call_target="tpu_custom_call" | custom-call | flops 1 | bytes 1 | tf_op jit(solution)/shard_map/forward_2/pallas_call | solution.py:129
  58.0 2.9 %backward_2.1 = (bf16[128,2048]{1,0:T(8,128)(2,1)S(1)}, bf16[128,2048]{1,0:T(8,128)(2,1)S(1)}, bf16[256,704]{1,0:T(8,128)(2,1)S(1)}, bf16[256,704]{1,0:T(8,128)(...) custom-call(s32[9]{0:T(128)S(1)} %stack.39.offs, ...), custom_call_target="tpu_custom_call" | custom-call | flops 1 | bytes 1 | tf_op jit(solution)/shard_map/backward_2/pallas_call | solution.py:129
  66.4 2.6 %forward_3.1 = (bf16[256,704]{1,0:T(8,128)(2,1)S(1)}, f32[256,704]{1,0:T(8,128)S(1)}, f32[256,704]{1,0:T(8,128)S(1)}, bf16[256,1024]{1,0:T(8,128)(2,1)S(1)}, bf16[256,1024]{1,0:T(8,128)(2,1)S(1)}) custom-call(s32[9]{0:T(128)S(1)} %stack.39.offs, bf16[128,2048]{1,0:T(8,128)(2,1)S(1)} %collective-permute-done.9.refs_0_, ...), custom_call_target="tpu_custom_call" | custom-call | flops 1 | bytes 1 | tf_op jit(solution)/shard_map/forward_3/pallas_call | solution.py:129
  82.5 3.2 %both_s.1 = (bf16[2,704,512]{2,1,0:T(8,128)(2,1)S(1)}, bf16[2,704,512]{2,1,0:T(8,128)(2,1)S(1)}) custom-call(bf16[256,704]{1,0:T(8,128)(2,1)S(1)} %get-tuple-element.352.refs_0_, bf16[256,704]{1,0:T(8,128)(2,1)S(1)} %get-tuple-element.314.refs_1_.refs_0_, bf16[256,704]{1,0:T(8,128)(2,1)S(1)} %get-tuple-element.329.refs_2_.refs_0_, ...), custom_call_target="tpu_custom_call" | custom-call | flops 1 | bytes 1 | tf_op jit(solution)/shard_map/both_s/pallas_call | solution.py:129
  88.3 2.0 %collective-permute-start.28 = (bf16[128,2048]{1,0:T(8,128)(2,1)S(1)}, bf16[128,2048]{1,0:T(8,128)(2,1)S(1)}, u32[]{:S(2)}, u32[]{:S(2)}) collective-permute-start(bf16[128,2048]{1,0:T(8,128)(2,1)S(1)} %add_m2.1), channel_id=1, source_target_pairs={{0,2},{1,3},{2,6},{3,7},{6,4},{7,5},{4,0},{5,1},{8,10},{9,11},{10,... | collective-permute-start | bytes 1572872 | tf_op jit(solution)/shard_map/m2/ppermute | solution.py:307
  96.8 1.8 %rows_3.1 = (bf16[128,2048]{1,0:T(8,128)(2,1)S(1)}, bf16[128,2048]{1,0:T(8,128)(2,1)S(1)}) custom-call(bf16[256,704]{1,0:T(8,128)(2,1)S(1)} %get-tuple-element.348.refs_3_.refs_0_, bf16[256,704]{1,0:T(8,128)(2,1)S(1)} %get-tuple-element.305.refs_7_.refs_1_, bf16[704,2048]{1,0:T(8,128)(2,1)S(1)} %bitcast.29, bf16[704,2048]{1,0:T(8,128)(2,1)S(1)} %bitcast.37), custom_call_target="tpu_custom_call" | custom-call | flops 1 | bytes 1 | tf_op jit(solution)/shard_map/rows_3/pallas_call | solution.py:129
  100.5 3.1 %collective-permute-start.27 = (bf16[128,2048]{1,0:T(8,128)(2,1)S(1)}, bf16[128,2048]{1,0:T(8,128)(2,1)S(1)}, u32[]{:S(2)}, u32[]{:S(2)}) collective-permute-start(bf16[128,2048]{1,0:T(8,128)(2,1)S(1)} %add_g1.1), channel_id=1, source_target_pairs={{0,2},{1,3},{2,6},{3,7},{6,4},{7,5},{4,0},{5,1},{8,10},{9,11},{10,... | collective-permute-start | bytes 1572872 | tf_op jit(solution)/shard_map/ga1/ppermute | solution.py:307
  103.7 4.8 %kept_k.1 = (bf16[3,704,512]{2,1,0:T(8,128)(2,1)S(1)}, bf16[3,704,512]{2,1,0:T(8,128)(2,1)S(1)}) custom-call(bf16[256,704]{1,0:T(8,128)(2,1)S(1)} %get-tuple-element.352.refs_0_, bf16[256,704]{1,0:T(8,128)(2,1)S(1)} %get-tuple-element.314.refs_1_.refs_0_, bf16[256,704]{1,0:T(8,128)(2,1)S(1)} %get-tuple-element.329.refs_2_.refs_0_, ...), custom_call_target="tpu_custom_call" | custom-call | flops 1 | bytes 1 | tf_op jit(solution)/shard_map/kept_k/pallas_call | solution.py:129
  109.0 7.5 %collective-permute-done.27.refs_0_ = bf16[128,2048]{1,0:T(8,128)(2,1)S(1)} collective-permute-done((bf16[128,2048]{1,0:T(8,128)(2,1)S(1)}, bf16[128,2048]{1,0:T(8,128)(2,1)S(1)}, u32[]{:S(2)}, u32[]{:S(2)}) %collective-permute-start.27) | collective-permute-done | bytes 524320 | tf_op jit(solution)/shard_map/ga1/ppermute | solution.py:307
  116.8 2.0 %collective-permute-start.31 = (bf16[128,2048]{1,0:T(8,128)(2,1)S(1)}, bf16[128,2048]{1,0:T(8,128)(2,1)S(1)}, u32[]{:S(2)}, u32[]{:S(2)}) collective-permute-start(bf16[128,2048]{1,0:T(8,128)(2,1)S(1)} %add_g2.1), channel_id=1, source_target_pairs={{0,2},{1,3},{2,6},{3,7},{6,4},{7,5},{4,0},{5,1},{8,10},{9,11},{10,... | collective-permute-start | bytes 1572872 | tf_op jit(solution)/shard_map/ga2/ppermute | solution.py:307
  118.8 9.0 %collective-permute-done.35.refs_0_ = bf16[128,2048]{1,0:T(8,128)(2,1)S(1)} collective-permute-done((bf16[128,2048]{1,0:T(8,128)(2,1)S(1)}, bf16[128,2048]{1,0:T(8,128)(2,1)S(1)}, u32[]{:S(2)}, u32[]{:S(2)}) %collective-permute-start.35) | collective-permute-done | bytes 524320 | tf_op jit(solution)/shard_map/m3/ppermute | solution.py:307
  131.6 6.4 %collective-permute-done.31 = bf16[128,2048]{1,0:T(8,128)(2,1)S(1)} collective-permute-done((bf16[128,2048]{1,0:T(8,128)(2,1)S(1)}, bf16[128,2048]{1,0:T(8,128)(2,1)S(1)}, u32[]{:S(2)}, u32[]{:S(2)}) %collective-permute-start.31) | collective-permute-done | bytes 524320 | tf_op jit(solution)/shard_map/ga2/ppermute | solution.py:307
  138.3 2.0 %collective-permute-start.36 = (bf16[128,2048]{1,0:T(8,128)(2,1)S(1)}, bf16[128,2048]{1,0:T(8,128)(2,1)S(1)}, u32[]{:S(2)}, u32[]{:S(2)}) collective-permute-start(bf16[128,2048]{1,0:T(8,128)(2,1)S(1)} %add_convert_fusion.1), channel_id=1, source_target_pairs={{0,2},{1,3},{2,6},{3,7},{6,4},{7,5},{4,0},{5,1},{8,10},{9,11},{10,... | collective-permute-start | bytes 1572872 | tf_op jit(solution)/shard_map/ga3/ppermute | solution.py:307
  141.7 11.8 %collective-permute-done.36 = bf16[128,2048]{1,0:T(8,128)(2,1)S(1)} collective-permute-done((bf16[128,2048]{1,0:T(8,128)(2,1)S(1)}, bf16[128,2048]{1,0:T(8,128)(2,1)S(1)}, u32[]{:S(2)}, u32[]{:S(2)}) %collective-permute-start.36) | collective-permute-done | bytes 524320 | tf_op jit(solution)/shard_map/ga3/ppermute | solution.py:307
  156.0 2.4 %finish.1 = (f32[704,512]{1,0:T(8,128)}, f32[704,512]{1,0:T(8,128)}, f32[704,512]{1,0:T(8,128)}) custom-call(f32[3,704,256]{2,1,0:T(8,128)S(1)} %get-tuple-element.419.near_a, f32[3,704,256]{2,1,0:T(8,128)S(1)} %get-tuple-element.420.near_b, bf16[3,704,256]{2,1,0:T(8,128)(2,1)S(1)} %collective-permute-done.38.last_a, ...), custom_call_target="tpu_custom_call" | custom-call | flops 1 | bytes 1 | tf_op jit(solution)/shard_map/finish/pallas_call | solution.py:129
  (115 shorter events, 54.6 us)
Async XLA Ops:
  0.6 17.2 %collective-permute-start = (bf16[128,2048]{1,0:T(8,128)(2,1)}, bf16[128,2048]{1,0:T(8,128)(2,1)}, u32[]{:S(2)}, u32[]{:S(2)}) collective-permute-start(bf16[128,2048]{1,0:T(8,128)(2,1)} %refs_0_), channel_id=1, source_target_pairs={{0,2},{1,3},{2,6},{3,7},{6,4},{7,5},{4,0},{5,1},{8,10},{9,11},{10,... | collective-permute-start | bytes 1572872 | tf_op jit(solution)/shard_map/t1/ppermute | solution.py:307
  6.8 22.8 %collective-permute-start.2 = (bf16[128,2176]{1,0:T(8,128)(2,1)S(1)}, bf16[128,2176]{1,0:T(8,128)(2,1)S(1)}, u32[]{:S(2)}, u32[]{:S(2)}) collective-permute-start(bf16[128,2176]{1,0:T(8,128)(2,1)S(1)} %pack.1.refs_0_), channel_id=1, source_target_pairs={{0,2},{1,3},{2,6},{3,7},{6,4},{7,5},{4,0},{5,1},{8,10},{9,11},{10,... | collective-permute-start | bytes 1671176 | tf_op jit(solution)/shard_map/c1/ppermute | solution.py:307
  17.8 11.8 %collective-permute-start.4 = (bf16[128,2048]{1,0:T(8,128)(2,1)}, bf16[128,2048]{1,0:T(8,128)(2,1)S(1)}, u32[]{:S(2)}, u32[]{:S(2)}) collective-permute-start(bf16[128,2048]{1,0:T(8,128)(2,1)} %collective-permute-done.refs_0_), channel_id=1, source_target_pairs={{0,1},{1,0},{2,3},{3,2},{4,5},{5,4},{6,7},{7,6},{8,9},{9,8},{10,11... | collective-permute-start | bytes 1572872 | tf_op jit(solution)/shard_map/p1/ppermute | solution.py:311
  17.8 24.4 %collective-permute-start.1 = (bf16[128,2048]{1,0:T(8,128)(2,1)}, bf16[128,2048]{1,0:T(8,128)(2,1)S(1)}, u32[]{:S(2)}, u32[]{:S(2)}) collective-permute-start(bf16[128,2048]{1,0:T(8,128)(2,1)} %collective-permute-done.refs_0_), channel_id=1, source_target_pairs={{0,2},{1,3},{2,6},{3,7},{6,4},{7,5},{4,0},{5,1},{8,10},{9,11},{10,... | collective-permute-start | bytes 1572872 | tf_op jit(solution)/shard_map/t2/ppermute | solution.py:307
  18.9 27.0 %collective-permute-start.6 = (bf16[128,2176]{1,0:T(8,128)(2,1)S(1)}, bf16[128,2176]{1,0:T(8,128)(2,1)S(1)}, u32[]{:S(2)}, u32[]{:S(2)}) collective-permute-start(bf16[128,2176]{1,0:T(8,128)(2,1)S(1)} %pack.1.refs_0_), channel_id=1, source_target_pairs={{0,1},{1,0},{2,3},{3,2},{4,5},{5,4},{6,7},{7,6},{8,9},{9,8},{10,11... | collective-permute-start | bytes 1671176 | tf_op jit(solution)/shard_map/q0/ppermute | solution.py:311
  30.4 18.4 %collective-permute-start.5 = (bf16[128,2176]{1,0:T(8,128)(2,1)S(1)}, bf16[128,2176]{1,0:T(8,128)(2,1)S(1)}, u32[]{:S(2)}, u32[]{:S(2)}) collective-permute-start(bf16[128,2176]{1,0:T(8,128)(2,1)S(1)} %collective-permute-done.2.refs_0_), channel_id=1, source_target_pairs={{0,1},{1,0},{2,3},{3,2},{4,5},{5,4},{6,7},{7,6},{8,9},{9,8},{10,11... | collective-permute-start | bytes 1671176 | tf_op jit(solution)/shard_map/q1/ppermute | solution.py:311
  30.4 22.4 %collective-permute-start.7 = (bf16[128,2176]{1,0:T(8,128)(2,1)S(1)}, bf16[128,2176]{1,0:T(8,128)(2,1)S(1)}, u32[]{:S(2)}, u32[]{:S(2)}) collective-permute-start(bf16[128,2176]{1,0:T(8,128)(2,1)S(1)} %collective-permute-done.2.refs_0_), channel_id=1, source_target_pairs={{0,2},{1,3},{2,6},{3,7},{6,4},{7,5},{4,0},{5,1},{8,10},{9,11},{10,... | collective-permute-start | bytes 1671176 | tf_op jit(solution)/shard_map/c2/ppermute | solution.py:307
  42.5 21.5 %collective-permute-start.9 = (bf16[128,2048]{1,0:T(8,128)(2,1)S(1)}, bf16[128,2048]{1,0:T(8,128)(2,1)S(1)}, u32[]{:S(2)}, u32[]{:S(2)}) collective-permute-start(bf16[128,2048]{1,0:T(8,128)(2,1)S(1)} %collective-permute-done.1.refs_0_), channel_id=1, source_target_pairs={{0,2},{1,3},{2,6},{3,7},{6,4},{7,5},{4,0},{5,1},{8,10},{9,11},{10,... | collective-permute-start | bytes 1572872 | tf_op jit(solution)/shard_map/t3/ppermute | solution.py:307
  51.7 12.3 %collective-permute-start.10 = (bf16[128,2048]{1,0:T(8,128)(2,1)S(1)}, bf16[128,2048]{1,0:T(8,128)(2,1)S(1)}, u32[]{:S(2)}, u32[]{:S(2)}) collective-permute-start(bf16[128,2048]{1,0:T(8,128)(2,1)S(1)} %get-tuple-element.250), channel_id=1, source_target_pairs={{0,1},{1,0},{2,3},{3,2},{4,5},{5,4},{6,7},{7,6},{8,9},{9,8},{10,11... | collective-permute-start | bytes 1572872 | tf_op jit(solution)/shard_map/o1/ppermute | solution.py:311
  54.0 16.3 %collective-permute-start.14 = (bf16[128,1152]{1,0:T(8,128)(2,1)S(1)}, bf16[128,1152]{1,0:T(8,128)(2,1)S(1)}, u32[]{:S(2)}, u32[]{:S(2)}) collective-permute-start(bf16[128,1152]{1,0:T(8,128)(2,1)S(1)} %get-tuple-element.268), channel_id=1, source_target_pairs={{0,2},{1,3},{2,6},{3,7},{6,4},{7,5},{4,0},{5,1},{8,10},{9,11},{10,... | collective-permute-start | bytes 884744 | tf_op jit(solution)/shard_map/c3s/ppermute | solution.py:307
  70.5 17.1 %collective-permute-start.22 = (bf16[128,2048]{1,0:T(8,128)(2,1)S(1)}, bf16[128,2048]{1,0:T(8,128)(2,1)S(1)}, u32[]{:S(2)}, u32[]{:S(2)}) collective-permute-start(bf16[128,2048]{1,0:T(8,128)(2,1)S(1)} %add_m1.1), channel_id=1, source_target_pairs={{0,2},{1,3},{2,6},{3,7},{6,4},{7,5},{4,0},{5,1},{8,10},{9,11},{10,... | collective-permute-start | bytes 1572872 | tf_op jit(solution)/shard_map/m1/ppermute | solution.py:307
  76.0 17.5 %collective-permute-start.26 = (bf16[1,704,512]{2,1,0:T(8,128)(2,1)S(1)}, bf16[1,704,512]{2,1,0:T(8,128)(2,1)S(1)}, u32[]{:S(2)}, u32[]{:S(2)}) collective-permute-start(bf16[1,704,512]{2,1,0:T(8,128)(2,1)S(1)} %get-tuple-element.335), channel_id=1, source_target_pairs={{0,16},{8,24},{16,0},{24,8},{1,17},{9,25},{17,1},{25,9},{2,18},{10... | collective-permute-start | bytes 2162696 | tf_op jit(solution)/shard_map/d1/ppermute | solution.py:315
  77.6 17.1 %collective-permute-start.25 = (bf16[1,704,512]{2,1,0:T(8,128)(2,1)S(1)}, bf16[1,704,512]{2,1,0:T(8,128)(2,1)S(1)}, u32[]{:S(2)}, u32[]{:S(2)}) collective-permute-start(bf16[1,704,512]{2,1,0:T(8,128)(2,1)S(1)} %get-tuple-element.333), channel_id=1, source_target_pairs={{0,8},{8,0},{16,24},{24,16},{1,9},{9,1},{17,25},{25,17},{2,10},{10... | collective-permute-start | bytes 2162696 | tf_op jit(solution)/shard_map/d1/ppermute | solution.py:315
  88.3 20.1 %collective-permute-start.28 = (bf16[128,2048]{1,0:T(8,128)(2,1)S(1)}, bf16[128,2048]{1,0:T(8,128)(2,1)S(1)}, u32[]{:S(2)}, u32[]{:S(2)}) collective-permute-start(bf16[128,2048]{1,0:T(8,128)(2,1)S(1)} %add_m2.1), channel_id=1, source_target_pairs={{0,2},{1,3},{2,6},{3,7},{6,4},{7,5},{4,0},{5,1},{8,10},{9,11},{10,... | collective-permute-start | bytes 1572872 | tf_op jit(solution)/shard_map/m2/ppermute | solution.py:307
  94.7 13.7 %collective-permute-start.29 = (bf16[128,2048]{1,0:T(8,128)(2,1)S(1)}, bf16[128,2048]{1,0:T(8,128)(2,1)S(1)}, u32[]{:S(2)}, u32[]{:S(2)}) collective-permute-start(bf16[128,2048]{1,0:T(8,128)(2,1)S(1)} %get-tuple-element.347), channel_id=1, source_target_pairs={{0,1},{1,0},{2,3},{3,2},{4,5},{5,4},{6,7},{7,6},{8,9},{9,8},{10,11... | collective-permute-start | bytes 1572872 | tf_op jit(solution)/shard_map/o0/ppermute | solution.py:311
  94.7 34.0 %collective-permute-start.33 = (bf16[2,704,512]{2,1,0:T(8,128)(2,1)S(1)}, bf16[2,704,512]{2,1,0:T(8,128)(2,1)S(1)}, u32[]{:S(2)}, u32[]{:S(2)}) collective-permute-start(bf16[2,704,512]{2,1,0:T(8,128)(2,1)S(1)} %get-tuple-element.377), channel_id=1, source_target_pairs={{0,8},{8,0},{16,24},{24,16},{1,9},{9,1},{17,25},{25,17},{2,10},{10... | collective-permute-start | bytes 4325384 | tf_op jit(solution)/shard_map/gu1/ppermute | solution.py:315
  96.2 33.7 %collective-permute-start.34 = (bf16[2,704,512]{2,1,0:T(8,128)(2,1)S(1)}, bf16[2,704,512]{2,1,0:T(8,128)(2,1)S(1)}, u32[]{:S(2)}, u32[]{:S(2)}) collective-permute-start(bf16[2,704,512]{2,1,0:T(8,128)(2,1)S(1)} %get-tuple-element.379), channel_id=1, source_target_pairs={{0,16},{8,24},{16,0},{24,8},{1,17},{9,25},{17,1},{25,9},{2,18},{10... | collective-permute-start | bytes 4325384 | tf_op jit(solution)/shard_map/gu1/ppermute | solution.py:315
  100.5 16.0 %collective-permute-start.27 = (bf16[128,2048]{1,0:T(8,128)(2,1)S(1)}, bf16[128,2048]{1,0:T(8,128)(2,1)S(1)}, u32[]{:S(2)}, u32[]{:S(2)}) collective-permute-start(bf16[128,2048]{1,0:T(8,128)(2,1)S(1)} %add_g1.1), channel_id=1, source_target_pairs={{0,2},{1,3},{2,6},{3,7},{6,4},{7,5},{4,0},{5,1},{8,10},{9,11},{10,... | collective-permute-start | bytes 1572872 | tf_op jit(solution)/shard_map/ga1/ppermute | solution.py:307
  108.7 19.0 %collective-permute-start.35 = (bf16[128,2048]{1,0:T(8,128)(2,1)S(1)}, bf16[128,2048]{1,0:T(8,128)(2,1)S(1)}, u32[]{:S(2)}, u32[]{:S(2)}) collective-permute-start(bf16[128,2048]{1,0:T(8,128)(2,1)S(1)} %add_m3.1), channel_id=1, source_target_pairs={{0,2},{1,3},{2,6},{3,7},{6,4},{7,5},{4,0},{5,1},{8,10},{9,11},{10,... | collective-permute-start | bytes 1572872 | tf_op jit(solution)/shard_map/m3/ppermute | solution.py:307
  116.7 14.8 %collective-permute-start.32 = (bf16[128,2048]{1,0:T(8,128)(2,1)S(1)}, bf16[128,2048]{1,0:T(8,128)(2,1)S(1)}, u32[]{:S(2)}, u32[]{:S(2)}) collective-permute-start(bf16[128,2048]{1,0:T(8,128)(2,1)S(1)} %get-tuple-element.375), channel_id=1, source_target_pairs={{0,1},{1,0},{2,3},{3,2},{4,5},{5,4},{6,7},{7,6},{8,9},{9,8},{10,11... | collective-permute-start | bytes 1572872 | tf_op jit(solution)/shard_map/r3/ppermute | solution.py:311
  116.8 21.2 %collective-permute-start.31 = (bf16[128,2048]{1,0:T(8,128)(2,1)S(1)}, bf16[128,2048]{1,0:T(8,128)(2,1)S(1)}, u32[]{:S(2)}, u32[]{:S(2)}) collective-permute-start(bf16[128,2048]{1,0:T(8,128)(2,1)S(1)} %add_g2.1), channel_id=1, source_target_pairs={{0,2},{1,3},{2,6},{3,7},{6,4},{7,5},{4,0},{5,1},{8,10},{9,11},{10,... | collective-permute-start | bytes 1572872 | tf_op jit(solution)/shard_map/ga2/ppermute | solution.py:307
  130.5 25.2 %collective-permute-start.39 = (bf16[3,704,256]{2,1,0:T(8,128)(2,1)S(1)}, bf16[3,704,256]{2,1,0:T(8,128)(2,1)S(1)}, u32[]{:S(2)}, u32[]{:S(2)}) collective-permute-start(bf16[3,704,256]{2,1,0:T(8,128)(2,1)S(1)} %get-tuple-element.417), channel_id=1, source_target_pairs={{0,8},{8,0},{16,24},{24,16},{1,9},{9,1},{17,25},{25,17},{2,10},{10... | collective-permute-start | bytes 3244040 | tf_op jit(solution)/shard_map/last/ppermute | solution.py:315
  131.1 25.0 %collective-permute-start.38 = (bf16[3,704,256]{2,1,0:T(8,128)(2,1)S(1)}, bf16[3,704,256]{2,1,0:T(8,128)(2,1)S(1)}, u32[]{:S(2)}, u32[]{:S(2)}) collective-permute-start(bf16[3,704,256]{2,1,0:T(8,128)(2,1)S(1)} %get-tuple-element.415), channel_id=1, source_target_pairs={{0,16},{8,24},{16,0},{24,8},{1,17},{9,25},{17,1},{25,9},{2,18},{10... | collective-permute-start | bytes 3244040 | tf_op jit(solution)/shard_map/last/ppermute | solution.py:315
  138.3 15.2 %collective-permute-start.36 = (bf16[128,2048]{1,0:T(8,128)(2,1)S(1)}, bf16[128,2048]{1,0:T(8,128)(2,1)S(1)}, u32[]{:S(2)}, u32[]{:S(2)}) collective-permute-start(bf16[128,2048]{1,0:T(8,128)(2,1)S(1)} %add_convert_fusion.1), channel_id=1, source_target_pairs={{0,2},{1,3},{2,6},{3,7},{6,4},{7,5},{4,0},{5,1},{8,10},{9,11},{10,... | collective-permute-start | bytes 1572872 | tf_op jit(solution)/shard_map/ga3/ppermute | solution.py:307
  (27 other events, 104.3 us)

commit v7 on v6

--- a/solution.py
+++ b/solution.py
@@ -125,16 +125,17 @@
     return lax.dot_general(left, right, (((0,), (0,)), ((), ())), preferred_element_type=F32)
 
 
-def call(name, kernel, outs, ins, scratch=(), smem=0, flops=1):
+def call(name, kernel, outs, ins, scratch=(), smem=0, copies=0):
     return list(pl.pallas_call(
         kernel,
         name=name,
         out_shape=[jax.ShapeDtypeStruct(shape, dtype) for shape, dtype in outs],
         in_specs=[SMEM] * smem + [VMEM] * (len(ins) - smem),
-        out_specs=[VMEM] * len(outs),
-        scratch_shapes=[pltpu.VMEM(shape, dtype) for shape, dtype in scratch],
+        out_specs=[pl.BlockSpec(memory_space=pl.ANY) if copies else VMEM] * len(outs),
+        scratch_shapes=[pltpu.VMEM(shape, dtype) for shape, dtype in scratch]
+        + ([pltpu.SemaphoreType.DMA((copies,))] if copies else []),
         compiler_params=pltpu.CompilerParams(vmem_limit_bytes=16 * 1024 * 1024),
-        cost_estimate=pl.CostEstimate(flops=flops, bytes_accessed=1, transcendentals=0),
+        cost_estimate=pl.CostEstimate(flops=1, bytes_accessed=1, transcendentals=0),
     )(*ins))
 
 
@@ -280,11 +281,17 @@
             out[at, :, :] = (first.astype(F32) + own[at, :, part].astype(F32)).astype(out.dtype)
 
 
-def finish_kernel(near_a, near_b, last_a, last_b, *outs):
+def finish_kernel(near_a, near_b, last_a, last_b, *refs):
+    outs, (held, sems) = refs[:-2], refs[-2:]
     cut = near_a.shape[2]
+    copies = []
     for at, out in enumerate(outs):
-        out[:, :cut] = near_a[at, :, :] + last_a[at, :, :].astype(F32)
-        out[:, cut:] = near_b[at, :, :] + last_b[at, :, :].astype(F32)
+        held[at, :, :cut] = near_a[at, :, :] + last_a[at, :, :].astype(F32)
+        held[at, :, cut:] = near_b[at, :, :] + last_b[at, :, :].astype(F32)
+        copies.append(pltpu.make_async_copy(held.at[at], out, sems.at[at]))
+        copies[-1].start()
+    for copy in copies:
+        copy.wait()
 
 
 def rows_kernel(*refs):
@@ -349,8 +356,8 @@
         with jax.named_scope(name):
             return [flip(order.after(value), mask) for value, mask in zip(pair, masks)]
 
-    def launch(name, kernel, outs, ins, scratch=(), smem=0, flops=1):
-        return call(name, kernel, outs, [*ins[:smem], order.after(ins[smem]), *ins[smem + 1 :]], scratch, smem, flops)
+    def launch(name, kernel, outs, ins, scratch=(), smem=0, copies=0):
+        return call(name, kernel, outs, [*ins[:smem], order.after(ins[smem]), *ins[smem + 1 :]], scratch, smem, copies)
 
     gate_w, up_w, down_w = w_gate[0].T, w_up[0].T, w_down[0]
     me = lax.axis_index("dp")
@@ -524,7 +531,12 @@
     token_grad = add(g, kept(m0, r0)).astype(BF16)
     token_grad, *last = order.point(token_grad, *last)
     grad_gate, grad_up, grad_down = launch(
-        "finish", finish_kernel, [((ff, 2 * cut), F32)] * 3, [near_a, near_b, *last]
+        "finish",
+        finish_kernel,
+        [((ff, 2 * cut), F32)] * 3,
+        [near_a, near_b, *last],
+        [((3, ff, 2 * cut), F32)],
+        copies=3,
     )
     return (mixed, token_grad, grad_gate.T[None], grad_up.T[None], grad_down[None])
 

time: 159 us -> 159 us (level)
  no operation moved by 1% of the time
where the time goes in v7:
time: 159 us; the launch traced here: 158 us
  waiting for transfers between devices  65 us (41%)
  Pallas kernels  46.1 us (29%)
  starting transfers between devices  35.6 us (22%)
  local copies, waits for them, and re-layouts  9.1 us (6%)
    ppermute x13, waiting for transfers between devices, step(): lax.ppermute(value, 'expert', [(2 * at + core, 2 * follow[at] + core) for...  57.6 us
    pallas_call x28, Pallas kernels, call(): pl.pallas_call(kernel, name=name, out_shape=[jax.ShapeDtypeStruct(shape,...  46.1 us
    ppermute x13, starting transfers between devices, step(): lax.ppermute(value, 'expert', [(2 * at + core, 2 * follow[at] + core) for...  25.6 us
    unnamed x23, local copies, waits for them, and re-layouts  8.11 us
    ppermute x6, waiting for transfers between devices, flip(): return lax.ppermute(value, 'dp', [(at, at ^ mask) for at in range(4)])  6.3 us
    ppermute x6, starting transfers between devices, flip(): return lax.ppermute(value, 'dp', [(at, at ^ mask) for at in range(4)])  6.24 us
    ppermute x21, starting transfers between devices, swap(): lax.ppermute(value, 'expert', [(at, at ^ 1) for at in range(n_expert)])  3.73 us
  transfers between devices with their start and end apart: 40, of which 18 were waited for; matrix products, arithmetic and copies ran while one was open for 2% of the time, Pallas kernels for 28%

profile of v7, /device:TPU:0, one launch (start us, length us, event | category | flops | bytes accessed | tf_op | source)
XLA Modules:
  0.0 158.4 jit_solution(12969418458065161501)
XLA Ops:
  0.6 3.1 %collective-permute-start = (bf16[128,2048]{1,0:T(8,128)(2,1)}, bf16[128,2048]{1,0:T(8,128)(2,1)}, u32[]{:S(2)}, u32[]{:S(2)}) collective-permute-start(bf16[128,2048]{1,0:T(8,128)(2,1)} %refs_0_), channel_id=1, source_target_pairs={{0,2},{1,3},{2,6},{3,7},{6,4},{7,5},{4,0},{5,1},{8,10},{9,11},{10,... | collective-permute-start | bytes 1572872 | tf_op jit(solution)/shard_map/t1/ppermute | solution.py:314
  6.8 2.6 %collective-permute-start.2 = (bf16[128,2176]{1,0:T(8,128)(2,1)S(1)}, bf16[128,2176]{1,0:T(8,128)(2,1)S(1)}, u32[]{:S(2)}, u32[]{:S(2)}) collective-permute-start(bf16[128,2176]{1,0:T(8,128)(2,1)S(1)} %pack.1.refs_0_), channel_id=1, source_target_pairs={{0,2},{1,3},{2,6},{3,7},{6,4},{7,5},{4,0},{5,1},{8,10},{9,11},{10,... | collective-permute-start | bytes 1671176 | tf_op jit(solution)/shard_map/c1/ppermute | solution.py:314
  9.5 8.3 %collective-permute-done.refs_0_ = bf16[128,2048]{1,0:T(8,128)(2,1)} collective-permute-done((bf16[128,2048]{1,0:T(8,128)(2,1)}, bf16[128,2048]{1,0:T(8,128)(2,1)}, u32[]{:S(2)}, u32[]{:S(2)}) %collective-permute-start) | collective-permute-done | bytes 524320 | tf_op jit(solution)/shard_map/t1/ppermute | solution.py:314
  20.0 9.7 %collective-permute-done.2.refs_0_ = bf16[128,2176]{1,0:T(8,128)(2,1)S(1)} collective-permute-done((bf16[128,2176]{1,0:T(8,128)(2,1)S(1)}, bf16[128,2176]{1,0:T(8,128)(2,1)S(1)}, u32[]{:S(2)}, u32[]{:S(2)}) %collective-permute-start.2) | collective-permute-done | bytes 557088 | tf_op jit(solution)/shard_map/c1/ppermute | solution.py:314
  36.3 3.2 %forward_1.1 = (bf16[256,704]{1,0:T(8,128)(2,1)S(1)}, f32[256,704]{1,0:T(8,128)S(1)}, f32[256,704]{1,0:T(8,128)S(1)}, bf16[256,1024]{1,0:T(8,128)(2,1)S(1)}, bf16[256,1024]{1,0:T(8,128)(2,1)S(1)}) custom-call(s32[9]{0:T(128)S(1)} %stack.39.offs, bf16[128,2048]{1,0:T(8,128)(2,1)} %collective-permute-done.refs_0_, bf16[128,2048]{1,0:T(8,128)(2,1)S(1)} %copy-done.10, ...), custom_call_target="tpu_custom_call" | custom-call | flops 1 | bytes 1 | tf_op jit(solution)/shard_map/forward_1/pallas_call | solution.py:129
  39.6 2.6 %forward_0.1 = (bf16[256,704]{1,0:T(8,128)(2,1)S(1)}, f32[256,704]{1,0:T(8,128)S(1)}, f32[256,704]{1,0:T(8,128)S(1)}, bf16[256,1024]{1,0:T(8,128)(2,1)S(1)}, bf16[256,1024]{1,0:T(8,128)(2,1)S(1)}) custom-call(s32[9]{0:T(128)S(1)} %stack.39.offs, bf16[128,2048]{1,0:T(8,128)(2,1)S(1)} %copy-done.6, bf16[128,2048]{1,0:T(8,128)(2,1)S(1)} %copy-done.8, ...), custom_call_target="tpu_custom_call" | custom-call | flops 1 | bytes 1 | tf_op jit(solution)/shard_map/forward_0/pallas_call | solution.py:129
  42.5 3.4 %collective-permute-start.9 = (bf16[128,2048]{1,0:T(8,128)(2,1)S(1)}, bf16[128,2048]{1,0:T(8,128)(2,1)S(1)}, u32[]{:S(2)}, u32[]{:S(2)}) collective-permute-start(bf16[128,2048]{1,0:T(8,128)(2,1)S(1)} %collective-permute-done.1.refs_0_), channel_id=1, source_target_pairs={{0,2},{1,3},{2,6},{3,7},{6,4},{7,5},{4,0},{5,1},{8,10},{9,11},{10,... | collective-permute-start | bytes 1572872 | tf_op jit(solution)/shard_map/t3/ppermute | solution.py:314
  45.9 2.9 %backward_0.1 = (bf16[128,2048]{1,0:T(8,128)(2,1)S(1)}, bf16[128,2048]{1,0:T(8,128)(2,1)S(1)}, bf16[256,704]{1,0:T(8,128)(2,1)S(1)}, bf16[256,704]{1,0:T(8,128)(...) custom-call(s32[9]{0:T(128)S(1)} %stack.39.offs, ...), custom_call_target="tpu_custom_call" | custom-call | flops 1 | bytes 1 | tf_op jit(solution)/shard_map/backward_0/pallas_call | solution.py:129
  48.8 2.9 %backward_1.1 = (bf16[128,2048]{1,0:T(8,128)(2,1)S(1)}, bf16[128,2048]{1,0:T(8,128)(2,1)S(1)}, bf16[256,704]{1,0:T(8,128)(2,1)S(1)}, bf16[256,704]{1,0:T(8,128)(...) custom-call(s32[9]{0:T(128)S(1)} %stack.39.offs, ...), custom_call_target="tpu_custom_call" | custom-call | flops 1 | bytes 1 | tf_op jit(solution)/shard_map/backward_1/pallas_call | solution.py:129
  55.4 2.6 %forward_2.1 = (bf16[256,704]{1,0:T(8,128)(2,1)S(1)}, f32[256,704]{1,0:T(8,128)S(1)}, f32[256,704]{1,0:T(8,128)S(1)}, bf16[256,1024]{1,0:T(8,128)(2,1)S(1)}, bf16[256,1024]{1,0:T(8,128)(2,1)S(1)}) custom-call(s32[9]{0:T(128)S(1)} %stack.39.offs, bf16[128,2048]{1,0:T(8,128)(2,1)S(1)} %collective-permute-done.1.refs_0_, ...), custom_call_target="tpu_custom_call" | custom-call | flops 1 | bytes 1 | tf_op jit(solution)/shard_map/forward_2/pallas_call | solution.py:129
  58.0 2.9 %backward_2.1 = (bf16[128,2048]{1,0:T(8,128)(2,1)S(1)}, bf16[128,2048]{1,0:T(8,128)(2,1)S(1)}, bf16[256,704]{1,0:T(8,128)(2,1)S(1)}, bf16[256,704]{1,0:T(8,128)(...) custom-call(s32[9]{0:T(128)S(1)} %stack.39.offs, ...), custom_call_target="tpu_custom_call" | custom-call | flops 1 | bytes 1 | tf_op jit(solution)/shard_map/backward_2/pallas_call | solution.py:129
  66.4 2.6 %forward_3.1 = (bf16[256,704]{1,0:T(8,128)(2,1)S(1)}, f32[256,704]{1,0:T(8,128)S(1)}, f32[256,704]{1,0:T(8,128)S(1)}, bf16[256,1024]{1,0:T(8,128)(2,1)S(1)}, bf16[256,1024]{1,0:T(8,128)(2,1)S(1)}) custom-call(s32[9]{0:T(128)S(1)} %stack.39.offs, bf16[128,2048]{1,0:T(8,128)(2,1)S(1)} %collective-permute-done.9.refs_0_, ...), custom_call_target="tpu_custom_call" | custom-call | flops 1 | bytes 1 | tf_op jit(solution)/shard_map/forward_3/pallas_call | solution.py:129
  82.5 3.2 %both_s.1 = (bf16[2,704,512]{2,1,0:T(8,128)(2,1)S(1)}, bf16[2,704,512]{2,1,0:T(8,128)(2,1)S(1)}) custom-call(bf16[256,704]{1,0:T(8,128)(2,1)S(1)} %get-tuple-element.352.refs_0_, bf16[256,704]{1,0:T(8,128)(2,1)S(1)} %get-tuple-element.314.refs_1_.refs_0_, bf16[256,704]{1,0:T(8,128)(2,1)S(1)} %get-tuple-element.329.refs_2_.refs_0_, ...), custom_call_target="tpu_custom_call" | custom-call | flops 1 | bytes 1 | tf_op jit(solution)/shard_map/both_s/pallas_call | solution.py:129
  88.3 2.0 %collective-permute-start.28 = (bf16[128,2048]{1,0:T(8,128)(2,1)S(1)}, bf16[128,2048]{1,0:T(8,128)(2,1)S(1)}, u32[]{:S(2)}, u32[]{:S(2)}) collective-permute-start(bf16[128,2048]{1,0:T(8,128)(2,1)S(1)} %add_m2.1), channel_id=1, source_target_pairs={{0,2},{1,3},{2,6},{3,7},{6,4},{7,5},{4,0},{5,1},{8,10},{9,11},{10,... | collective-permute-start | bytes 1572872 | tf_op jit(solution)/shard_map/m2/ppermute | solution.py:314
  96.8 1.8 %rows_3.1 = (bf16[128,2048]{1,0:T(8,128)(2,1)S(1)}, bf16[128,2048]{1,0:T(8,128)(2,1)S(1)}) custom-call(bf16[256,704]{1,0:T(8,128)(2,1)S(1)} %get-tuple-element.348.refs_3_.refs_0_, bf16[256,704]{1,0:T(8,128)(2,1)S(1)} %get-tuple-element.305.refs_7_.refs_1_, bf16[704,2048]{1,0:T(8,128)(2,1)S(1)} %bitcast.29, bf16[704,2048]{1,0:T(8,128)(2,1)S(1)} %bitcast.37), custom_call_target="tpu_custom_call" | custom-call | flops 1 | bytes 1 | tf_op jit(solution)/shard_map/rows_3/pallas_call | solution.py:129
  100.5 3.1 %collective-permute-start.27 = (bf16[128,2048]{1,0:T(8,128)(2,1)S(1)}, bf16[128,2048]{1,0:T(8,128)(2,1)S(1)}, u32[]{:S(2)}, u32[]{:S(2)}) collective-permute-start(bf16[128,2048]{1,0:T(8,128)(2,1)S(1)} %add_g1.1), channel_id=1, source_target_pairs={{0,2},{1,3},{2,6},{3,7},{6,4},{7,5},{4,0},{5,1},{8,10},{9,11},{10,... | collective-permute-start | bytes 1572872 | tf_op jit(solution)/shard_map/ga1/ppermute | solution.py:314
  103.7 4.8 %kept_k.1 = (bf16[3,704,512]{2,1,0:T(8,128)(2,1)S(1)}, bf16[3,704,512]{2,1,0:T(8,128)(2,1)S(1)}) custom-call(bf16[256,704]{1,0:T(8,128)(2,1)S(1)} %get-tuple-element.352.refs_0_, bf16[256,704]{1,0:T(8,128)(2,1)S(1)} %get-tuple-element.314.refs_1_.refs_0_, bf16[256,704]{1,0:T(8,128)(2,1)S(1)} %get-tuple-element.329.refs_2_.refs_0_, ...), custom_call_target="tpu_custom_call" | custom-call | flops 1 | bytes 1 | tf_op jit(solution)/shard_map/kept_k/pallas_call | solution.py:129
  109.0 7.5 %collective-permute-done.27.refs_0_ = bf16[128,2048]{1,0:T(8,128)(2,1)S(1)} collective-permute-done((bf16[128,2048]{1,0:T(8,128)(2,1)S(1)}, bf16[128,2048]{1,0:T(8,128)(2,1)S(1)}, u32[]{:S(2)}, u32[]{:S(2)}) %collective-permute-start.27) | collective-permute-done | bytes 524320 | tf_op jit(solution)/shard_map/ga1/ppermute | solution.py:314
  116.8 2.0 %collective-permute-start.31 = (bf16[128,2048]{1,0:T(8,128)(2,1)S(1)}, bf16[128,2048]{1,0:T(8,128)(2,1)S(1)}, u32[]{:S(2)}, u32[]{:S(2)}) collective-permute-start(bf16[128,2048]{1,0:T(8,128)(2,1)S(1)} %add_g2.1), channel_id=1, source_target_pairs={{0,2},{1,3},{2,6},{3,7},{6,4},{7,5},{4,0},{5,1},{8,10},{9,11},{10,... | collective-permute-start | bytes 1572872 | tf_op jit(solution)/shard_map/ga2/ppermute | solution.py:314
  118.8 9.0 %collective-permute-done.35.refs_0_ = bf16[128,2048]{1,0:T(8,128)(2,1)S(1)} collective-permute-done((bf16[128,2048]{1,0:T(8,128)(2,1)S(1)}, bf16[128,2048]{1,0:T(8,128)(2,1)S(1)}, u32[]{:S(2)}, u32[]{:S(2)}) %collective-permute-start.35) | collective-permute-done | bytes 524320 | tf_op jit(solution)/shard_map/m3/ppermute | solution.py:314
  131.6 6.4 %collective-permute-done.31 = bf16[128,2048]{1,0:T(8,128)(2,1)S(1)} collective-permute-done((bf16[128,2048]{1,0:T(8,128)(2,1)S(1)}, bf16[128,2048]{1,0:T(8,128)(2,1)S(1)}, u32[]{:S(2)}, u32[]{:S(2)}) %collective-permute-start.31) | collective-permute-done | bytes 524320 | tf_op jit(solution)/shard_map/ga2/ppermute | solution.py:314
  138.3 2.0 %collective-permute-start.36 = (bf16[128,2048]{1,0:T(8,128)(2,1)S(1)}, bf16[128,2048]{1,0:T(8,128)(2,1)S(1)}, u32[]{:S(2)}, u32[]{:S(2)}) collective-permute-start(bf16[128,2048]{1,0:T(8,128)(2,1)S(1)} %add_convert_fusion.1), channel_id=1, source_target_pairs={{0,2},{1,3},{2,6},{3,7},{6,4},{7,5},{4,0},{5,1},{8,10},{9,11},{10,... | collective-permute-start | bytes 1572872 | tf_op jit(solution)/shard_map/ga3/ppermute | solution.py:314
  141.7 11.8 %collective-permute-done.36 = bf16[128,2048]{1,0:T(8,128)(2,1)S(1)} collective-permute-done((bf16[128,2048]{1,0:T(8,128)(2,1)S(1)}, bf16[128,2048]{1,0:T(8,128)(2,1)S(1)}, u32[]{:S(2)}, u32[]{:S(2)}) %collective-permute-start.36) | collective-permute-done | bytes 524320 | tf_op jit(solution)/shard_map/ga3/ppermute | solution.py:314
  156.0 2.2 %finish.1 = (f32[704,512]{1,0:T(8,128)}, f32[704,512]{1,0:T(8,128)}, f32[704,512]{1,0:T(8,128)}) custom-call(f32[3,704,256]{2,1,0:T(8,128)S(1)} %get-tuple-element.419.near_a, f32[3,704,256]{2,1,0:T(8,128)S(1)} %get-tuple-element.420.near_b, bf16[3,704,256]{2,1,0:T(8,128)(2,1)S(1)} %collective-permute-done.38.last_a, ...), custom_call_target="tpu_custom_call" | custom-call | flops 1 | bytes 1 | tf_op jit(solution)/shard_map/finish/pallas_call | solution.py:129
  (115 shorter events, 54.6 us)
Async XLA Ops:
  0.6 17.2 %collective-permute-start = (bf16[128,2048]{1,0:T(8,128)(2,1)}, bf16[128,2048]{1,0:T(8,128)(2,1)}, u32[]{:S(2)}, u32[]{:S(2)}) collective-permute-start(bf16[128,2048]{1,0:T(8,128)(2,1)} %refs_0_), channel_id=1, source_target_pairs={{0,2},{1,3},{2,6},{3,7},{6,4},{7,5},{4,0},{5,1},{8,10},{9,11},{10,... | collective-permute-start | bytes 1572872 | tf_op jit(solution)/shard_map/t1/ppermute | solution.py:314
  6.8 22.8 %collective-permute-start.2 = (bf16[128,2176]{1,0:T(8,128)(2,1)S(1)}, bf16[128,2176]{1,0:T(8,128)(2,1)S(1)}, u32[]{:S(2)}, u32[]{:S(2)}) collective-permute-start(bf16[128,2176]{1,0:T(8,128)(2,1)S(1)} %pack.1.refs_0_), channel_id=1, source_target_pairs={{0,2},{1,3},{2,6},{3,7},{6,4},{7,5},{4,0},{5,1},{8,10},{9,11},{10,... | collective-permute-start | bytes 1671176 | tf_op jit(solution)/shard_map/c1/ppermute | solution.py:314
  17.8 11.8 %collective-permute-start.4 = (bf16[128,2048]{1,0:T(8,128)(2,1)}, bf16[128,2048]{1,0:T(8,128)(2,1)S(1)}, u32[]{:S(2)}, u32[]{:S(2)}) collective-permute-start(bf16[128,2048]{1,0:T(8,128)(2,1)} %collective-permute-done.refs_0_), channel_id=1, source_target_pairs={{0,1},{1,0},{2,3},{3,2},{4,5},{5,4},{6,7},{7,6},{8,9},{9,8},{10,11... | collective-permute-start | bytes 1572872 | tf_op jit(solution)/shard_map/p1/ppermute | solution.py:318
  17.8 24.4 %collective-permute-start.1 = (bf16[128,2048]{1,0:T(8,128)(2,1)}, bf16[128,2048]{1,0:T(8,128)(2,1)S(1)}, u32[]{:S(2)}, u32[]{:S(2)}) collective-permute-start(bf16[128,2048]{1,0:T(8,128)(2,1)} %collective-permute-done.refs_0_), channel_id=1, source_target_pairs={{0,2},{1,3},{2,6},{3,7},{6,4},{7,5},{4,0},{5,1},{8,10},{9,11},{10,... | collective-permute-start | bytes 1572872 | tf_op jit(solution)/shard_map/t2/ppermute | solution.py:314
  18.9 27.0 %collective-permute-start.6 = (bf16[128,2176]{1,0:T(8,128)(2,1)S(1)}, bf16[128,2176]{1,0:T(8,128)(2,1)S(1)}, u32[]{:S(2)}, u32[]{:S(2)}) collective-permute-start(bf16[128,2176]{1,0:T(8,128)(2,1)S(1)} %pack.1.refs_0_), channel_id=1, source_target_pairs={{0,1},{1,0},{2,3},{3,2},{4,5},{5,4},{6,7},{7,6},{8,9},{9,8},{10,11... | collective-permute-start | bytes 1671176 | tf_op jit(solution)/shard_map/q0/ppermute | solution.py:318
  30.4 18.4 %collective-permute-start.5 = (bf16[128,2176]{1,0:T(8,128)(2,1)S(1)}, bf16[128,2176]{1,0:T(8,128)(2,1)S(1)}, u32[]{:S(2)}, u32[]{:S(2)}) collective-permute-start(bf16[128,2176]{1,0:T(8,128)(2,1)S(1)} %collective-permute-done.2.refs_0_), channel_id=1, source_target_pairs={{0,1},{1,0},{2,3},{3,2},{4,5},{5,4},{6,7},{7,6},{8,9},{9,8},{10,11... | collective-permute-start | bytes 1671176 | tf_op jit(solution)/shard_map/q1/ppermute | solution.py:318
  30.4 22.4 %collective-permute-start.7 = (bf16[128,2176]{1,0:T(8,128)(2,1)S(1)}, bf16[128,2176]{1,0:T(8,128)(2,1)S(1)}, u32[]{:S(2)}, u32[]{:S(2)}) collective-permute-start(bf16[128,2176]{1,0:T(8,128)(2,1)S(1)} %collective-permute-done.2.refs_0_), channel_id=1, source_target_pairs={{0,2},{1,3},{2,6},{3,7},{6,4},{7,5},{4,0},{5,1},{8,10},{9,11},{10,... | collective-permute-start | bytes 1671176 | tf_op jit(solution)/shard_map/c2/ppermute | solution.py:314
  42.5 21.5 %collective-permute-start.9 = (bf16[128,2048]{1,0:T(8,128)(2,1)S(1)}, bf16[128,2048]{1,0:T(8,128)(2,1)S(1)}, u32[]{:S(2)}, u32[]{:S(2)}) collective-permute-start(bf16[128,2048]{1,0:T(8,128)(2,1)S(1)} %collective-permute-done.1.refs_0_), channel_id=1, source_target_pairs={{0,2},{1,3},{2,6},{3,7},{6,4},{7,5},{4,0},{5,1},{8,10},{9,11},{10,... | collective-permute-start | bytes 1572872 | tf_op jit(solution)/shard_map/t3/ppermute | solution.py:314
  51.7 12.3 %collective-permute-start.10 = (bf16[128,2048]{1,0:T(8,128)(2,1)S(1)}, bf16[128,2048]{1,0:T(8,128)(2,1)S(1)}, u32[]{:S(2)}, u32[]{:S(2)}) collective-permute-start(bf16[128,2048]{1,0:T(8,128)(2,1)S(1)} %get-tuple-element.250), channel_id=1, source_target_pairs={{0,1},{1,0},{2,3},{3,2},{4,5},{5,4},{6,7},{7,6},{8,9},{9,8},{10,11... | collective-permute-start | bytes 1572872 | tf_op jit(solution)/shard_map/o1/ppermute | solution.py:318
  54.0 16.3 %collective-permute-start.14 = (bf16[128,1152]{1,0:T(8,128)(2,1)S(1)}, bf16[128,1152]{1,0:T(8,128)(2,1)S(1)}, u32[]{:S(2)}, u32[]{:S(2)}) collective-permute-start(bf16[128,1152]{1,0:T(8,128)(2,1)S(1)} %get-tuple-element.268), channel_id=1, source_target_pairs={{0,2},{1,3},{2,6},{3,7},{6,4},{7,5},{4,0},{5,1},{8,10},{9,11},{10,... | collective-permute-start | bytes 884744 | tf_op jit(solution)/shard_map/c3s/ppermute | solution.py:314
  70.5 17.1 %collective-permute-start.22 = (bf16[128,2048]{1,0:T(8,128)(2,1)S(1)}, bf16[128,2048]{1,0:T(8,128)(2,1)S(1)}, u32[]{:S(2)}, u32[]{:S(2)}) collective-permute-start(bf16[128,2048]{1,0:T(8,128)(2,1)S(1)} %add_m1.1), channel_id=1, source_target_pairs={{0,2},{1,3},{2,6},{3,7},{6,4},{7,5},{4,0},{5,1},{8,10},{9,11},{10,... | collective-permute-start | bytes 1572872 | tf_op jit(solution)/shard_map/m1/ppermute | solution.py:314
  76.0 17.5 %collective-permute-start.26 = (bf16[1,704,512]{2,1,0:T(8,128)(2,1)S(1)}, bf16[1,704,512]{2,1,0:T(8,128)(2,1)S(1)}, u32[]{:S(2)}, u32[]{:S(2)}) collective-permute-start(bf16[1,704,512]{2,1,0:T(8,128)(2,1)S(1)} %get-tuple-element.335), channel_id=1, source_target_pairs={{0,16},{8,24},{16,0},{24,8},{1,17},{9,25},{17,1},{25,9},{2,18},{10... | collective-permute-start | bytes 2162696 | tf_op jit(solution)/shard_map/d1/ppermute | solution.py:322
  77.6 17.1 %collective-permute-start.25 = (bf16[1,704,512]{2,1,0:T(8,128)(2,1)S(1)}, bf16[1,704,512]{2,1,0:T(8,128)(2,1)S(1)}, u32[]{:S(2)}, u32[]{:S(2)}) collective-permute-start(bf16[1,704,512]{2,1,0:T(8,128)(2,1)S(1)} %get-tuple-element.333), channel_id=1, source_target_pairs={{0,8},{8,0},{16,24},{24,16},{1,9},{9,1},{17,25},{25,17},{2,10},{10... | collective-permute-start | bytes 2162696 | tf_op jit(solution)/shard_map/d1/ppermute | solution.py:322
  88.3 20.1 %collective-permute-start.28 = (bf16[128,2048]{1,0:T(8,128)(2,1)S(1)}, bf16[128,2048]{1,0:T(8,128)(2,1)S(1)}, u32[]{:S(2)}, u32[]{:S(2)}) collective-permute-start(bf16[128,2048]{1,0:T(8,128)(2,1)S(1)} %add_m2.1), channel_id=1, source_target_pairs={{0,2},{1,3},{2,6},{3,7},{6,4},{7,5},{4,0},{5,1},{8,10},{9,11},{10,... | collective-permute-start | bytes 1572872 | tf_op jit(solution)/shard_map/m2/ppermute | solution.py:314
  94.7 13.7 %collective-permute-start.29 = (bf16[128,2048]{1,0:T(8,128)(2,1)S(1)}, bf16[128,2048]{1,0:T(8,128)(2,1)S(1)}, u32[]{:S(2)}, u32[]{:S(2)}) collective-permute-start(bf16[128,2048]{1,0:T(8,128)(2,1)S(1)} %get-tuple-element.347), channel_id=1, source_target_pairs={{0,1},{1,0},{2,3},{3,2},{4,5},{5,4},{6,7},{7,6},{8,9},{9,8},{10,11... | collective-permute-start | bytes 1572872 | tf_op jit(solution)/shard_map/o0/ppermute | solution.py:318
  94.7 34.0 %collective-permute-start.33 = (bf16[2,704,512]{2,1,0:T(8,128)(2,1)S(1)}, bf16[2,704,512]{2,1,0:T(8,128)(2,1)S(1)}, u32[]{:S(2)}, u32[]{:S(2)}) collective-permute-start(bf16[2,704,512]{2,1,0:T(8,128)(2,1)S(1)} %get-tuple-element.377), channel_id=1, source_target_pairs={{0,8},{8,0},{16,24},{24,16},{1,9},{9,1},{17,25},{25,17},{2,10},{10... | collective-permute-start | bytes 4325384 | tf_op jit(solution)/shard_map/gu1/ppermute | solution.py:322
  96.2 33.7 %collective-permute-start.34 = (bf16[2,704,512]{2,1,0:T(8,128)(2,1)S(1)}, bf16[2,704,512]{2,1,0:T(8,128)(2,1)S(1)}, u32[]{:S(2)}, u32[]{:S(2)}) collective-permute-start(bf16[2,704,512]{2,1,0:T(8,128)(2,1)S(1)} %get-tuple-element.379), channel_id=1, source_target_pairs={{0,16},{8,24},{16,0},{24,8},{1,17},{9,25},{17,1},{25,9},{2,18},{10... | collective-permute-start | bytes 4325384 | tf_op jit(solution)/shard_map/gu1/ppermute | solution.py:322
  100.5 16.0 %collective-permute-start.27 = (bf16[128,2048]{1,0:T(8,128)(2,1)S(1)}, bf16[128,2048]{1,0:T(8,128)(2,1)S(1)}, u32[]{:S(2)}, u32[]{:S(2)}) collective-permute-start(bf16[128,2048]{1,0:T(8,128)(2,1)S(1)} %add_g1.1), channel_id=1, source_target_pairs={{0,2},{1,3},{2,6},{3,7},{6,4},{7,5},{4,0},{5,1},{8,10},{9,11},{10,... | collective-permute-start | bytes 1572872 | tf_op jit(solution)/shard_map/ga1/ppermute | solution.py:314
  108.7 19.0 %collective-permute-start.35 = (bf16[128,2048]{1,0:T(8,128)(2,1)S(1)}, bf16[128,2048]{1,0:T(8,128)(2,1)S(1)}, u32[]{:S(2)}, u32[]{:S(2)}) collective-permute-start(bf16[128,2048]{1,0:T(8,128)(2,1)S(1)} %add_m3.1), channel_id=1, source_target_pairs={{0,2},{1,3},{2,6},{3,7},{6,4},{7,5},{4,0},{5,1},{8,10},{9,11},{10,... | collective-permute-start | bytes 1572872 | tf_op jit(solution)/shard_map/m3/ppermute | solution.py:314
  116.7 14.8 %collective-permute-start.32 = (bf16[128,2048]{1,0:T(8,128)(2,1)S(1)}, bf16[128,2048]{1,0:T(8,128)(2,1)S(1)}, u32[]{:S(2)}, u32[]{:S(2)}) collective-permute-start(bf16[128,2048]{1,0:T(8,128)(2,1)S(1)} %get-tuple-element.375), channel_id=1, source_target_pairs={{0,1},{1,0},{2,3},{3,2},{4,5},{5,4},{6,7},{7,6},{8,9},{9,8},{10,11... | collective-permute-start | bytes 1572872 | tf_op jit(solution)/shard_map/r3/ppermute | solution.py:318
  116.8 21.2 %collective-permute-start.31 = (bf16[128,2048]{1,0:T(8,128)(2,1)S(1)}, bf16[128,2048]{1,0:T(8,128)(2,1)S(1)}, u32[]{:S(2)}, u32[]{:S(2)}) collective-permute-start(bf16[128,2048]{1,0:T(8,128)(2,1)S(1)} %add_g2.1), channel_id=1, source_target_pairs={{0,2},{1,3},{2,6},{3,7},{6,4},{7,5},{4,0},{5,1},{8,10},{9,11},{10,... | collective-permute-start | bytes 1572872 | tf_op jit(solution)/shard_map/ga2/ppermute | solution.py:314
  130.5 25.2 %collective-permute-start.39 = (bf16[3,704,256]{2,1,0:T(8,128)(2,1)S(1)}, bf16[3,704,256]{2,1,0:T(8,128)(2,1)S(1)}, u32[]{:S(2)}, u32[]{:S(2)}) collective-permute-start(bf16[3,704,256]{2,1,0:T(8,128)(2,1)S(1)} %get-tuple-element.417), channel_id=1, source_target_pairs={{0,8},{8,0},{16,24},{24,16},{1,9},{9,1},{17,25},{25,17},{2,10},{10... | collective-permute-start | bytes 3244040 | tf_op jit(solution)/shard_map/last/ppermute | solution.py:322
  131.1 25.0 %collective-permute-start.38 = (bf16[3,704,256]{2,1,0:T(8,128)(2,1)S(1)}, bf16[3,704,256]{2,1,0:T(8,128)(2,1)S(1)}, u32[]{:S(2)}, u32[]{:S(2)}) collective-permute-start(bf16[3,704,256]{2,1,0:T(8,128)(2,1)S(1)} %get-tuple-element.415), channel_id=1, source_target_pairs={{0,16},{8,24},{16,0},{24,8},{1,17},{9,25},{17,1},{25,9},{2,18},{10... | collective-permute-start | bytes 3244040 | tf_op jit(solution)/shard_map/last/ppermute | solution.py:322
  138.3 15.2 %collective-permute-start.36 = (bf16[128,2048]{1,0:T(8,128)(2,1)S(1)}, bf16[128,2048]{1,0:T(8,128)(2,1)S(1)}, u32[]{:S(2)}, u32[]{:S(2)}) collective-permute-start(bf16[128,2048]{1,0:T(8,128)(2,1)S(1)} %add_convert_fusion.1), channel_id=1, source_target_pairs={{0,2},{1,3},{2,6},{3,7},{6,4},{7,5},{4,0},{5,1},{8,10},{9,11},{10,... | collective-permute-start | bytes 1572872 | tf_op jit(solution)/shard_map/ga3/ppermute | solution.py:314
  (27 other events, 104.3 us)

commit v8 on v6

--- a/solution.py
+++ b/solution.py
@@ -271,13 +271,12 @@
         out_b[at, :, :] = tn(left[...], right[:, half:]).astype(BF16)
 
 
-def cross_kernel(near, came_a, came_b, down_a, down_b, own_a, own_b, *outs):
-    cut = outs[0].shape[2]
+def cross_kernel(near, came, down, own, out):
+    cut = out.shape[2]
     part = slice(0, cut) if near else slice(cut, 2 * cut)
-    for came, down, own, out in ((came_a, down_a, own_a, outs[0]), (came_b, down_b, own_b, outs[1])):
-        for at in range(3):
-            first = down[0, :, part] if at == 2 else came[at, :, part]
-            out[at, :, :] = (first.astype(F32) + own[at, :, part].astype(F32)).astype(out.dtype)
+    for at in range(3):
+        first = down[0, :, part] if at == 2 else came[at, :, part]
+        out[at, :, :] = (first.astype(F32) + own[at, :, part].astype(F32)).astype(out.dtype)
 
 
 def finish_kernel(near_a, near_b, last_a, last_b, *outs):
@@ -510,12 +509,25 @@
     g, r2 = order.point(g, r2)
     g = ring(sums("add_g2", g, m2, r2), "ga2")
     r3 = twin(r3, "r3")
-    both_came[0], both_came[1], m = order.point(*both_came, m)
-    parts = [*both_came, *down_came, *own]
-    far = launch("cross", partial(cross_kernel, False), [((3, ff, cut), BF16)] * 2, parts)
-    far = order.point(*far)
-    last = flips(far, (2, 1), "last")
-    near_a, near_b = launch("settle", partial(cross_kernel, True), [((3, ff, cut), F32)] * 2, parts)
+    last = [None, None]
+    for at, mask in ((1, 1), (0, 2)):
+        both_came[at], m = order.point(both_came[at], m)
+        far = launch(
+            f"cross_{at}",
+            partial(cross_kernel, False),
+            [((3, ff, cut), BF16)],
+            [both_came[at], down_came[at], own[at]],
+        )
+        last[at] = flips(far, (mask,), "last")[0]
+    near_a, near_b = (
+        launch(
+            f"settle_{at}",
+            partial(cross_kernel, True),
+            [((3, ff, cut), F32)],
+            [both_came[at], down_came[at], own[at]],
+        )[0]
+        for at in range(2)
+    )
     g, r3 = order.point(g, r3)
     g = ring(add(g, kept(m3, r3)).astype(BF16), "ga3")
     r0 = twin(r0, "r0")

time: 159 us -> 158 us (level)
  waiting for transfers between devices: 65 us -> 62.8 us
  starting transfers between devices: 35.6 us -> 37.6 us
    ppermute x6, starting transfers between devices: 6.24 us -> 8.18 us  [flip(): return lax.ppermute(value, 'dp', [(at, at ^ mask) for at in range(4)])]
    pallas_call x28 -> x30, Pallas kernels: 46.4 us -> 46.3 us  [call(): pl.pallas_call(kernel, name=name, out_shape=[jax.ShapeDtypeStruct(shape,...]
  transfers between devices with their start and end apart: 40 -> 40, of which waited for: 18 -> 17; matrix products, arithmetic and copies ran while one was open for 2% -> 2% of each run, Pallas kernels for 28% -> 28%
where the time goes in v8:
time: 158 us
  waiting for transfers between devices  62.8 us (40%)
  Pallas kernels  46.3 us (29%)
  starting transfers between devices  37.6 us (24%)
  local copies, waits for them, and re-layouts  9.11 us (6%)
    ppermute x13, waiting for transfers between devices, step(): lax.ppermute(value, 'expert', [(2 * at + core, 2 * follow[at] + core) for...  56.8 us
    pallas_call x30, Pallas kernels, call(): pl.pallas_call(kernel, name=name, out_shape=[jax.ShapeDtypeStruct(shape,...  46.3 us
    ppermute x13, starting transfers between devices, step(): lax.ppermute(value, 'expert', [(2 * at + core, 2 * follow[at] + core) for...  25.6 us
    ppermute x6, starting transfers between devices, flip(): return lax.ppermute(value, 'dp', [(at, at ^ mask) for at in range(4)])  8.18 us
    unnamed x23, local copies, waits for them, and re-layouts  8.11 us
    ppermute x6, waiting for transfers between devices, flip(): return lax.ppermute(value, 'dp', [(at, at ^ mask) for at in range(4)])  4.86 us
    ppermute x21, starting transfers between devices, swap(): lax.ppermute(value, 'expert', [(at, at ^ 1) for at in range(n_expert)])  3.73 us
  transfers between devices with their start and end apart: 40, of which 17 were waited for; matrix products, arithmetic and copies ran while one was open for 2% of the time, Pallas kernels for 28%

profile of v8, /device:TPU:0, one launch (start us, length us, event | category | flops | bytes accessed | tf_op | source)
XLA Modules:
  0.0 158.1 jit_solution(3061305886508964641)
XLA Ops:
  0.6 3.1 %collective-permute-start = (bf16[128,2048]{1,0:T(8,128)(2,1)}, bf16[128,2048]{1,0:T(8,128)(2,1)}, u32[]{:S(2)}, u32[]{:S(2)}) collective-permute-start(bf16[128,2048]{1,0:T(8,128)(2,1)} %refs_0_), channel_id=1, source_target_pairs={{0,2},{1,3},{2,6},{3,7},{6,4},{7,5},{4,0},{5,1},{8,10},{9,11},{10,... | collective-permute-start | bytes 1572872 | tf_op jit(solution)/shard_map/t1/ppermute | solution.py:306
  6.8 2.6 %collective-permute-start.2 = (bf16[128,2176]{1,0:T(8,128)(2,1)S(1)}, bf16[128,2176]{1,0:T(8,128)(2,1)S(1)}, u32[]{:S(2)}, u32[]{:S(2)}) collective-permute-start(bf16[128,2176]{1,0:T(8,128)(2,1)S(1)} %pack.1.refs_0_), channel_id=1, source_target_pairs={{0,2},{1,3},{2,6},{3,7},{6,4},{7,5},{4,0},{5,1},{8,10},{9,11},{10,... | collective-permute-start | bytes 1671176 | tf_op jit(solution)/shard_map/c1/ppermute | solution.py:306
  9.5 8.3 %collective-permute-done.refs_0_ = bf16[128,2048]{1,0:T(8,128)(2,1)} collective-permute-done((bf16[128,2048]{1,0:T(8,128)(2,1)}, bf16[128,2048]{1,0:T(8,128)(2,1)}, u32[]{:S(2)}, u32[]{:S(2)}) %collective-permute-start) | collective-permute-done | bytes 524320 | tf_op jit(solution)/shard_map/t1/ppermute | solution.py:306
  20.0 9.7 %collective-permute-done.2.refs_0_ = bf16[128,2176]{1,0:T(8,128)(2,1)S(1)} collective-permute-done((bf16[128,2176]{1,0:T(8,128)(2,1)S(1)}, bf16[128,2176]{1,0:T(8,128)(2,1)S(1)}, u32[]{:S(2)}, u32[]{:S(2)}) %collective-permute-start.2) | collective-permute-done | bytes 557088 | tf_op jit(solution)/shard_map/c1/ppermute | solution.py:306
  31.7 1.8 %copy-done = bf16[1,2048,704]{1,2,0:T(8,128)(2,1)S(1)} copy-done((bf16[1,2048,704]{1,2,0:T(8,128)(2,1)S(1)}, bf16[1,2048,704]{1,2,0:T(8,128)(2,1)}, u32[]{:S(2)}) %copy-start) | copy-done | bytes 2883608
  36.3 3.2 %forward_1.1 = (bf16[256,704]{1,0:T(8,128)(2,1)S(1)}, f32[256,704]{1,0:T(8,128)S(1)}, f32[256,704]{1,0:T(8,128)S(1)}, bf16[256,1024]{1,0:T(8,128)(2,1)S(1)}, bf16[256,1024]{1,0:T(8,128)(2,1)S(1)}) custom-call(s32[9]{0:T(128)S(1)} %stack.39.offs, bf16[128,2048]{1,0:T(8,128)(2,1)} %collective-permute-done.refs_0_, bf16[128,2048]{1,0:T(8,128)(2,1)S(1)} %copy-done.10, ...), custom_call_target="tpu_custom_call" | custom-call | flops 1 | bytes 1 | tf_op jit(solution)/shard_map/forward_1/pallas_call | solution.py:129
  39.6 2.6 %forward_0.1 = (bf16[256,704]{1,0:T(8,128)(2,1)S(1)}, f32[256,704]{1,0:T(8,128)S(1)}, f32[256,704]{1,0:T(8,128)S(1)}, bf16[256,1024]{1,0:T(8,128)(2,1)S(1)}, bf16[256,1024]{1,0:T(8,128)(2,1)S(1)}) custom-call(s32[9]{0:T(128)S(1)} %stack.39.offs, bf16[128,2048]{1,0:T(8,128)(2,1)S(1)} %copy-done.6, bf16[128,2048]{1,0:T(8,128)(2,1)S(1)} %copy-done.8, ...), custom_call_target="tpu_custom_call" | custom-call | flops 1 | bytes 1 | tf_op jit(solution)/shard_map/forward_0/pallas_call | solution.py:129
  42.5 3.4 %collective-permute-start.9 = (bf16[128,2048]{1,0:T(8,128)(2,1)S(1)}, bf16[128,2048]{1,0:T(8,128)(2,1)S(1)}, u32[]{:S(2)}, u32[]{:S(2)}) collective-permute-start(bf16[128,2048]{1,0:T(8,128)(2,1)S(1)} %collective-permute-done.1.refs_0_), channel_id=1, source_target_pairs={{0,2},{1,3},{2,6},{3,7},{6,4},{7,5},{4,0},{5,1},{8,10},{9,11},{10,... | collective-permute-start | bytes 1572872 | tf_op jit(solution)/shard_map/t3/ppermute | solution.py:306
  45.9 2.9 %backward_0.1 = (bf16[128,2048]{1,0:T(8,128)(2,1)S(1)}, bf16[128,2048]{1,0:T(8,128)(2,1)S(1)}, bf16[256,704]{1,0:T(8,128)(2,1)S(1)}, bf16[256,704]{1,0:T(8,128)(...) custom-call(s32[9]{0:T(128)S(1)} %stack.39.offs, ...), custom_call_target="tpu_custom_call" | custom-call | flops 1 | bytes 1 | tf_op jit(solution)/shard_map/backward_0/pallas_call | solution.py:129
  48.8 2.9 %backward_1.1 = (bf16[128,2048]{1,0:T(8,128)(2,1)S(1)}, bf16[128,2048]{1,0:T(8,128)(2,1)S(1)}, bf16[256,704]{1,0:T(8,128)(2,1)S(1)}, bf16[256,704]{1,0:T(8,128)(...) custom-call(s32[9]{0:T(128)S(1)} %stack.39.offs, ...), custom_call_target="tpu_custom_call" | custom-call | flops 1 | bytes 1 | tf_op jit(solution)/shard_map/backward_1/pallas_call | solution.py:129
  55.4 2.6 %forward_2.1 = (bf16[256,704]{1,0:T(8,128)(2,1)S(1)}, f32[256,704]{1,0:T(8,128)S(1)}, f32[256,704]{1,0:T(8,128)S(1)}, bf16[256,1024]{1,0:T(8,128)(2,1)S(1)}, bf16[256,1024]{1,0:T(8,128)(2,1)S(1)}) custom-call(s32[9]{0:T(128)S(1)} %stack.39.offs, bf16[128,2048]{1,0:T(8,128)(2,1)S(1)} %collective-permute-done.1.refs_0_, ...), custom_call_target="tpu_custom_call" | custom-call | flops 1 | bytes 1 | tf_op jit(solution)/shard_map/forward_2/pallas_call | solution.py:129
  58.0 2.9 %backward_2.1 = (bf16[128,2048]{1,0:T(8,128)(2,1)S(1)}, bf16[128,2048]{1,0:T(8,128)(2,1)S(1)}, bf16[256,704]{1,0:T(8,128)(2,1)S(1)}, bf16[256,704]{1,0:T(8,128)(...) custom-call(s32[9]{0:T(128)S(1)} %stack.39.offs, ...), custom_call_target="tpu_custom_call" | custom-call | flops 1 | bytes 1 | tf_op jit(solution)/shard_map/backward_2/pallas_call | solution.py:129
  66.4 2.6 %forward_3.1 = (bf16[256,704]{1,0:T(8,128)(2,1)S(1)}, f32[256,704]{1,0:T(8,128)S(1)}, f32[256,704]{1,0:T(8,128)S(1)}, bf16[256,1024]{1,0:T(8,128)(2,1)S(1)}, bf16[256,1024]{1,0:T(8,128)(2,1)S(1)}) custom-call(s32[9]{0:T(128)S(1)} %stack.39.offs, bf16[128,2048]{1,0:T(8,128)(2,1)S(1)} %collective-permute-done.9.refs_0_, ...), custom_call_target="tpu_custom_call" | custom-call | flops 1 | bytes 1 | tf_op jit(solution)/shard_map/forward_3/pallas_call | solution.py:129
  82.5 3.2 %both_s.1 = (bf16[2,704,512]{2,1,0:T(8,128)(2,1)S(1)}, bf16[2,704,512]{2,1,0:T(8,128)(2,1)S(1)}) custom-call(bf16[256,704]{1,0:T(8,128)(2,1)S(1)} %get-tuple-element.348.refs_0_, bf16[256,704]{1,0:T(8,128)(2,1)S(1)} %get-tuple-element.310.refs_1_.refs_0_, bf16[256,704]{1,0:T(8,128)(2,1)S(1)} %get-tuple-element.325.refs_2_.refs_0_, ...), custom_call_target="tpu_custom_call" | custom-call | flops 1 | bytes 1 | tf_op jit(solution)/shard_map/both_s/pallas_call | solution.py:129
  88.3 2.0 %collective-permute-start.28 = (bf16[128,2048]{1,0:T(8,128)(2,1)S(1)}, bf16[128,2048]{1,0:T(8,128)(2,1)S(1)}, u32[]{:S(2)}, u32[]{:S(2)}) collective-permute-start(bf16[128,2048]{1,0:T(8,128)(2,1)S(1)} %add_m2.1), channel_id=1, source_target_pairs={{0,2},{1,3},{2,6},{3,7},{6,4},{7,5},{4,0},{5,1},{8,10},{9,11},{10,... | collective-permute-start | bytes 1572872 | tf_op jit(solution)/shard_map/m2/ppermute | solution.py:306
  100.5 3.1 %collective-permute-start.27 = (bf16[128,2048]{1,0:T(8,128)(2,1)S(1)}, bf16[128,2048]{1,0:T(8,128)(2,1)S(1)}, u32[]{:S(2)}, u32[]{:S(2)}) collective-permute-start(bf16[128,2048]{1,0:T(8,128)(2,1)S(1)} %add_g1.1), channel_id=1, source_target_pairs={{0,2},{1,3},{2,6},{3,7},{6,4},{7,5},{4,0},{5,1},{8,10},{9,11},{10,... | collective-permute-start | bytes 1572872 | tf_op jit(solution)/shard_map/ga1/ppermute | solution.py:306
  103.6 4.8 %kept_k.1 = (bf16[3,704,512]{2,1,0:T(8,128)(2,1)S(1)}, bf16[3,704,512]{2,1,0:T(8,128)(2,1)S(1)}) custom-call(bf16[256,704]{1,0:T(8,128)(2,1)S(1)} %get-tuple-element.348.refs_0_, bf16[256,704]{1,0:T(8,128)(2,1)S(1)} %get-tuple-element.310.refs_1_.refs_0_, bf16[256,704]{1,0:T(8,128)(2,1)S(1)} %get-tuple-element.325.refs_2_.refs_0_, ...), custom_call_target="tpu_custom_call" | custom-call | flops 1 | bytes 1 | tf_op jit(solution)/shard_map/kept_k/pallas_call | solution.py:129
  109.0 7.5 %collective-permute-done.27.refs_0_ = bf16[128,2048]{1,0:T(8,128)(2,1)S(1)} collective-permute-done((bf16[128,2048]{1,0:T(8,128)(2,1)S(1)}, bf16[128,2048]{1,0:T(8,128)(2,1)S(1)}, u32[]{:S(2)}, u32[]{:S(2)}) %collective-permute-start.27) | collective-permute-done | bytes 524320 | tf_op jit(solution)/shard_map/ga1/ppermute | solution.py:306
  116.8 2.0 %collective-permute-start.31 = (bf16[128,2048]{1,0:T(8,128)(2,1)S(1)}, bf16[128,2048]{1,0:T(8,128)(2,1)S(1)}, u32[]{:S(2)}, u32[]{:S(2)}) collective-permute-start(bf16[128,2048]{1,0:T(8,128)(2,1)S(1)} %add_g2.1), channel_id=1, source_target_pairs={{0,2},{1,3},{2,6},{3,7},{6,4},{7,5},{4,0},{5,1},{8,10},{9,11},{10,... | collective-permute-start | bytes 1572872 | tf_op jit(solution)/shard_map/ga2/ppermute | solution.py:306
  118.7 9.0 %collective-permute-done.35.refs_0_ = bf16[128,2048]{1,0:T(8,128)(2,1)S(1)} collective-permute-done((bf16[128,2048]{1,0:T(8,128)(2,1)S(1)}, bf16[128,2048]{1,0:T(8,128)(2,1)S(1)}, u32[]{:S(2)}, u32[]{:S(2)}) %collective-permute-start.35) | collective-permute-done | bytes 524320 | tf_op jit(solution)/shard_map/m3/ppermute | solution.py:306
  132.3 5.6 %collective-permute-done.31 = bf16[128,2048]{1,0:T(8,128)(2,1)S(1)} collective-permute-done((bf16[128,2048]{1,0:T(8,128)(2,1)S(1)}, bf16[128,2048]{1,0:T(8,128)(2,1)S(1)}, u32[]{:S(2)}, u32[]{:S(2)}) %collective-permute-start.31) | collective-permute-done | bytes 524320 | tf_op jit(solution)/shard_map/ga2/ppermute | solution.py:306
  138.3 2.0 %collective-permute-start.36 = (bf16[128,2048]{1,0:T(8,128)(2,1)S(1)}, bf16[128,2048]{1,0:T(8,128)(2,1)S(1)}, u32[]{:S(2)}, u32[]{:S(2)}) collective-permute-start(bf16[128,2048]{1,0:T(8,128)(2,1)S(1)} %add_convert_fusion.1), channel_id=1, source_target_pairs={{0,2},{1,3},{2,6},{3,7},{6,4},{7,5},{4,0},{5,1},{8,10},{9,11},{10,... | collective-permute-start | bytes 1572872 | tf_op jit(solution)/shard_map/ga3/ppermute | solution.py:306
  141.7 11.8 %collective-permute-done.36 = bf16[128,2048]{1,0:T(8,128)(2,1)S(1)} collective-permute-done((bf16[128,2048]{1,0:T(8,128)(2,1)S(1)}, bf16[128,2048]{1,0:T(8,128)(2,1)S(1)}, u32[]{:S(2)}, u32[]{:S(2)}) %collective-permute-start.36) | collective-permute-done | bytes 524320 | tf_op jit(solution)/shard_map/ga3/ppermute | solution.py:306
  155.7 2.4 %finish.1 = (f32[704,512]{1,0:T(8,128)}, f32[704,512]{1,0:T(8,128)}, f32[704,512]{1,0:T(8,128)}) custom-call(f32[3,704,256]{2,1,0:T(8,128)S(1)} %settle_0.1.near_a, f32[3,704,256]{2,1,0:T(8,128)S(1)} %settle_1.1.near_b, bf16[3,704,256]{2,1,0:T(8,128)(2,1)S(1)} %collective-permute-done.38.last_a, bf16[3,704,256]{2,1,0:T(8,128)(2,1)S(1)} %collective-permute-done.39.last_b), custom_call_target="tpu_custom_call" | custom-call | flops 1 | bytes 1 | tf_op jit(solution)/shard_map/finish/pallas_call | solution.py:129
  (117 shorter events, 55.1 us)
Async XLA Ops:
  0.6 17.2 %collective-permute-start = (bf16[128,2048]{1,0:T(8,128)(2,1)}, bf16[128,2048]{1,0:T(8,128)(2,1)}, u32[]{:S(2)}, u32[]{:S(2)}) collective-permute-start(bf16[128,2048]{1,0:T(8,128)(2,1)} %refs_0_), channel_id=1, source_target_pairs={{0,2},{1,3},{2,6},{3,7},{6,4},{7,5},{4,0},{5,1},{8,10},{9,11},{10,... | collective-permute-start | bytes 1572872 | tf_op jit(solution)/shard_map/t1/ppermute | solution.py:306
  6.8 22.8 %collective-permute-start.2 = (bf16[128,2176]{1,0:T(8,128)(2,1)S(1)}, bf16[128,2176]{1,0:T(8,128)(2,1)S(1)}, u32[]{:S(2)}, u32[]{:S(2)}) collective-permute-start(bf16[128,2176]{1,0:T(8,128)(2,1)S(1)} %pack.1.refs_0_), channel_id=1, source_target_pairs={{0,2},{1,3},{2,6},{3,7},{6,4},{7,5},{4,0},{5,1},{8,10},{9,11},{10,... | collective-permute-start | bytes 1671176 | tf_op jit(solution)/shard_map/c1/ppermute | solution.py:306
  17.8 11.8 %collective-permute-start.4 = (bf16[128,2048]{1,0:T(8,128)(2,1)}, bf16[128,2048]{1,0:T(8,128)(2,1)S(1)}, u32[]{:S(2)}, u32[]{:S(2)}) collective-permute-start(bf16[128,2048]{1,0:T(8,128)(2,1)} %collective-permute-done.refs_0_), channel_id=1, source_target_pairs={{0,1},{1,0},{2,3},{3,2},{4,5},{5,4},{6,7},{7,6},{8,9},{9,8},{10,11... | collective-permute-start | bytes 1572872 | tf_op jit(solution)/shard_map/p1/ppermute | solution.py:310
  17.8 24.4 %collective-permute-start.1 = (bf16[128,2048]{1,0:T(8,128)(2,1)}, bf16[128,2048]{1,0:T(8,128)(2,1)S(1)}, u32[]{:S(2)}, u32[]{:S(2)}) collective-permute-start(bf16[128,2048]{1,0:T(8,128)(2,1)} %collective-permute-done.refs_0_), channel_id=1, source_target_pairs={{0,2},{1,3},{2,6},{3,7},{6,4},{7,5},{4,0},{5,1},{8,10},{9,11},{10,... | collective-permute-start | bytes 1572872 | tf_op jit(solution)/shard_map/t2/ppermute | solution.py:306
  18.9 27.0 %collective-permute-start.6 = (bf16[128,2176]{1,0:T(8,128)(2,1)S(1)}, bf16[128,2176]{1,0:T(8,128)(2,1)S(1)}, u32[]{:S(2)}, u32[]{:S(2)}) collective-permute-start(bf16[128,2176]{1,0:T(8,128)(2,1)S(1)} %pack.1.refs_0_), channel_id=1, source_target_pairs={{0,1},{1,0},{2,3},{3,2},{4,5},{5,4},{6,7},{7,6},{8,9},{9,8},{10,11... | collective-permute-start | bytes 1671176 | tf_op jit(solution)/shard_map/q0/ppermute | solution.py:310
  30.4 18.4 %collective-permute-start.5 = (bf16[128,2176]{1,0:T(8,128)(2,1)S(1)}, bf16[128,2176]{1,0:T(8,128)(2,1)S(1)}, u32[]{:S(2)}, u32[]{:S(2)}) collective-permute-start(bf16[128,2176]{1,0:T(8,128)(2,1)S(1)} %collective-permute-done.2.refs_0_), channel_id=1, source_target_pairs={{0,1},{1,0},{2,3},{3,2},{4,5},{5,4},{6,7},{7,6},{8,9},{9,8},{10,11... | collective-permute-start | bytes 1671176 | tf_op jit(solution)/shard_map/q1/ppermute | solution.py:310
  30.4 22.4 %collective-permute-start.7 = (bf16[128,2176]{1,0:T(8,128)(2,1)S(1)}, bf16[128,2176]{1,0:T(8,128)(2,1)S(1)}, u32[]{:S(2)}, u32[]{:S(2)}) collective-permute-start(bf16[128,2176]{1,0:T(8,128)(2,1)S(1)} %collective-permute-done.2.refs_0_), channel_id=1, source_target_pairs={{0,2},{1,3},{2,6},{3,7},{6,4},{7,5},{4,0},{5,1},{8,10},{9,11},{10,... | collective-permute-start | bytes 1671176 | tf_op jit(solution)/shard_map/c2/ppermute | solution.py:306
  42.5 21.5 %collective-permute-start.9 = (bf16[128,2048]{1,0:T(8,128)(2,1)S(1)}, bf16[128,2048]{1,0:T(8,128)(2,1)S(1)}, u32[]{:S(2)}, u32[]{:S(2)}) collective-permute-start(bf16[128,2048]{1,0:T(8,128)(2,1)S(1)} %collective-permute-done.1.refs_0_), channel_id=1, source_target_pairs={{0,2},{1,3},{2,6},{3,7},{6,4},{7,5},{4,0},{5,1},{8,10},{9,11},{10,... | collective-permute-start | bytes 1572872 | tf_op jit(solution)/shard_map/t3/ppermute | solution.py:306
  51.7 12.3 %collective-permute-start.10 = (bf16[128,2048]{1,0:T(8,128)(2,1)S(1)}, bf16[128,2048]{1,0:T(8,128)(2,1)S(1)}, u32[]{:S(2)}, u32[]{:S(2)}) collective-permute-start(bf16[128,2048]{1,0:T(8,128)(2,1)S(1)} %get-tuple-element.246), channel_id=1, source_target_pairs={{0,1},{1,0},{2,3},{3,2},{4,5},{5,4},{6,7},{7,6},{8,9},{9,8},{10,11... | collective-permute-start | bytes 1572872 | tf_op jit(solution)/shard_map/o1/ppermute | solution.py:310
  54.0 16.3 %collective-permute-start.14 = (bf16[128,1152]{1,0:T(8,128)(2,1)S(1)}, bf16[128,1152]{1,0:T(8,128)(2,1)S(1)}, u32[]{:S(2)}, u32[]{:S(2)}) collective-permute-start(bf16[128,1152]{1,0:T(8,128)(2,1)S(1)} %get-tuple-element.264), channel_id=1, source_target_pairs={{0,2},{1,3},{2,6},{3,7},{6,4},{7,5},{4,0},{5,1},{8,10},{9,11},{10,... | collective-permute-start | bytes 884744 | tf_op jit(solution)/shard_map/c3s/ppermute | solution.py:306
  70.5 17.1 %collective-permute-start.22 = (bf16[128,2048]{1,0:T(8,128)(2,1)S(1)}, bf16[128,2048]{1,0:T(8,128)(2,1)S(1)}, u32[]{:S(2)}, u32[]{:S(2)}) collective-permute-start(bf16[128,2048]{1,0:T(8,128)(2,1)S(1)} %add_m1.1), channel_id=1, source_target_pairs={{0,2},{1,3},{2,6},{3,7},{6,4},{7,5},{4,0},{5,1},{8,10},{9,11},{10,... | collective-permute-start | bytes 1572872 | tf_op jit(solution)/shard_map/m1/ppermute | solution.py:306
  76.0 17.5 %collective-permute-start.26 = (bf16[1,704,512]{2,1,0:T(8,128)(2,1)S(1)}, bf16[1,704,512]{2,1,0:T(8,128)(2,1)S(1)}, u32[]{:S(2)}, u32[]{:S(2)}) collective-permute-start(bf16[1,704,512]{2,1,0:T(8,128)(2,1)S(1)} %get-tuple-element.331), channel_id=1, source_target_pairs={{0,16},{8,24},{16,0},{24,8},{1,17},{9,25},{17,1},{25,9},{2,18},{10... | collective-permute-start | bytes 2162696 | tf_op jit(solution)/shard_map/d1/ppermute | solution.py:314
  77.6 17.1 %collective-permute-start.25 = (bf16[1,704,512]{2,1,0:T(8,128)(2,1)S(1)}, bf16[1,704,512]{2,1,0:T(8,128)(2,1)S(1)}, u32[]{:S(2)}, u32[]{:S(2)}) collective-permute-start(bf16[1,704,512]{2,1,0:T(8,128)(2,1)S(1)} %get-tuple-element.329), channel_id=1, source_target_pairs={{0,8},{8,0},{16,24},{24,16},{1,9},{9,1},{17,25},{25,17},{2,10},{10... | collective-permute-start | bytes 2162696 | tf_op jit(solution)/shard_map/d1/ppermute | solution.py:314
  88.3 20.1 %collective-permute-start.28 = (bf16[128,2048]{1,0:T(8,128)(2,1)S(1)}, bf16[128,2048]{1,0:T(8,128)(2,1)S(1)}, u32[]{:S(2)}, u32[]{:S(2)}) collective-permute-start(bf16[128,2048]{1,0:T(8,128)(2,1)S(1)} %add_m2.1), channel_id=1, source_target_pairs={{0,2},{1,3},{2,6},{3,7},{6,4},{7,5},{4,0},{5,1},{8,10},{9,11},{10,... | collective-permute-start | bytes 1572872 | tf_op jit(solution)/shard_map/m2/ppermute | solution.py:306
  94.8 13.7 %collective-permute-start.29 = (bf16[128,2048]{1,0:T(8,128)(2,1)S(1)}, bf16[128,2048]{1,0:T(8,128)(2,1)S(1)}, u32[]{:S(2)}, u32[]{:S(2)}) collective-permute-start(bf16[128,2048]{1,0:T(8,128)(2,1)S(1)} %get-tuple-element.343), channel_id=1, source_target_pairs={{0,1},{1,0},{2,3},{3,2},{4,5},{5,4},{6,7},{7,6},{8,9},{9,8},{10,11... | collective-permute-start | bytes 1572872 | tf_op jit(solution)/shard_map/o0/ppermute | solution.py:310
  94.8 34.0 %collective-permute-start.34 = (bf16[2,704,512]{2,1,0:T(8,128)(2,1)S(1)}, bf16[2,704,512]{2,1,0:T(8,128)(2,1)S(1)}, u32[]{:S(2)}, u32[]{:S(2)}) collective-permute-start(bf16[2,704,512]{2,1,0:T(8,128)(2,1)S(1)} %get-tuple-element.375), channel_id=1, source_target_pairs={{0,16},{8,24},{16,0},{24,8},{1,17},{9,25},{17,1},{25,9},{2,18},{10... | collective-permute-start | bytes 4325384 | tf_op jit(solution)/shard_map/gu1/ppermute | solution.py:314
  95.3 33.7 %collective-permute-start.33 = (bf16[2,704,512]{2,1,0:T(8,128)(2,1)S(1)}, bf16[2,704,512]{2,1,0:T(8,128)(2,1)S(1)}, u32[]{:S(2)}, u32[]{:S(2)}) collective-permute-start(bf16[2,704,512]{2,1,0:T(8,128)(2,1)S(1)} %get-tuple-element.373), channel_id=1, source_target_pairs={{0,8},{8,0},{16,24},{24,16},{1,9},{9,1},{17,25},{25,17},{2,10},{10... | collective-permute-start | bytes 4325384 | tf_op jit(solution)/shard_map/gu1/ppermute | solution.py:314
  100.5 16.0 %collective-permute-start.27 = (bf16[128,2048]{1,0:T(8,128)(2,1)S(1)}, bf16[128,2048]{1,0:T(8,128)(2,1)S(1)}, u32[]{:S(2)}, u32[]{:S(2)}) collective-permute-start(bf16[128,2048]{1,0:T(8,128)(2,1)S(1)} %add_g1.1), channel_id=1, source_target_pairs={{0,2},{1,3},{2,6},{3,7},{6,4},{7,5},{4,0},{5,1},{8,10},{9,11},{10,... | collective-permute-start | bytes 1572872 | tf_op jit(solution)/shard_map/ga1/ppermute | solution.py:306
  108.7 19.0 %collective-permute-start.35 = (bf16[128,2048]{1,0:T(8,128)(2,1)S(1)}, bf16[128,2048]{1,0:T(8,128)(2,1)S(1)}, u32[]{:S(2)}, u32[]{:S(2)}) collective-permute-start(bf16[128,2048]{1,0:T(8,128)(2,1)S(1)} %add_m3.1), channel_id=1, source_target_pairs={{0,2},{1,3},{2,6},{3,7},{6,4},{7,5},{4,0},{5,1},{8,10},{9,11},{10,... | collective-permute-start | bytes 1572872 | tf_op jit(solution)/shard_map/m3/ppermute | solution.py:306
  116.7 15.6 %collective-permute-start.32 = (bf16[128,2048]{1,0:T(8,128)(2,1)S(1)}, bf16[128,2048]{1,0:T(8,128)(2,1)S(1)}, u32[]{:S(2)}, u32[]{:S(2)}) collective-permute-start(bf16[128,2048]{1,0:T(8,128)(2,1)S(1)} %get-tuple-element.371), channel_id=1, source_target_pairs={{0,1},{1,0},{2,3},{3,2},{4,5},{5,4},{6,7},{7,6},{8,9},{9,8},{10,11... | collective-permute-start | bytes 1572872 | tf_op jit(solution)/shard_map/r3/ppermute | solution.py:310
  116.8 21.2 %collective-permute-start.31 = (bf16[128,2048]{1,0:T(8,128)(2,1)S(1)}, bf16[128,2048]{1,0:T(8,128)(2,1)S(1)}, u32[]{:S(2)}, u32[]{:S(2)}) collective-permute-start(bf16[128,2048]{1,0:T(8,128)(2,1)S(1)} %add_g2.1), channel_id=1, source_target_pairs={{0,2},{1,3},{2,6},{3,7},{6,4},{7,5},{4,0},{5,1},{8,10},{9,11},{10,... | collective-permute-start | bytes 1572872 | tf_op jit(solution)/shard_map/ga2/ppermute | solution.py:306
  129.3 25.6 %collective-permute-start.38 = (bf16[3,704,256]{2,1,0:T(8,128)(2,1)S(1)}, bf16[3,704,256]{2,1,0:T(8,128)(2,1)S(1)}, u32[]{:S(2)}, u32[]{:S(2)}) collective-permute-start(bf16[3,704,256]{2,1,0:T(8,128)(2,1)S(1)} %cross_0.1), channel_id=1, source_target_pairs={{0,16},{8,24},{16,0},{24,8},{1,17},{9,25},{17,1},{25,9},{2,18},{10... | collective-permute-start | bytes 3244040 | tf_op jit(solution)/shard_map/last/ppermute | solution.py:314
  130.8 24.9 %collective-permute-start.39 = (bf16[3,704,256]{2,1,0:T(8,128)(2,1)S(1)}, bf16[3,704,256]{2,1,0:T(8,128)(2,1)S(1)}, u32[]{:S(2)}, u32[]{:S(2)}) collective-permute-start(bf16[3,704,256]{2,1,0:T(8,128)(2,1)S(1)} %cross_1.1), channel_id=1, source_target_pairs={{0,8},{8,0},{16,24},{24,16},{1,9},{9,1},{17,25},{25,17},{2,10},{10... | collective-permute-start | bytes 3244040 | tf_op jit(solution)/shard_map/last/ppermute | solution.py:314
  138.3 15.2 %collective-permute-start.36 = (bf16[128,2048]{1,0:T(8,128)(2,1)S(1)}, bf16[128,2048]{1,0:T(8,128)(2,1)S(1)}, u32[]{:S(2)}, u32[]{:S(2)}) collective-permute-start(bf16[128,2048]{1,0:T(8,128)(2,1)S(1)} %add_convert_fusion.1), channel_id=1, source_target_pairs={{0,2},{1,3},{2,6},{3,7},{6,4},{7,5},{4,0},{5,1},{8,10},{9,11},{10,... | collective-permute-start | bytes 1572872 | tf_op jit(solution)/shard_map/ga3/ppermute | solution.py:306
  (27 other events, 104.2 us)
